TPU v7x, 32 devices: a whole 2x2x4 slice. The times are simulated.
32 devices in a mesh: section: 2 (over y), dp: 16 (over z, x, core).
Axes of the slice: x: 2, y: 2, z: 4, core: 2. Of those that a mesh axis runs over, the one named last changes fastest.
Arguments:
- tokens: bfloat16 [2, 16, 512, 768], P(None, 'dp'), may hold values from -6 to 6
- out_cotangent: bfloat16 [2, 16, 512, 768], P(None, 'dp'), may hold values from -0.011962891 to 0.011962891
- lengths: int32 [2, 16, 4], P(None, 'dp'), may hold values from 1 to 256, 512 in all within a row
- partner: int32 [2, 64], P(None, 'dp'), may hold values from 0 to 63, as said below
- group_ids: int32 [2, 64], replicated, may hold values from 0 to 1, as said below
- attn_in: float32 [2, 768, 2304], P('section', 'dp'), may hold values from -0.21875 to 0.21875
- attn_out: float32 [2, 768, 768], P('section', 'dp'), may hold values from -1.75 to 1.75
- ff_in: float32 [2, 768, 3072], P('section', 'dp'), may hold values from -0.21875 to 0.21875
- ff_out: float32 [2, 3072, 768], P('section', 'dp'), may hold values from -0.109375 to 0.109375
- norm_gains: float32 [2, 2, 768], P('section', None, 'dp'), may hold values from 0.5 to 1.5
- biases: float32 [2, 6, 768], P('section', None, 'dp'), may hold values from -1 to 1
- ff_bias: float32 [2, 3072], P('section', 'dp'), may hold values from -1 to 1
Outputs:
- contrast_loss: float32 [], replicated
- hidden_states: bfloat16 [2, 2, 16, 512, 768], P('section', None, 'dp')
- hidden_grads: float32 [2, 2, 16, 512, 768], P('section', None, 'dp')
- attn_in_grad: float32 [2, 768, 2304], P('section', 'dp')
- attn_out_grad: float32 [2, 768, 768], P('section', 'dp')
- ff_in_grad: float32 [2, 768, 3072], P('section', 'dp')
- ff_out_grad: float32 [2, 3072, 768], P('section', 'dp')
- gains_grad: float32 [2, 2, 768], P('section', None, 'dp')
- biases_grad: float32 [2, 6, 768], P('section', None, 'dp')
- ff_bias_grad: float32 [2, 3072], P('section', 'dp')
Inputs may be any that keep to these rules, and one draw needn't show every extreme that they name: Each row's 4 lengths sum to 512; in every row the longest is 256. In each micro-batch the sentences form twin pairs: partner[m, partner[m, i]] = i and partner[m, i] != i; twins share a group; sentences 0 and 32 are twins. `group_ids`: in each micro-batch every group holds exactly 32 sentences.
All inputs are finite; a program needn't handle non-finite values.
Results may differ from a plain program's by a relative error of at most 0.015.
Values may be sent and summed in bfloat16 or wider, within the bound.
No kernel may reach another device: no remote copies, remote signals or barrier semaphores. Data moves between devices by JAX's collectives and lax.ppermute only.
A program may use at most 320 MiB of HBM per device.

v0:
```python
from functools import partial

import jax
import jax.numpy as jnp
from jax import lax
from jax.sharding import PartitionSpec as P

D = 768
HEADS = 12
HEAD = 64
SEQ = 512
MICRO = 2


highest = lax.Precision.HIGHEST
norm_eps = 1e-05
unit_eps = 1e-06
masked_value = -1000000000.0
contrast_scale = 10.0


def passed_along(value, axis, steps):
    count = lax.axis_size(axis)
    first, last = (max(0, -steps), min(count, count - steps))
    return lax.ppermute(value, axis, [(source, source + steps) for source in range(first, last)])


def norm_rows(value, gain_row, shift_row):
    row_mean = jnp.mean(value, axis=-1, keepdims=True)
    centered = value - row_mean
    variance = jnp.mean(centered * centered, axis=-1, keepdims=True)
    return centered * lax.rsqrt(variance + norm_eps) * gain_row + shift_row


def segment_rows(lengths):
    row_ends = jnp.cumsum(lengths, axis=-1, dtype=jnp.int32)
    places = jnp.arange(SEQ, dtype=jnp.int32)
    return jnp.sum((places[None, :, None] >= row_ends[:, None, :]).astype(jnp.int32), axis=-1)


def pool_unit(final_rows, lengths):
    row_ends = jnp.cumsum(lengths, axis=-1, dtype=jnp.int32)
    row_starts = row_ends - lengths
    places = jnp.arange(SEQ, dtype=jnp.int32)
    member = (
        (places[None, None, :] >= row_starts[:, :, None])
        & (places[None, None, :] < row_ends[:, :, None])
    ).astype(jnp.float32)
    pooled = jnp.einsum("rst,rtd->rsd", member, final_rows, precision=highest) / lengths[
        :, :, None
    ].astype(jnp.float32)
    scaled = pooled * lax.rsqrt(jnp.sum(pooled * pooled, axis=-1, keepdims=True) + unit_eps)
    return scaled.reshape(-1, D)


def attend(query_rows, key_rows, value_rows, segment):
    scores = jnp.einsum(
        "qhd,khd->hqk", query_rows, key_rows, preferred_element_type=jnp.float32
    ) * HEAD ** (-0.5)
    same = segment[:, None] == segment[None, :]
    scores = jnp.where(same[None], scores, masked_value)
    row_top = jnp.max(scores, axis=-1, keepdims=True)
    raw = jnp.exp(scores - row_top)
    row_total = jnp.sum(raw, axis=-1, keepdims=True)
    probs = raw / row_total
    mixture = jnp.einsum(
        "hqk,khd->qhd", probs.astype(jnp.bfloat16), value_rows, preferred_element_type=jnp.float32
    )
    return (mixture, row_top + jnp.log(row_total))


def attend_back(query_rows, key_rows, value_rows, segment, log_total, grad_mixture):
    scores = jnp.einsum(
        "qhd,khd->hqk", query_rows, key_rows, preferred_element_type=jnp.float32
    ) * HEAD ** (-0.5)
    same = segment[:, None] == segment[None, :]
    scores = jnp.where(same[None], scores, masked_value)
    probs = jnp.exp(scores - log_total)
    grad_value = jnp.einsum(
        "hqk,qhd->khd", probs.astype(jnp.bfloat16), grad_mixture, preferred_element_type=jnp.float32
    )
    grad_probs = jnp.einsum(
        "qhd,khd->hqk", grad_mixture, value_rows, preferred_element_type=jnp.float32
    )
    row_dot = jnp.sum(grad_probs * probs, axis=-1, keepdims=True)
    grad_scores = (probs * (grad_probs - row_dot)).astype(jnp.bfloat16)
    grad_query = jnp.einsum(
        "hqk,khd->qhd", grad_scores, key_rows, preferred_element_type=jnp.float32
    ) * HEAD ** (-0.5)
    grad_key = jnp.einsum(
        "hqk,qhd->khd", grad_scores, query_rows, preferred_element_type=jnp.float32
    ) * HEAD ** (-0.5)
    return (grad_query, grad_key, grad_value)


def layer_forward(inputs, segment, weights):
    attn_in, attn_out, ff_in, ff_out, norm_gains, biases, ff_bias = weights
    count = inputs.shape[0]
    flat_rows = inputs.reshape(count * SEQ, D)
    zero_part = jnp.zeros((D,), jnp.float32)
    qkv_bias = jnp.concatenate([biases[0], zero_part, biases[1]])
    qkv_rows = (jnp.dot(flat_rows, attn_in, preferred_element_type=jnp.float32) + qkv_bias).astype(
        jnp.bfloat16
    )
    split_rows = qkv_rows.reshape(count, SEQ, 3, HEADS, HEAD)

    def one_row(packed):
        parts, segment_one = packed
        return attend(parts[:, 0], parts[:, 1], parts[:, 2], segment_one)

    mixture, log_total = lax.map(one_row, (split_rows, segment))
    mixture = mixture.reshape(count * SEQ, D).astype(jnp.bfloat16)
    attended = jnp.dot(mixture, attn_out, preferred_element_type=jnp.float32) + biases[2]
    hidden = flat_rows.astype(jnp.float32) + attended
    normed = norm_rows(hidden, norm_gains[0], biases[3])
    pre_act = (
        jnp.dot(normed.astype(jnp.bfloat16), ff_in, preferred_element_type=jnp.float32) + ff_bias
    )
    gelu_out = jax.nn.gelu(pre_act, approximate=False).astype(jnp.bfloat16)
    branch = jnp.dot(gelu_out, ff_out, preferred_element_type=jnp.float32) + biases[4]
    output = norm_rows(normed + branch, norm_gains[1], biases[5])
    return (output, (split_rows, log_total, mixture, hidden, normed, pre_act, branch))


def layer_backward(inputs, segment, weights, stored, grad_out):
    attn_in, attn_out, ff_in, ff_out, norm_gains, biases, ff_bias = weights
    split_rows, log_total, mixture, hidden, normed, pre_act, branch = stored
    count = inputs.shape[0]
    flat_rows = inputs.reshape(count * SEQ, D)
    norm_out, out_pull = jax.vjp(norm_rows, normed + branch, norm_gains[1], biases[5])
    grad_sum, grad_gain_out, grad_shift_out = out_pull(grad_out)
    grad_branch = grad_sum.astype(jnp.bfloat16)
    gelu_value, gelu_pull = jax.vjp(partial(jax.nn.gelu, approximate=False), pre_act)
    grad_ff_out = jnp.einsum(
        "tf,td->fd",
        gelu_value.astype(jnp.bfloat16),
        grad_branch,
        preferred_element_type=jnp.float32,
    )
    grad_bias_out = jnp.sum(grad_branch, axis=0, dtype=jnp.float32)
    grad_gelu = jnp.einsum("td,fd->tf", grad_branch, ff_out, preferred_element_type=jnp.float32)
    grad_pre = gelu_pull(grad_gelu)[0].astype(jnp.bfloat16)
    grad_ff_in = jnp.einsum(
        "td,tf->df", normed.astype(jnp.bfloat16), grad_pre, preferred_element_type=jnp.float32
    )
    grad_ff_bias = jnp.sum(grad_pre, axis=0, dtype=jnp.float32)
    grad_normed = grad_sum + jnp.einsum(
        "tf,df->td", grad_pre, ff_in, preferred_element_type=jnp.float32
    )
    norm_in, in_pull = jax.vjp(norm_rows, hidden, norm_gains[0], biases[3])
    grad_hidden, grad_gain_in, grad_shift_in = in_pull(grad_normed)
    grad_attended = grad_hidden.astype(jnp.bfloat16)
    grad_attn_out = jnp.einsum(
        "ti,to->io", mixture, grad_attended, preferred_element_type=jnp.float32
    )
    grad_bias_attn = jnp.sum(grad_attended, axis=0, dtype=jnp.float32)
    grad_mixture = jnp.einsum(
        "to,io->ti", grad_attended, attn_out, preferred_element_type=jnp.float32
    )
    grad_mixture = grad_mixture.astype(jnp.bfloat16).reshape(count, SEQ, HEADS, HEAD)

    def one_row(packed):
        parts, segment_one, total_one, grad_one = packed
        return attend_back(parts[:, 0], parts[:, 1], parts[:, 2], segment_one, total_one, grad_one)

    grad_query, grad_key, grad_value = lax.map(
        one_row, (split_rows, segment, log_total, grad_mixture)
    )
    grad_qkv = (
        jnp.stack([grad_query, grad_key, grad_value], axis=2)
        .reshape(count * SEQ, 3 * D)
        .astype(jnp.bfloat16)
    )
    grad_attn_in = jnp.einsum("ti,tj->ij", flat_rows, grad_qkv, preferred_element_type=jnp.float32)
    grad_bias_qkv = jnp.sum(grad_qkv, axis=0, dtype=jnp.float32)
    grad_inputs = grad_hidden + jnp.einsum(
        "tj,ij->ti", grad_qkv, attn_in, preferred_element_type=jnp.float32
    )
    grad_gains = jnp.stack([grad_gain_in, grad_gain_out])
    grad_biases = jnp.stack(
        [
            grad_bias_qkv[:D],
            grad_bias_qkv[2 * D :],
            grad_bias_attn,
            grad_shift_in,
            grad_bias_out,
            grad_shift_out,
        ]
    )
    return (
        grad_inputs,
        (
            grad_attn_in,
            grad_attn_out,
            grad_ff_in,
            grad_ff_out,
            grad_gains,
            grad_biases,
            grad_ff_bias,
        ),
    )


def contrast_part(final_rows, lengths, partner_ids, group_row):
    unit_local, unit_pull = jax.vjp(lambda value: pool_unit(value, lengths), final_rows)
    table = lax.all_gather(unit_local, "dp", axis=0, tiled=True)
    local_count = unit_local.shape[0]
    total_count = table.shape[0]
    norm_count = float(MICRO * total_count)
    offset = lax.axis_index("dp") * local_count
    own_ids = offset + jnp.arange(local_count, dtype=jnp.int32)
    column_ids = jnp.arange(total_count, dtype=jnp.int32)
    chosen = (column_ids[None, :] == partner_ids[:, None]).astype(jnp.float32)
    own_groups = lax.dynamic_slice_in_dim(group_row, offset, local_count)
    logits = contrast_scale * jnp.dot(unit_local, table.T, precision=highest)
    allowed = (own_groups[:, None] == group_row[None, :]) & (
        own_ids[:, None] != column_ids[None, :]
    )
    masked = jnp.where(allowed, logits, masked_value)
    row_top = jnp.max(masked, axis=1, keepdims=True)
    raw = jnp.exp(masked - row_top)
    row_total = jnp.sum(raw, axis=1, keepdims=True)
    loss_part = (
        jnp.sum(row_top[:, 0] + jnp.log(row_total[:, 0]) - jnp.sum(chosen * logits, axis=1))
        / norm_count
    )
    grad_logits = (raw / row_total - chosen) * contrast_scale
    grad_table = jnp.dot(grad_logits.T, unit_local, precision=highest)
    grad_unit = jnp.dot(grad_logits, table, precision=highest) + lax.psum_scatter(
        grad_table, "dp", scatter_dimension=0, tiled=True
    )
    return (loss_part, unit_pull(grad_unit)[0])


def local(
    tokens,
    out_cotangent,
    lengths,
    partner,
    group_ids,
    attn_in,
    attn_out,
    ff_in,
    ff_out,
    norm_gains,
    biases,
    ff_bias,
):
    gathered = (
        lax.all_gather(attn_in[0].astype(jnp.bfloat16), "dp", axis=0, tiled=True),
        lax.all_gather(attn_out[0].astype(jnp.bfloat16), "dp", axis=0, tiled=True),
        lax.all_gather(ff_in[0].astype(jnp.bfloat16), "dp", axis=0, tiled=True),
        lax.all_gather(ff_out[0].astype(jnp.bfloat16), "dp", axis=0, tiled=True),
        lax.all_gather(norm_gains[0].astype(jnp.bfloat16), "dp", axis=1, tiled=True),
        lax.all_gather(biases[0].astype(jnp.bfloat16), "dp", axis=1, tiled=True),
        lax.all_gather(ff_bias[0].astype(jnp.bfloat16), "dp", axis=0, tiled=True),
    )
    weights = (
        gathered[0],
        gathered[1],
        gathered[2],
        gathered[3],
        gathered[4].astype(jnp.float32),
        gathered[5].astype(jnp.float32),
        gathered[6].astype(jnp.float32),
    )
    leading = lax.axis_index("section") == 0
    segments = [segment_rows(lengths[micro]) for micro in range(MICRO)]
    received = jnp.zeros_like(tokens[0])
    inputs_at = []
    segment_at = []
    stored_at = []
    outputs_at = []
    grad_final_at = []
    loss_sum = jnp.zeros((), jnp.float32)
    for moment in range(MICRO + 1):
        early = min(moment, MICRO - 1)
        late = max(moment - 1, 0)
        inputs = jnp.where(leading, tokens[early], received)
        segment = jnp.where(leading, segments[early], segments[late])
        output, stored = layer_forward(inputs, segment, weights)
        output_rows = output.reshape(inputs.shape)
        if moment < MICRO:
            received = passed_along(output_rows.astype(jnp.bfloat16), "section", 1)
        inputs_at.append(inputs)
        segment_at.append(segment)
        stored_at.append(stored)
        outputs_at.append(output_rows.astype(jnp.bfloat16))
        if moment >= 1:
            loss_part, grad_final = contrast_part(
                output_rows, lengths[late], partner[late], group_ids[late]
            )
            loss_sum = loss_sum + jnp.where(leading, 0.0, loss_part)
            grad_final_at.append(grad_final + out_cotangent[late].astype(jnp.float32))
    contrast_loss = lax.psum(loss_sum, ("section", "dp"))
    row_count = tokens.shape[1] * SEQ
    grad_received = jnp.zeros((row_count, D), jnp.bfloat16)
    grad_inputs_at = []
    accum = None
    for moment in range(MICRO + 1):
        upper = max(MICRO - 1 - moment, 0)
        lower = min(MICRO - moment, MICRO - 1)
        inputs = jnp.where(leading, inputs_at[lower], inputs_at[upper + 1])
        segment = jnp.where(leading, segment_at[lower], segment_at[upper + 1])
        stored = jax.tree.map(
            lambda early_val, late_val: jnp.where(leading, early_val, late_val),
            stored_at[lower],
            stored_at[upper + 1],
        )
        grad_out = jnp.where(
            leading, grad_received.astype(jnp.float32), grad_final_at[upper].reshape(row_count, D)
        )
        grad_inputs, grads = layer_backward(inputs, segment, weights, stored, grad_out)
        if moment < MICRO:
            grad_received = passed_along(grad_inputs.astype(jnp.bfloat16), "section", -1)
        valid = jnp.where(leading, 1.0 if moment >= 1 else 0.0, 1.0 if moment < MICRO else 0.0)
        grads = tuple((piece * valid for piece in grads))
        grad_inputs_at.append(grad_inputs.reshape(inputs.shape))
        accum = grads if accum is None else jax.tree.map(jnp.add, accum, grads)
    shares = (
        lax.psum_scatter(accum[0], "dp", scatter_dimension=0, tiled=True),
        lax.psum_scatter(accum[1], "dp", scatter_dimension=0, tiled=True),
        lax.psum_scatter(accum[2], "dp", scatter_dimension=0, tiled=True),
        lax.psum_scatter(accum[3], "dp", scatter_dimension=0, tiled=True),
        lax.psum_scatter(accum[4], "dp", scatter_dimension=1, tiled=True),
        lax.psum_scatter(accum[5], "dp", scatter_dimension=1, tiled=True),
        lax.psum_scatter(accum[6], "dp", scatter_dimension=0, tiled=True),
    )
    hidden_states = jnp.stack(
        [jnp.where(leading, outputs_at[micro], outputs_at[micro + 1]) for micro in range(MICRO)]
    )
    hidden_grads = jnp.stack(
        [
            jnp.where(leading, grad_inputs_at[MICRO - micro], grad_inputs_at[MICRO - 1 - micro])
            for micro in range(MICRO)
        ]
    )
    return (
        contrast_loss,
        hidden_states[None],
        hidden_grads[None],
        shares[0][None],
        shares[1][None],
        shares[2][None],
        shares[3][None],
        shares[4][None],
        shares[5][None],
        shares[6][None],
    )


def solution(mesh):
    return jax.shard_map(
        local,
        mesh=mesh,
        in_specs=(
            P(None, "dp", None, None),
            P(None, "dp", None, None),
            P(None, "dp", None),
            P(None, "dp"),
            P(),
            P("section", "dp", None),
            P("section", "dp", None),
            P("section", "dp", None),
            P("section", "dp", None),
            P("section", None, "dp"),
            P("section", None, "dp"),
            P("section", "dp"),
        ),
        out_specs=(
            P(),
            P("section", None, "dp", None, None),
            P("section", None, "dp", None, None),
            P("section", "dp", None),
            P("section", "dp", None),
            P("section", "dp", None),
            P("section", "dp", None),
            P("section", None, "dp"),
            P("section", None, "dp"),
            P("section", "dp"),
        ),
        check_vma=False,
    )
```

profile of v0, /device:TPU:0, one launch (start us, length us, event | category | flops | bytes accessed | tf_op | source)
XLA Modules:
  0.0 1268.3 jit_solution(1732946469144147723)
XLA Ops:
  15.4 25.2 %all-gather.1 = bf16[1,6,768]{1,0,2:T(2,128)(2,1)S(1)} all-gather(bf16[1,6,48]{1,0,2:T(2,128)(2,1)S(1)} %copy.165), channel_id=3, replica_groups=mesh['section'=2,'dp'=16] {'dp'}, dimensions={2}, use_global_device_ids=true | all-gather | bytes 9792 | tf_op jit(solution)/shard_map/all_gather | solution.py:255
  41.8 20.0 %all-gather.3 = bf16[1,2,768]{1,0,2:T(2,128)(2,1)S(1)} all-gather(bf16[1,2,48]{1,0,2:T(2,128)(2,1)S(1)} %copy.168), channel_id=5, replica_groups=mesh['section'=2,'dp'=16] {'dp'}, dimensions={2}, use_global_device_ids=true | all-gather | bytes 3264 | tf_op jit(solution)/shard_map/all_gather | solution.py:254
  66.7 31.2 %all-reduce = bf16[3072]{0:T(1024)(128)(2,1)S(1)} all-reduce(bf16[3072]{0:T(1024)(128)(2,1)S(1)} %dynamic-update-slice), channel_id=7, replica_groups=mesh['section'=2,'dp'=16] {'dp'}, use_global_device_ids=true, to_apply=%add | all-reduce | flops 3072 | bytes 12288
  100.5 12.8 %slice_reduce_fusion.2 = (f32[768]{0:T(1024)S(1)}, f32[768]{0:T(1024)S(1)}, f32[768]{0:T(1024)S(1)}, f32[768]{0:T(1024)S(1)}, f32[768]{0:T(1024)S(1)}, /*index=5*/f32[768]{0:T(1024)S(1)}) fusion(f32[1,6,768]{1,0,2:T(1,128)S(1)} %convert_element_type.534), kind=kLoop, calls=%fused_computation.365 | loop fusion | bytes 36864 | tf_op jit(solution)/shard_map/slice | solution.py:120
  140.0 19.5 %all-gather.18.cloned.1.call-done = bf16[1,768,3072]{2,1,0:T(8,128)(2,1)} async-done(((bf16[1,48,3072]{2,1,0:T(8,128)(2,1)}), bf16[1,768,3072]{2,1,0:T(8,128)(2,1)}) %all-gather.18.cloned.1.call-update) | async-done | bytes 4718608 | tf_op jit(solution)/shard_map/all_gather | solution.py:252
  166.5 47.5 %all-gather.20.cloned.1.call-done = bf16[1,3072,768]{2,1,0:T(8,128)(2,1)} async-done(((bf16[1,192,768]{2,1,0:T(8,128)(2,1)}), bf16[1,3072,768]{2,1,0:T(8,128)(2,1)}) %all-gather.20.cloned.1.call-update) | async-done | bytes 4718608 | tf_op jit(solution)/shard_map/all_gather | solution.py:253
  214.0 20.6 %fusion.355 = (f32[512]{0:T(512)S(1)}, f32[512,768]{1,0:T(8,128)S(1)}, f32[512,768]{1,0:T(8,128)}) fusion(f32[768]{0:T(1024)S(1)} %get-tuple-element.204, f32[768]{0:T(1024)S(1)} %get-tuple-element.205, f32[768]{0:T(1024)S(1)} %get-tuple-element.210, f32[512]{0:T(512)S(1)} %add_rsqrt_fusion.3, f32[512,768]{1,0:T(8,128)S(1)} %get-tuple-element.319, ...), kind=kOutput, calls=%fused_computation.599 | convolution fusion | flops 2522480128 | bytes 15756288 | tf_op jit(solution)/shard_map/dot_general | solution.py:120
  244.5 13.5 %collective-permute-done = bf16[1,512,768]{2,1,0:T(8,128)(2,1)S(1)} collective-permute-done((bf16[1,512,768]{2,1,0:T(8,128)(2,1)}, bf16[1,512,768]{2,1,0:T(8,128)(2,1)S(1)}, u32[]{:S(2)}, u32[]{:S(2)}) %collective-permute-start) | collective-permute-done | bytes 786464 | tf_op jit(solution)/shard_map/ppermute | solution.py:25
  278.6 20.4 %multiply_convert_fusion.5 = (bf16[512,3072]{1,0:T(8,128)(2,1)S(1)}, f32[512,3072]{1,0:T(8,128)}, f32[512,3072]{1,0:T(8,128)}) fusion(f32[3072]{0:T(1024)S(1)} %convert_element_type.537, bf16[1,768,3072]{2,1,0:T(8,128)(2,1)} %all-gather.18.cloned.1.call-done, f32[768]{0:T(1024)S(1)} %get-tuple-element.205, f32[768]{0:T(1024)S(1)} %get-tuple-element.210, ...), kind=kOutput, calls=%fused_computation.90 | convolution fusion | flops 2521694208 | bytes 22042624 | tf_op jit(solution)/shard_map/dot_general | solution.py:117
  313.6 19.5 %all-gather.7 = f32[16,4,768]{2,1,0:T(4,128)S(1)} all-gather(f32[1,4,768]{2,1,0:T(4,128)S(1)} %multiply_bitcast_fusion.7), channel_id=1, replica_groups=mesh['section'=2,'dp'=16] {'dp'}, dimensions={0}, use_global_device_ids=true | all-gather | bytes 208896 | tf_op jit(solution)/shard_map/all_gather | solution.py:206
  363.4 20.9 %fusion.15 = (f32[512,3072]{1,0:T(8,128)}, f32[512,3072]{1,0:T(8,128)}, f32[512,3072]{1,0:T(8,128)S(1)}) fusion(f32[512,3072]{1,0:T(8,128)} %get-tuple-element.325, f32[3072]{0:T(1024)S(1)} %copy-done.119, pred[]{:T(512)S(6)} %eq.198, bf16[1,768,3072]{2,1,0:T(8,128)(2,1)} %all-gather.18.cloned.1.call-done, f32[512,768]{1,0:T(8,128)S(1)} %get-tuple-element.330, ...), kind=kOutput, calls=%fused_computation.41 | convolution fusion | flops 2520121344 | bytes 31479808 | tf_op jit(solution)/shard_map/dot_general | solution.py:117
  384.5 18.8 %fusion.337 = (f32[512]{0:T(512)S(1)}, f32[512,768]{1,0:T(8,128)}, f32[512]{0:T(512)S(1)}, f32[512,768]{1,0:T(8,128)}, f32[512]{0:T(512)S(1)}, /*index=5*/f32[51...) fusion(f32[512,768]{1,0:T(8,128)S(1)} %copy-done.27, ...), kind=kOutput, calls=%fused_computation.586 | convolution fusion | flops 2530735616 | bytes 26782720 | tf_op jit(solution)/shard_map/dot_general | solution.py:120
  405.7 18.2 %all-gather.8 = f32[16,4,768]{2,1,0:T(4,128)S(1)} all-gather(f32[1,4,768]{2,1,0:T(4,128)S(1)} %multiply_bitcast_fusion.6), channel_id=1, replica_groups=mesh['section'=2,'dp'=16] {'dp'}, dimensions={0}, use_global_device_ids=true | all-gather | bytes 208896 | tf_op jit(solution)/shard_map/all_gather | solution.py:206
  445.9 85.9 %all-reduce.7.cloned.1.call-done = (f32[64,768]{1,0:T(8,128)}, f32[64,768]{1,0:T(8,128)}) async-done(((f32[64,768]{1,0:T(8,128)}, f32[64,768]{1,0:T(8,128)}), (f32[64,768]{1,0:T(8,128)}, f32[64,768]{1,0:T(8,128)})) %all-reduce.7.cloned.1.call-update) | async-done | bytes 393232
  540.1 9.8 convert_reduce_fusion.2
  560.3 7.4 fusion.109
  567.6 9.7 multiply_reduce_fusion.2
  577.3 7.4 multiply_convert_fusion.2
  599.0 15.3 %collective-permute-done.2 = bf16[512,768]{1,0:T(8,128)(2,1)} collective-permute-done((bf16[512,768]{1,0:T(8,128)(2,1)}, bf16[512,768]{1,0:T(8,128)(2,1)}, u32[]{:S(2)}, u32[]{:S(2)}) %collective-permute-start.2) | collective-permute-done | bytes 786464 | tf_op jit(solution)/shard_map/ppermute | solution.py:25
  620.1 9.8 convert_reduce_fusion.1
  639.3 7.4 fusion.115
  646.6 9.9 multiply_reduce_fusion.1
  680.3 12.0 collective-permute-done.3
  697.1 21.1 %convert_reduce_fusion = (f32[3072]{0:T(1024)}, bf16[512,3072]{1,0:T(8,128)(2,1)S(1)}) fusion(bf16[512,768]{1,0:T(8,128)(2,1)S(1)} %get-tuple-element.227, bf16[1,3072,768]{2,1,0:T(8,128)(2,1)S(1)} %bitcast.450, f32[512,3072]{1,0:T(8,128)} %get-tuple-element.325, f32[512,3072]{1,0:T(8,128)} %fusion.80, f32[3072]{0:T(1024)S(1)} %copy-done.120, pred[]{:T(512)S(6)} %eq.198), kind=kOutput, calls=%fused_computation.44 | convolution fusion | flops 2537026560 | bytes 21258240 | tf_op jit(solution)/shard_map/td,fd->tf/dot_general | solution.py:141
  734.9 9.8 multiply_reduce_fusion
  789.8 9.1 multiply_add_fusion.1
  809.3 19.9 %multiply_add_fusion = f32[3072,768]{1,0:T(8,128)} fusion(f32[3072,768]{1,0:T(8,128)S(1)} %fusion.367, f32[3072,768]{1,0:T(8,128)S(1)} %fusion.95, bf16[512,768]{1,0:T(8,128)(2,1)S(1)} %copy-done.74, f32[]{:T(128)S(6)} %select_n.345, f32[]{:T(128)S(6)} %select_n.342, f32[512,3072]{1,0:T(8,128)} %fusion.80, f32[512,3072]{1,0:T(8,128)} %get-tuple-element.325, ...), kind=kOutput, calls=%fused_computation.29 | convolution fusion | flops 2532311040 | bytes 41693192 | tf_op jit(solution)/shard_map/tf,td->fd/dot_general | solution.py:134
  833.1 37.7 %psum.7 = f32[]{:T(128)} all-reduce(f32[]{:T(128)S(6)} %add.492), channel_id=1, replica_groups=mesh['section'=2,'dp'=16] {'section','dp'}, use_global_device_ids=true, to_apply=%region_32.33 | all-reduce | flops 1 | bytes 8 | tf_op jit(solution)/shard_map/psum | solution.py:295
  874.2 60.1 %all-reduce.3 = f32[3072]{0:T(1024)S(1)} all-reduce(f32[3072]{0:T(1024)S(1)} %multiply_add_fusion.16), channel_id=17, replica_groups=mesh['section'=2,'dp'=16] {'dp'}, use_global_device_ids=true, to_apply=%region_90.91.clone | all-reduce | flops 3072 | bytes 24576
  944.4 85.4 %reduce-scatter.11.cloned.1.call-done = f32[48,2304]{1,0:T(8,128)} async-done(((f32[768,2304]{1,0:T(8,128)}), f32[48,2304]{1,0:T(8,128)}) %reduce-scatter.11.cloned.1.call-update) | async-done | bytes 442384 | tf_op jit(solution)/shard_map/reduce_scatter | solution.py:321
  1029.7 116.0 %reduce-scatter.15.cloned.1.call-done = f32[48,3072]{1,0:T(8,128)} async-done(((f32[768,3072]{1,0:T(8,128)}), f32[48,3072]{1,0:T(8,128)}) %reduce-scatter.15.cloned.1.call-update) | async-done | bytes 589840 | tf_op jit(solution)/shard_map/reduce_scatter | solution.py:323
  1145.7 115.8 %reduce-scatter.17.cloned.1.call-done = f32[192,768]{1,0:T(8,128)} async-done(((f32[3072,768]{1,0:T(8,128)}), f32[192,768]{1,0:T(8,128)}) %reduce-scatter.17.cloned.1.call-update) | async-done | bytes 589840 | tf_op jit(solution)/shard_map/reduce_scatter | solution.py:324
  (701 shorter events, 310.0 us)
Async XLA Ops:
  7.2 111.6 %copy-start.153 = (s32[2,1,4]{2,1,0:T(1,128)S(1)}, s32[2,1,4]{2,1,0:T(1,128)}, u32[]{:S(2)}) copy-start(s32[2,1,4]{2,1,0:T(1,128)} %param.14) | copy-start | bytes 100
  7.2 111.0 %copy-start.170 = (s32[2,4]{1,0:T(2,128)S(1)}, s32[2,4]{1,0:T(2,128)}, u32[]{:S(2)}) copy-start(s32[2,4]{1,0:T(2,128)} %param.15) | copy-start | bytes 100
  7.2 112.3 %copy-start.41 = (bf16[2,1,512,768]{3,2,1,0:T(8,128)(2,1)S(1)}, bf16[2,1,512,768]{3,2,1,0:T(8,128)(2,1)}, u32[]{:S(2)}) copy-start(bf16[2,1,512,768]{3,2,1,0:T(8,128)(2,1)} %param.12) | copy-start | bytes 4718596
  7.2 112.3 %all-gather.14.cloned.1.call-start = ((), (), s32[]{:S(2)}) async-start(), calls=%async_computation.10 | async-start | bytes 3760128 | tf_op jit(solution)/shard_map/all_gather | solution.py:250
  9.1 127.9 %all-gather.16.cloned.1.call-start = ((), (), s32[]{:S(2)}) async-start(), calls=%async_computation.11 | async-start | bytes 1253376 | tf_op jit(solution)/shard_map/all_gather | solution.py:251
  10.7 148.7 %all-gather.18.cloned.1.call-start = ((), (), s32[]{:S(2)}) async-start(), calls=%async_computation.12 | async-start | bytes 5013504 | tf_op jit(solution)/shard_map/all_gather | solution.py:252
  12.6 201.4 %all-gather.20.cloned.1.call-start = ((), (), s32[]{:S(2)}) async-start(), calls=%async_computation.13 | async-start | bytes 5013504 | tf_op jit(solution)/shard_map/all_gather | solution.py:253
  14.5 517.3 %all-reduce.7.cloned.1.call-start = ((), (), s32[]{:S(2)}) async-start(), calls=%async_computation.16 | async-start | bytes 786432
  97.9 180.7 %copy-start.118 = (f32[3072]{0:T(1024)}, f32[3072]{0:T(1024)S(1)}, u32[]{:S(2)}) copy-start(f32[3072]{0:T(1024)S(1)} %convert_element_type.537) | copy-start | bytes 36868
  113.3 163.9 %copy-start.151 = (f32[768]{0:T(1024)}, f32[768]{0:T(1024)S(1)}, u32[]{:S(2)}) copy-start(f32[768]{0:T(1024)S(1)} %get-tuple-element.206) | copy-start | bytes 9220
  113.3 185.7 %copy-start.113 = (f32[768]{0:T(1024)}, f32[768]{0:T(1024)S(1)}, u32[]{:S(2)}) copy-start(f32[768]{0:T(1024)S(1)} %get-tuple-element.205) | copy-start | bytes 9220
  113.4 185.7 %copy-start.149 = (f32[768]{0:T(1024)}, f32[768]{0:T(1024)S(1)}, u32[]{:S(2)}) copy-start(f32[768]{0:T(1024)S(1)} %get-tuple-element.204) | copy-start | bytes 9220
  113.4 196.7 %copy-start.84 = (f32[768]{0:T(1024)}, f32[768]{0:T(1024)S(1)}, u32[]{:S(2)}) copy-start(f32[768]{0:T(1024)S(1)} %get-tuple-element.209) | copy-start | bytes 9220
  113.4 144.6 %copy-start.121 = (f32[2304]{0:T(1024)}, f32[2304]{0:T(1024)S(1)}, u32[]{:S(2)}) copy-start(f32[2304]{0:T(1024)S(1)} %pad_maximum_fusion) | copy-start | bytes 27652
  118.2 180.9 %copy-start.82 = (f32[768]{0:T(1024)}, f32[768]{0:T(1024)S(1)}, u32[]{:S(2)}) copy-start(f32[768]{0:T(1024)S(1)} %get-tuple-element.210) | copy-start | bytes 9220
  118.2 576.3 %copy-start.78 = (f32[768]{0:T(1024)}, f32[768]{0:T(1024)S(1)}, u32[]{:S(2)}) copy-start(f32[768]{0:T(1024)S(1)} %get-tuple-element.211) | copy-start | bytes 9220
  237.1 20.9 %collective-permute-start = (bf16[1,512,768]{2,1,0:T(8,128)(2,1)}, bf16[1,512,768]{2,1,0:T(8,128)(2,1)S(1)}, u32[]{:S(2)}, u32[]{:S(2)}) collective-permute-start(bf16[1,512,768]{2,1,0:T(8,128)(2,1)} %fusion.333), channel_id=1, source_target_pairs={{0,16},{1,17},{2,18},{3,19},{4,20},{5,21},{6,22},{7,23},{8,24},{9,... | collective-permute-start | bytes 2359304 | tf_op jit(solution)/shard_map/ppermute | solution.py:25
  266.8 81.1 %copy-start.1 = (bf16[512,2304]{0,1:T(8,128)(2,1)}, bf16[512,2304]{0,1:T(8,128)(2,1)S(1)}, u32[]{:S(2)}) copy-start(bf16[512,2304]{0,1:T(8,128)(2,1)S(1)} %copy.169) | copy-start | bytes 7077892
  304.9 30.6 %collective-permute-start.1 = (bf16[1,512,768]{2,1,0:T(8,128)(2,1)S(1)}, bf16[1,512,768]{2,1,0:T(8,128)(2,1)}, u32[]{:S(2)}, u32[]{:S(2)}) collective-permute-start(bf16[1,512,768]{2,1,0:T(8,128)(2,1)S(1)} %bitcast.418), channel_id=1, source_target_pairs={{0,16},{1,17},{2,18},{3,19},{4,20},{5,21},{6,22},{7,23},{8,24},{9,... | collective-permute-start | bytes 2359304 | tf_op jit(solution)/shard_map/ppermute | solution.py:25
  427.4 104.4 %copy-start.139 = (f32[4]{0:T(128)}, f32[4]{0:T(128)S(1)}, u32[]{:S(2)}) copy-start(f32[4]{0:T(128)S(1)} %get-tuple-element.258) | copy-start | bytes 52
  428.9 102.9 %copy-start.144 = (f32[4]{0:T(128)}, f32[4]{0:T(128)S(1)}, u32[]{:S(2)}) copy-start(f32[4]{0:T(128)S(1)} %fusion.242) | copy-start | bytes 52
  443.5 498.1 %reduce-scatter.19.cloned.1.call-start = ((), (), s32[]{:S(2)}) async-start(), calls=%async_computation.14 | async-start | bytes 417792
  443.6 96.5 %copy-start.89 = (f32[512]{0:T(512)}, f32[512]{0:T(512)S(1)}, u32[]{:S(2)}) copy-start(f32[512]{0:T(512)S(1)} %broadcast_multiply_fusion.1) | copy-start | bytes 6148
  593.6 20.7 %collective-permute-start.2 = (bf16[512,768]{1,0:T(8,128)(2,1)}, bf16[512,768]{1,0:T(8,128)(2,1)}, u32[]{:S(2)}, u32[]{:S(2)}) collective-permute-start(bf16[512,768]{1,0:T(8,128)(2,1)} %get-tuple-element.344), channel_id=1, source_target_pairs={{16,0},{17,1},{18,2},{19,3},{20,4},{21,5},{22,6},{23,7},{24,8},{25... | collective-permute-start | bytes 2359304 | tf_op jit(solution)/shard_map/ppermute | solution.py:25
  672.7 19.6 %collective-permute-start.3 = (bf16[512,768]{1,0:T(8,128)(2,1)}, bf16[512,768]{1,0:T(8,128)(2,1)S(1)}, u32[]{:S(2)}, u32[]{:S(2)}) collective-permute-start(bf16[512,768]{1,0:T(8,128)(2,1)} %get-tuple-element.286), channel_id=1, source_target_pairs={{16,0},{17,1},{18,2},{19,3},{20,4},{21,5},{22,6},{23,7},{24,8},{25... | collective-permute-start | bytes 2359304 | tf_op jit(solution)/shard_map/ppermute | solution.py:25
  756.9 186.1 %reduce-scatter.21.cloned.1.call-start = ((), (), s32[]{:S(2)}) async-start(), calls=%async_computation.15 | async-start | bytes 417792
  761.3 183.1 %reduce-scatter.13.cloned.1.call-start = ((), (), s32[]{:S(2)}) async-start(), calls=%async_computation.7 | async-start | bytes 2506752 | tf_op jit(solution)/shard_map/reduce_scatter | solution.py:322
  766.5 263.2 %reduce-scatter.11.cloned.1.call-start = ((), (), s32[]{:S(2)}) async-start(), calls=%async_computation.6 | async-start | bytes 7520256 | tf_op jit(solution)/shard_map/reduce_scatter | solution.py:321
  778.0 367.7 %reduce-scatter.15.cloned.1.call-start = ((), (), s32[]{:S(2)}) async-start(), calls=%async_computation.8 | async-start | bytes 10027008 | tf_op jit(solution)/shard_map/reduce_scatter | solution.py:323
  798.9 462.6 %reduce-scatter.17.cloned.1.call-start = ((), (), s32[]{:S(2)}) async-start(), calls=%async_computation.9 | async-start | bytes 10027008 | tf_op jit(solution)/shard_map/reduce_scatter | solution.py:324
  829.3 105.6 %copy-start.19 = (bf16[1,512,3,12,64]{1,4,3,2,0:T(8,128)(2,1)S(1)}, bf16[1,512,3,12,64]{1,4,3,2,0:T(8,128)(2,1)}, u32[]{:S(2)}) copy-start(bf16[1,512,3,12,64]{1,4,3,2,0:T(8,128)(2,1)} %get-tuple-element.231) | copy-start | bytes 7077892
  829.3 105.6 %copy-start.136 = (f32[512]{0:T(512)S(1)}, f32[512]{0:T(512)}, u32[]{:S(2)}) copy-start(f32[512]{0:T(512)} %copy-done.135) | copy-start | bytes 6148
  (204 other events, 2777.6 us)
Sparse Core Ops, SparseCore 0:
  10.9 53.1 all-gather.13
  67.0 37.2 all-gather.15
  107.1 52.3 all-gather.17
  162.2 51.7 all-gather.19
  443.6 88.1 all-reduce.6
  757.0 53.8 reduce-scatter.18
  814.4 54.6 reduce-scatter.20
  873.9 62.1 reduce-scatter.12
  940.7 88.9 reduce-scatter.10
  1034.8 110.8 reduce-scatter.14
  1150.4 111.1 reduce-scatter.16
where the time goes:
time: 1270 us
  waiting for transfers between devices  511 us (40%)
  matrix products  359 us (28%)
  blocking collectives  212 us (17%)
  other arithmetic  88 us (7%)
  local copies, waits for them, and re-layouts  66.2 us (5%)
  between operations  20.6 us (2%)
    reduce_scatter x1, waiting for transfers between devices, local(): lax.psum_scatter(accum[2], 'dp', scatter_dimension=0, tiled=True)  116 us
    reduce_scatter x1, waiting for transfers between devices, local(): lax.psum_scatter(accum[3], 'dp', scatter_dimension=0, tiled=True)  116 us
    unnamed x2, blocking collectives  91.3 us
    unnamed x14, waiting for transfers between devices  86.1 us
    reduce_scatter x1, waiting for transfers between devices, local(): lax.psum_scatter(accum[0], 'dp', scatter_dimension=0, tiled=True)  85.4 us
    dot_general x3, matrix products, layer_forward(): jnp.dot(normed.astype(jnp.bfloat16), ff_in, preferred_element_type=jnp.fl...  48.4 us
    all_gather x1, waiting for transfers between devices, local(): lax.all_gather(ff_out[0].astype(jnp.bfloat16), 'dp', axis=0, tiled=True)  47.5 us
    dot_general x3, matrix products, layer_forward(): jnp.dot(gelu_out, ff_out, preferred_element_type=jnp.float32) + biases[4]  43.4 us
  transfers between devices with their start and end apart: 15, of which 9 were waited for; matrix products, arithmetic and copies ran while one was open for 13% of the time, Pallas kernels for 0%

commit v1 on v0

v1 whole, which is shorter than its diff:
```python
from functools import partial

import jax
import jax.numpy as jnp
from jax import lax
from jax.experimental import pallas as pl
from jax.experimental.pallas import tpu as pltpu
from jax.sharding import PartitionSpec as P

D = 768
HEADS = 12
HEAD = 64
SEQ = 512
MICRO = 2
FF = 3072

bf16 = jnp.bfloat16
f32 = jnp.float32
highest = lax.Precision.HIGHEST
norm_eps = 1e-05
unit_eps = 1e-06
masked_value = -1000000000.0
contrast_scale = 10.0
vmem_limit = 56 * 2**20


def swapped(value, axis, mask):
    count = lax.axis_size(axis)
    return lax.ppermute(value, axis, [(i, i ^ mask) for i in range(count)])


def ring_order(chips):
    return list(range(0, chips, 2)) + list(range(chips - 1, 0, -2))


def ring_hop(value, backward=False):
    chips = lax.axis_size("dp") // 2
    order = ring_order(chips)
    pairs = []
    for place in range(chips):
        for core in range(2):
            step = 1 if core == 0 else -1
            pairs.append((order[place] * 2 + core, order[(place + step) % chips] * 2 + core))
    return lax.ppermute(value, "dp", pairs)


def ring_place():
    me = lax.axis_index("dp").astype(jnp.int32)
    chips = lax.axis_size("dp") // 2
    order = ring_order(chips)
    places = [order.index(chip) for chip in range(chips)]
    place = jnp.asarray(places, jnp.int32)[me // 2]
    core = me % 2
    return place, 1 - 2 * core, core


def owners(steps, cores):
    chips = lax.axis_size("dp") // 2
    place, way, core = ring_place()
    order = jnp.asarray(ring_order(chips), jnp.int32)
    found = order[(place + way * jnp.asarray(steps, jnp.int32)) % chips] * 2
    return found + (core + jnp.asarray(cores, jnp.int32)) % 2


def fast_ring():
    return lax.axis_size("dp") == 16


def gather_pieces(shard):
    mate = swapped(shard, "dp", 1)
    first = jnp.stack([shard, mate])
    one = ring_hop(first)
    one_mate = swapped(one, "dp", 1)
    two = ring_hop(one)
    two_mate = swapped(two, "dp", 1)
    three = ring_hop(two)
    three_mate = swapped(three, "dp", 1)
    four = ring_hop(three[:1])
    four_mate = swapped(four, "dp", 1)
    return [first, one, two, three, four, one_mate, two_mate, three_mate, four_mate]


def gather_owners():
    steps = [0, 0, -1, -1, -2, -2, -3, -3, -4, 1, 1, 2, 2, 3, 3, 4]
    cores = [0, 1, 0, 1, 0, 1, 0, 1, 0, 1, 0, 1, 0, 1, 0, 1]
    return owners(steps, cores)


def assemble_kernel(blocks, counts, owner_ref, *refs):
    pieces, outs, sems = refs[: len(counts)], refs[len(counts) : -1], refs[-1]
    copies = []
    at = 0
    for piece, count in zip(pieces, counts):
        for k in range(count):
            owner = owner_ref[at]
            row = 0
            for which, (out, (rows, columns)) in enumerate(zip(outs, blocks)):
                for block in range(columns):
                    start = pl.multiple_of(owner * rows, 16)
                    copies.append(
                        pltpu.make_async_copy(
                            piece.at[k, pl.ds(row, rows)],
                            out.at[pl.ds(start, rows), pl.ds(block * D, D)],
                            sems.at[len(copies)],
                        )
                    )
                    row += rows
            at += 1
    for copy in copies:
        copy.start()
    for copy in copies:
        copy.wait()


def assemble(pieces, blocks, owner):
    counts = [piece.shape[0] for piece in pieces]
    total = sum(counts)
    return pl.pallas_call(
        partial(assemble_kernel, blocks, counts),
        out_shape=[jax.ShapeDtypeStruct((total * rows, columns * D), bf16) for rows, columns in blocks],
        in_specs=[pl.BlockSpec(memory_space=pltpu.SMEM)]
        + [pl.BlockSpec(memory_space=pl.ANY)] * len(pieces),
        out_specs=[pl.BlockSpec(memory_space=pltpu.VMEM)] * len(blocks),
        scratch_shapes=[pltpu.SemaphoreType.DMA((total * sum(c for _, c in blocks),))],
        compiler_params=pltpu.CompilerParams(vmem_limit_bytes=vmem_limit),
        name="assemble",
    )(owner, *pieces)


def deal_kernel(blocks, keep_ref, send_ref, *refs):
    ins, (keep_out, send_out, sems) = refs[: len(blocks)], refs[len(blocks) :]
    copies = []
    for table, out in ((keep_ref, keep_out), (send_ref, send_out)):
        for unit in range(8):
            owner = table[unit]
            row = 0
            for ref, (rows, columns) in zip(ins, blocks):
                for block in range(columns):
                    start = pl.multiple_of(owner * rows, 16)
                    copies.append(
                        pltpu.make_async_copy(
                            ref.at[pl.ds(start, rows), pl.ds(block * D, D)],
                            out.at[unit, pl.ds(row, rows)],
                            sems.at[len(copies)],
                        )
                    )
                    row += rows
    for copy in copies:
        copy.start()
    for copy in copies:
        copy.wait()


def deal(grads, blocks, keep, send):
    height = sum(rows * columns for rows, columns in blocks)
    return pl.pallas_call(
        partial(deal_kernel, blocks),
        out_shape=[jax.ShapeDtypeStruct((8, height, D), bf16)] * 2,
        in_specs=[pl.BlockSpec(memory_space=pltpu.SMEM)] * 2
        + [pl.BlockSpec(memory_space=pltpu.VMEM)] * len(grads),
        out_specs=[pl.BlockSpec(memory_space=pl.ANY)] * 2,
        scratch_shapes=[pltpu.SemaphoreType.DMA((16 * sum(c for _, c in blocks),))],
        compiler_params=pltpu.CompilerParams(vmem_limit_bytes=vmem_limit),
        name="deal",
    )(keep, send, *grads)


unit_steps = [1, 1, 2, 2, 3, 3, 4, 0]


def deal_tables():
    core = ring_place()[2]
    cores_keep = [0, 1, 0, 1, 0, 1]
    keep = owners(unit_steps, [0] * 8)
    send = owners([-step for step in unit_steps], [1] * 8)
    absolute = jnp.asarray(cores_keep, jnp.int32)
    keep = jnp.concatenate([keep[:6] // 2 * 2 + absolute, keep[6:]])
    send = jnp.concatenate([send[:6] // 2 * 2 + absolute, send[6:]])
    return keep, send, core


def reduce_units(keep, send, core):
    mine = keep.astype(f32) + swapped(send, "dp", 1).astype(f32)
    total = ring_hop(mine[6:7].astype(bf16))
    third = mine[4:6] + jnp.where(
        jnp.arange(2)[:, None, None] == core, total.astype(f32), jnp.zeros((), f32)
    )
    total = ring_hop(third.astype(bf16))
    total = ring_hop((mine[2:4] + total.astype(f32)).astype(bf16))
    total = ring_hop((mine[0:2] + total.astype(f32)).astype(bf16))
    own = lax.dynamic_index_in_dim(total, core, 0, keepdims=False)
    other = swapped(lax.dynamic_index_in_dim(total, 1 - core, 0, keepdims=False), "dp", 1)
    return mine[7] + own.astype(f32) + other.astype(f32)


def gather_small(value):
    me = lax.axis_index("dp")
    value = value[None]
    mask = 1
    while mask < lax.axis_size("dp"):
        other = swapped(value, "dp", mask)
        upper = (me & mask) != 0
        value = jnp.concatenate([jnp.where(upper, other, value), jnp.where(upper, value, other)])
        mask *= 2
    return value


def reduce_small(value):
    me = lax.axis_index("dp")
    mask = lax.axis_size("dp") // 2
    while mask >= 1:
        half = value.shape[0] // 2
        upper = (me & mask) != 0
        keep = jnp.where(upper, value[half:], value[:half])
        send = jnp.where(upper, value[:half], value[half:])
        value = keep + swapped(send, "dp", mask)
        mask //= 2
    return value[0]


def norm_rows(value, gain_row, shift_row):
    row_mean = jnp.mean(value, axis=-1, keepdims=True)
    centered = value - row_mean
    variance = jnp.mean(centered * centered, axis=-1, keepdims=True)
    return centered * lax.rsqrt(variance + norm_eps) * gain_row + shift_row


def pool_unit(final_rows, lengths):
    row_ends = jnp.cumsum(lengths, axis=-1, dtype=jnp.int32)
    row_starts = row_ends - lengths
    places = jnp.arange(SEQ, dtype=jnp.int32)
    member = ((places[None, :] >= row_starts[:, None]) & (places[None, :] < row_ends[:, None])).astype(f32)
    pooled = jnp.dot(member, final_rows, precision=highest) / lengths[:, None].astype(f32)
    return pooled * lax.rsqrt(jnp.sum(pooled * pooled, axis=-1, keepdims=True) + unit_eps)


def attend(query_rows, key_rows, value_rows, segment):
    scores = jnp.einsum(
        "qhd,khd->hqk", query_rows, key_rows, preferred_element_type=f32
    ) * HEAD ** (-0.5)
    same = segment[:, None] == segment[None, :]
    scores = jnp.where(same[None], scores, masked_value)
    row_top = jnp.max(scores, axis=-1, keepdims=True)
    raw = jnp.exp(scores - row_top)
    row_total = jnp.sum(raw, axis=-1, keepdims=True)
    probs = raw / row_total
    mixture = jnp.einsum(
        "hqk,khd->qhd", probs.astype(bf16), value_rows, preferred_element_type=f32
    )
    return (mixture, row_top + jnp.log(row_total))


def attend_back(query_rows, key_rows, value_rows, segment, log_total, grad_mixture):
    scores = jnp.einsum(
        "qhd,khd->hqk", query_rows, key_rows, preferred_element_type=f32
    ) * HEAD ** (-0.5)
    same = segment[:, None] == segment[None, :]
    scores = jnp.where(same[None], scores, masked_value)
    probs = jnp.exp(scores - log_total)
    grad_value = jnp.einsum(
        "hqk,qhd->khd", probs.astype(bf16), grad_mixture, preferred_element_type=f32
    )
    grad_probs = jnp.einsum("qhd,khd->hqk", grad_mixture, value_rows, preferred_element_type=f32)
    row_dot = jnp.sum(grad_probs * probs, axis=-1, keepdims=True)
    grad_scores = (probs * (grad_probs - row_dot)).astype(bf16)
    grad_query = jnp.einsum(
        "hqk,khd->qhd", grad_scores, key_rows, preferred_element_type=f32
    ) * HEAD ** (-0.5)
    grad_key = jnp.einsum(
        "hqk,qhd->khd", grad_scores, query_rows, preferred_element_type=f32
    ) * HEAD ** (-0.5)
    return (grad_query, grad_key, grad_value)


def layer_forward(rows, segment, weights, vectors):
    attn_in, attn_out, ff_in, ff_out = weights
    gains, biases, ff_bias = vectors
    zero_part = jnp.zeros((D,), f32)
    qkv_bias = jnp.concatenate([biases[0], zero_part, biases[1]])
    qkv = (jnp.dot(rows, attn_in, preferred_element_type=f32) + qkv_bias).astype(bf16)
    parts = qkv.reshape(SEQ, 3, HEADS, HEAD)
    mixture, log_total = attend(parts[:, 0], parts[:, 1], parts[:, 2], segment)
    mixture = mixture.reshape(SEQ, D).astype(bf16)
    attended = jnp.dot(mixture, attn_out, preferred_element_type=f32) + biases[2]
    hidden = rows.astype(f32) + attended
    normed = norm_rows(hidden, gains[0], biases[3])
    pre_act = jnp.dot(normed.astype(bf16), ff_in, preferred_element_type=f32) + ff_bias
    gelu_out = jax.nn.gelu(pre_act, approximate=False).astype(bf16)
    branch = jnp.dot(gelu_out, ff_out, preferred_element_type=f32) + biases[4]
    output = norm_rows(normed + branch, gains[1], biases[5])
    return (output, (parts, log_total, mixture, hidden, normed, pre_act, branch))


def layer_backward(rows, segment, weights, vectors, stored, grad_out):
    attn_in, attn_out, ff_in, ff_out = weights
    gains, biases, ff_bias = vectors
    parts, log_total, mixture, hidden, normed, pre_act, branch = stored
    _, out_pull = jax.vjp(norm_rows, normed + branch, gains[1], biases[5])
    grad_sum, grad_gain_out, grad_shift_out = out_pull(grad_out)
    grad_branch = grad_sum.astype(bf16)
    gelu_value, gelu_pull = jax.vjp(partial(jax.nn.gelu, approximate=False), pre_act)
    grad_ff_out = jnp.einsum(
        "tf,td->fd", gelu_value.astype(bf16), grad_branch, preferred_element_type=f32
    ).astype(bf16)
    grad_bias_out = jnp.sum(grad_branch, axis=0, dtype=f32)
    grad_gelu = jnp.einsum("td,fd->tf", grad_branch, ff_out, preferred_element_type=f32)
    grad_pre = gelu_pull(grad_gelu)[0].astype(bf16)
    grad_ff_in = jnp.einsum(
        "td,tf->df", normed.astype(bf16), grad_pre, preferred_element_type=f32
    ).astype(bf16)
    grad_ff_bias = jnp.sum(grad_pre, axis=0, dtype=f32)
    grad_normed = grad_sum + jnp.einsum("tf,df->td", grad_pre, ff_in, preferred_element_type=f32)
    _, in_pull = jax.vjp(norm_rows, hidden, gains[0], biases[3])
    grad_hidden, grad_gain_in, grad_shift_in = in_pull(grad_normed)
    grad_attended = grad_hidden.astype(bf16)
    grad_attn_out = jnp.einsum(
        "ti,to->io", mixture, grad_attended, preferred_element_type=f32
    ).astype(bf16)
    grad_bias_attn = jnp.sum(grad_attended, axis=0, dtype=f32)
    grad_mixture = jnp.einsum("to,io->ti", grad_attended, attn_out, preferred_element_type=f32)
    grad_mixture = grad_mixture.astype(bf16).reshape(SEQ, HEADS, HEAD)
    grad_query, grad_key, grad_value = attend_back(
        parts[:, 0], parts[:, 1], parts[:, 2], segment, log_total, grad_mixture
    )
    grad_qkv = (
        jnp.stack([grad_query, grad_key, grad_value], axis=1).reshape(SEQ, 3 * D).astype(bf16)
    )
    grad_attn_in = jnp.einsum("ti,tj->ij", rows, grad_qkv, preferred_element_type=f32).astype(bf16)
    grad_bias_qkv = jnp.sum(grad_qkv, axis=0, dtype=f32)
    grad_inputs = grad_hidden + jnp.einsum("tj,ij->ti", grad_qkv, attn_in, preferred_element_type=f32)
    small = jnp.stack(
        [
            grad_gain_in,
            grad_gain_out,
            grad_bias_qkv[:D],
            grad_bias_qkv[2 * D :],
            grad_bias_attn,
            grad_shift_in,
            grad_bias_out,
            grad_shift_out,
        ]
    )
    return grad_inputs, (grad_attn_in, grad_attn_out, grad_ff_in, grad_ff_out), (small, grad_ff_bias)


def contrast(final_rows, lengths, partner_all, group_row):
    unit_own, unit_pull = jax.vjp(lambda value: pool_unit(value, lengths), final_rows)
    table = gather_small(unit_own).reshape(-1, D)
    count = table.shape[0]
    offset = lax.axis_index("dp") * unit_own.shape[0]
    ids = jnp.arange(count, dtype=jnp.int32)
    chosen = (ids[None, :] == partner_all[:, None]).astype(f32)
    logits = contrast_scale * jnp.dot(table, table.T, precision=highest)
    allowed = (group_row[:, None] == group_row[None, :]) & (ids[:, None] != ids[None, :])
    masked = jnp.where(allowed, logits, masked_value)
    row_top = jnp.max(masked, axis=1, keepdims=True)
    raw = jnp.exp(masked - row_top)
    row_total = jnp.sum(raw, axis=1, keepdims=True)
    loss = jnp.sum(row_top[:, 0] + jnp.log(row_total[:, 0]) - jnp.sum(chosen * logits, axis=1))
    grad_logits = raw / row_total - chosen
    both = lax.dynamic_slice_in_dim(grad_logits + grad_logits.T, offset, unit_own.shape[0])
    grad_unit = contrast_scale * jnp.dot(both, table, precision=highest)
    return loss / (MICRO * count), unit_pull(grad_unit)[0]


def blocked(shard):
    rows, columns = shard.shape
    return shard.reshape(rows, columns // D, D).transpose(1, 0, 2).reshape(-1, D)


def unblocked(shard, columns):
    return shard.reshape(columns, -1, D).transpose(1, 0, 2).reshape(-1, columns * D)


def local(
    tokens,
    out_cotangent,
    lengths,
    partner,
    group_ids,
    attn_in,
    attn_out,
    ff_in,
    ff_out,
    norm_gains,
    biases,
    ff_bias,
):
    section = lax.axis_index("section")
    leading = section == 0
    n_dp = lax.axis_size("dp")
    rows_in = D // n_dp
    rows_out = FF // n_dp

    def pick(stack):
        return lax.dynamic_index_in_dim(stack, section, 0, keepdims=False)

    small = jnp.concatenate(
        [norm_gains[0].reshape(-1), biases[0].reshape(-1), ff_bias[0].reshape(-1)]
    )
    small = small.astype(bf16).astype(f32)
    small_other = swapped(small, "section", 1)
    small = jnp.concatenate([small, small_other, partner.astype(f32).reshape(-1)])
    small = gather_small(small)
    width = 8 * rows_in + rows_out
    vectors = []
    for layer in range(2):
        mine = jnp.where(
            section == layer, small[:, :width], small[:, width : 2 * width]
        )
        both = mine[:, : 8 * rows_in].reshape(n_dp, 8, rows_in).transpose(1, 0, 2).reshape(8, D)
        vectors.append((both[:2], both[2:8], mine[:, 8 * rows_in :].reshape(FF)))
    partner_all = small[:, 2 * width :].reshape(n_dp, MICRO, -1)
    partner_mine = lax.dynamic_index_in_dim(partner_all, section, 1, keepdims=False)
    partner_mine = partner_mine.reshape(-1).astype(jnp.int32)

    chunk_blocks = [
        [(rows_in, 3)],
        [(rows_in, 1), (rows_in, 4)],
        [(rows_out, 1)],
    ]
    weights = [[], []]
    if fast_ring():
        packed = [
            blocked(attn_in[0].astype(bf16)),
            jnp.concatenate([attn_out[0].astype(bf16), blocked(ff_in[0].astype(bf16))]),
            ff_out[0].astype(bf16),
        ]
        crossed = [swapped(piece, "section", 1) for piece in packed]
        owner = gather_owners()
        for layer in range(2):
            for mine, other, blocks in zip(packed, crossed, chunk_blocks):
                shard = jnp.where(section == layer, mine, other)
                weights[layer] += assemble(gather_pieces(shard), blocks, owner)
    else:
        for shard in (attn_in, attn_out, ff_in, ff_out):
            whole = lax.all_gather(shard[0].astype(bf16), ("section", "dp"), axis=0, tiled=True)
            half = whole.shape[0] // 2
            weights[0].append(whole[:half])
            weights[1].append(whole[half:])

    my_tokens = pick(tokens)[0]
    my_cotangent = pick(out_cotangent)[0]
    my_lengths = pick(lengths)[0]
    my_groups = pick(group_ids)
    row_ends = jnp.cumsum(my_lengths, dtype=jnp.int32)
    places = jnp.arange(SEQ, dtype=jnp.int32)
    segment = jnp.sum((places[:, None] >= row_ends[None, :]).astype(jnp.int32), axis=-1)

    first_out, first_stored = layer_forward(my_tokens, segment, weights[0], vectors[0])
    middle = first_out.astype(bf16)
    final, second_stored = layer_forward(middle, segment, weights[1], vectors[1])
    final_low = final.astype(bf16)
    loss, grad_final = contrast(final, my_lengths, partner_mine, my_groups)
    contrast_loss = loss + swapped(loss, "section", 1)
    grad_final = grad_final + my_cotangent.astype(f32)

    grad_middle, second_grads, second_small = layer_backward(
        middle, segment, weights[1], vectors[1], second_stored, grad_final
    )
    grad_middle_low = grad_middle.astype(bf16)
    grad_tokens, first_grads, first_small = layer_backward(
        my_tokens, segment, weights[0], vectors[0], first_stored, grad_middle_low.astype(f32)
    )

    if fast_ring():
        keep_table, send_table, core = deal_tables()
        totals = []
        for grads in (second_grads, first_grads):
            grad_in, grad_out, grad_ff_in, grad_ff_out = grads
            chunks = []
            for group, blocks in (
                ([grad_ff_out], chunk_blocks[2]),
                ([grad_out, grad_ff_in], chunk_blocks[1]),
                ([grad_in], chunk_blocks[0]),
            ):
                keep, send = deal(group, blocks, keep_table, send_table)
                chunks.append(reduce_units(keep, send, core))
            totals.append(chunks)
        own = []
        for second, first in zip(*totals):
            send = jnp.where(leading, second, first).astype(bf16)
            keep = jnp.where(leading, first, second)
            own.append(keep + swapped(send, "section", 1).astype(f32))
        own_ff_out = own[0]
        own_attn_out, own_ff_in = own[1][:rows_in], unblocked(own[1][rows_in:], 4)
        own_attn_in = unblocked(own[2], 3)
    else:
        shares = []
        for first, second in zip(first_grads, second_grads):
            both = jnp.concatenate([first, second]).astype(f32)
            shares.append(lax.psum_scatter(both, ("section", "dp"), scatter_dimension=0, tiled=True))
        own_attn_in, own_attn_out, own_ff_in, own_ff_out = shares

    def flat(pair):
        rows, bias = pair
        rows = rows.reshape(8, n_dp, rows_in).transpose(1, 0, 2).reshape(n_dp, -1)
        return jnp.concatenate([rows, bias.reshape(n_dp, -1)], axis=1)

    first_flat, second_flat = flat(first_small), flat(second_small)
    keep = jnp.where(leading, first_flat, second_flat)
    send = jnp.where(leading, second_flat, first_flat)
    own_small = reduce_small(keep + swapped(send, "section", 1))
    own_rows = own_small[: 8 * rows_in].reshape(8, rows_in)
    own_bias = own_small[8 * rows_in :]

    state_other = swapped(jnp.where(leading, final_low, middle), "section", 1)
    state_mine = jnp.where(leading, middle, final_low)
    hidden_states = jnp.stack(
        [jnp.where(leading, state_mine, state_other), jnp.where(leading, state_other, state_mine)]
    )
    grad_other = swapped(
        jnp.where(leading, grad_middle_low, grad_tokens.astype(bf16)), "section", 1
    ).astype(f32)
    grad_mine = jnp.where(leading, grad_tokens, grad_middle)
    hidden_grads = jnp.stack(
        [jnp.where(leading, grad_mine, grad_other), jnp.where(leading, grad_other, grad_mine)]
    )
    return (
        contrast_loss,
        hidden_states[None, :, None],
        hidden_grads[None, :, None],
        own_attn_in[None],
        own_attn_out[None],
        own_ff_in[None],
        own_ff_out[None],
        own_rows[None, :2],
        own_rows[None, 2:],
        own_bias[None],
    )


def solution(mesh):
    return jax.shard_map(
        local,
        mesh=mesh,
        in_specs=(
            P(None, "dp", None, None),
            P(None, "dp", None, None),
            P(None, "dp", None),
            P(None, "dp"),
            P(),
            P("section", "dp", None),
            P("section", "dp", None),
            P("section", "dp", None),
            P("section", "dp", None),
            P("section", None, "dp"),
            P("section", None, "dp"),
            P("section", "dp"),
        ),
        out_specs=(
            P(),
            P("section", None, "dp", None, None),
            P("section", None, "dp", None, None),
            P("section", "dp", None),
            P("section", "dp", None),
            P("section", "dp", None),
            P("section", "dp", None),
            P("section", None, "dp"),
            P("section", None, "dp"),
            P("section", "dp"),
        ),
        check_vma=False,
    )
```

time: 1270 us -> 699 us (0.55)
  waiting for transfers between devices: 511 us -> 200 us
  blocking collectives: 212 us -> 0 us
  matrix products: 359 us -> 191 us
  starting transfers between devices: 11.9 us -> 100 us
  Pallas kernels: 0 us -> 63.4 us
  local copies, waits for them, and re-layouts: 66.2 us -> 49 us
  between operations: 20.6 us -> 6.41 us
    reduce_scatter x4 -> x0, waiting for transfers between devices: 317 us -> none  [the longest x1 116 us: local(): lax.psum_scatter(accum[2], 'dp', scatter_dimension=0, tiled=True)]
    ppermute x4 -> x113, waiting for transfers between devices: 40.9 us -> 200 us  [the longest x48 143 us: ring_hop(): return lax.ppermute(value, 'dp', pairs)]
    dot_general x57 -> x34, matrix products: 319 us -> 163 us  [the longest x2 39.7 us: layer_forward(): jnp.dot(normed.astype(bf16), ff_in, preferred_element_type=f32) + ff_bias]
    unnamed x2 -> x0, blocking collectives: 91.3 us -> none
    ppermute x4 -> x113, starting transfers between devices: 11.3 us -> 100 us  [the longest x48 61.7 us: ring_hop(): return lax.ppermute(value, 'dp', pairs)]
    unnamed x14 -> x0, waiting for transfers between devices: 86.1 us -> none
    all_gather x4 -> x0, blocking collectives: 82.8 us -> none  [the longest x2 37.7 us: contrast_part(): table = lax.all_gather(unit_local, 'dp', axis=0, tiled=True)]
    all_gather x4 -> x0, waiting for transfers between devices: 67 us -> none  [the longest x1 47.5 us: local(): lax.all_gather(ff_out[0].astype(jnp.bfloat16), 'dp', axis=0, tiled=True)]
  transfers between devices with their start and end apart: 15 -> 113, of which waited for: 9 -> 40; matrix products, arithmetic and copies ran while one was open for 13% -> 40% of each run, Pallas kernels for 0% -> 8%
where the time goes in v1:
time: 699 us; the launch traced here: 690 us
  waiting for transfers between devices  200 us (29%)
  matrix products  191 us (27%)
  starting transfers between devices  100 us (14%)
  other arithmetic  80.6 us (12%)
  Pallas kernels  63.4 us (9%)
  local copies, waits for them, and re-layouts  49 us (7%)
    ppermute x48, waiting for transfers between devices, ring_hop(): return lax.ppermute(value, 'dp', pairs)  143 us
    ppermute x48, starting transfers between devices, ring_hop(): return lax.ppermute(value, 'dp', pairs)  61.7 us
    ppermute x65, waiting for transfers between devices, swapped(): return lax.ppermute(value, axis, [(i, i ^ mask) for i in range(count)])  57.2 us
    dot_general x2, matrix products, layer_forward(): jnp.dot(normed.astype(bf16), ff_in, preferred_element_type=f32) + ff_bias  39.7 us
    ppermute x65, starting transfers between devices, swapped(): return lax.ppermute(value, axis, [(i, i ^ mask) for i in range(count)])  38.6 us
    pallas_call x6, Pallas kernels, assemble(): pl.pallas_call(partial(assemble_kernel, blocks, counts), out_shape=[jax.S...  33.8 us
    pallas_call x6, Pallas kernels, deal(): pl.pallas_call(partial(deal_kernel, blocks), out_shape=[jax.ShapeDtypeStr...  29.7 us
    dot_general x2, matrix products, attend_back(): jnp.einsum('qhd,khd->hqk', grad_mixture, value_rows, preferred_element_ty...  19.4 us
  transfers between devices with their start and end apart: 113, of which 40 were waited for; matrix products, arithmetic and copies ran while one was open for 40% of the time, Pallas kernels for 8%

profile of v1, /device:TPU:0, one launch (start us, length us, event | category | flops | bytes accessed | tf_op | source)
XLA Modules:
  0.0 690.3 jit_solution(17016897737240210788)
XLA Ops:
  37.8 17.1 %collective-permute-done.14 = f32[8,1160]{1,0:T(8,128)S(1)} collective-permute-done((f32[8,1160]{1,0:T(8,128)S(1)}, f32[8,1160]{1,0:T(8,128)S(1)}, u32[]{:S(2)}, u32[]{:S(2)}) %collective-permute-start.14) | collective-permute-done | bytes 37152 | tf_op jit(solution)/shard_map/ppermute | solution.py:29
  64.4 16.6 %collective-permute-done.3.refs_2_ = bf16[2,144,768]{2,1,0:T(8,128)(2,1)} collective-permute-done((bf16[2,144,768]{2,1,0:T(8,128)(2,1)}, bf16[2,144,768]{2,1,0:T(8,128)(2,1)}, u32[]{:S(2)}, u32[]{:S(2)}) %collective-permute-start.3) | collective-permute-done | bytes 442400 | tf_op jit(solution)/shard_map/ppermute | solution.py:44
  106.2 15.9 %collective-permute-done.5.refs_4_ = bf16[1,144,768]{2,1,0:T(8,128)(2,1)} collective-permute-done((bf16[1,144,768]{2,1,0:T(8,128)(2,1)S(1)}, bf16[1,144,768]{2,1,0:T(8,128)(2,1)}, u32[]{:S(2)}, u32[]{:S(2)}) %collective-permute-start.5) | collective-permute-done | bytes 221216 | tf_op jit(solution)/shard_map/ppermute | solution.py:44
  135.8 5.1 assemble.6
  147.4 5.4 fusion.24
  186.3 5.2 assemble.8
  191.6 5.2 assemble.11
  198.8 6.6 assemble.7
  208.2 20.1 %multiply_convert_fusion.3 = (bf16[512,3072]{1,0:T(8,128)(2,1)S(1)}, f32[512,3072]{1,0:T(8,128)}, f32[512,3072]{1,0:T(8,128)}) fusion(f32[3072]{0:T(1024)S(1)} %add.530, bf16[768,3072]{1,0:T(8,128)(2,1)} %get-tuple-element.27, f32[512,768]{1,0:T(8,128)S(1)} %get-tuple-element.184, f32[768]{0:T(1024)S(1)} %add.527, f32[768]{0:T(1024)S(1)} %mul.452, ...), kind=kOutput, calls=%fused_computation.44 | convolution fusion | flops 2521694208 | bytes 22042624 | tf_op jit(solution)/shard_map/dot_general | solution.py:287
  252.5 6.7 assemble.10
  262.2 19.6 %multiply_convert_fusion.2 = (bf16[512,3072]{1,0:T(8,128)(2,1)S(1)}, f32[512,3072]{1,0:T(8,128)}, f32[512,3072]{1,0:T(8,128)}) fusion(f32[3072]{0:T(1024)S(1)} %add.551, bf16[768,3072]{1,0:T(8,128)(2,1)} %get-tuple-element.29, f32[512,768]{1,0:T(8,128)S(1)} %get-tuple-element.191, f32[768]{0:T(1024)S(1)} %add.548, f32[768]{0:T(1024)S(1)} %mul.468, ...), kind=kOutput, calls=%fused_computation.31 | convolution fusion | flops 2521694208 | bytes 22042624 | tf_op jit(solution)/shard_map/dot_general | solution.py:287
  313.6 9.1 %convert_reduce_fusion = (f32[3072]{0:T(1024)S(1)}, bf16[512,3072]{1,0:T(8,128)(2,1)S(1)}) fusion(f32[512,3072]{1,0:T(8,128)} %get-tuple-element.116, f32[512,3072]{1,0:T(8,128)} %get-tuple-element.192, f32[3072]{0:T(1024)S(1)} %copy-done.95, bf16[512,768]{1,0:T(8,128)(2,1)S(1)} %get-tuple-element.97, bf16[3072,768]{1,0:T(8,128)(2,1)} %assemble.11), kind=kOutput, calls=%fused_computation.25 | convolution fusion | flops 2442654720 | bytes 21258240 | tf_op jit(solution)/shard_map/td,fd->tf/dot_general | solution.py:306
  339.7 7.3 %fusion.34 = bf16[512,1,12,64]{0,3,2,1:T(8,128)(2,1)} fusion(bf16[512,12,64]{0,2,1:T(8,128)(2,1)S(1)} %bitcast.310, f32[12,512]{1,0:T(8,128)S(1)} %log_add_fusion.1, f32[12,512,512]{1,2,0:T(8,128)} %copy-done.4, pred[512,512]{0,1:T(8,128)(4,1)S(1)} %broadcast_compare_fusion), kind=kOutput, calls=%fused_computation.129 | convolution fusion | flops 415236096 | bytes 14442496 | tf_op jit(solution)/shard_map/hqk,qhd->khd/dot_general | solution.py:260
  347.1 9.7 %multiply_reduce_fusion.1 = (f32[12,512]{1,0:T(8,128)S(1)}, f32[12,512,512]{1,2,0:T(8,128)}) fusion(f32[12,512]{1,0:T(8,128)S(1)} %log_add_fusion.1, f32[12,512,512]{1,2,0:T(8,128)} %copy-done.4, pred[512,512]{0,1:T(8,128)(4,1)S(1)} %broadcast_compare_fusion, bf16[512,12,64]{0,2,1:T(8,128)(2,1)S(1)} %bitcast.311, bf16[512,3,12,64]{0,3,2,1:T(8,128)(2,1)} %bitcast.301), kind=kOutput, calls=%fused_computation.7 | convolution fusion | flops 418375680 | bytes 27049984 | tf_op jit(solution)/shard_map/qhd,khd->hqk/dot_general | solution.py:263
  356.8 7.1 %multiply_convert_fusion.1 = bf16[12,512,512]{1,2,0:T(8,128)(2,1)S(1)} fusion(f32[12,512,512]{1,2,0:T(8,128)} %get-tuple-element.202, f32[12,512]{1,0:T(8,128)S(1)} %get-tuple-element.201, f32[12,512]{1,0:T(8,128)S(1)} %log_add_fusion.1, f32[12,512,512]{1,2,0:T(8,128)S(1)} %bitcast.293, pred[512,512]{0,1:T(8,128)(4,1)S(1)} %broadcast_compare_fusion), kind=kLoop, calls=%fused_computation.6 | loop fusion | flops 18874368 | bytes 31768576 | tf_op jit(solution)/shard_map/convert_element_type | solution.py:265
  375.3 8.4 %convert_reduce_fusion.1 = (f32[3072]{0:T(1024)}, bf16[512,3072]{1,0:T(8,128)(2,1)S(1)}) fusion(f32[512,3072]{1,0:T(8,128)} %get-tuple-element.118, f32[512,3072]{1,0:T(8,128)} %get-tuple-element.185, f32[3072]{0:T(1024)S(1)} %copy-done.93, bf16[512,768]{1,0:T(8,128)(2,1)S(1)} %get-tuple-element.89, bf16[3072,768]{1,0:T(8,128)(2,1)S(1)} %bitcast.307), kind=kOutput, calls=%fused_computation.26 | convolution fusion | flops 2442654720 | bytes 21258240 | tf_op jit(solution)/shard_map/td,fd->tf/dot_general | solution.py:306
  400.8 7.3 %fusion.37 = bf16[512,1,12,64]{0,3,2,1:T(8,128)(2,1)} fusion(bf16[512,12,64]{0,2,1:T(8,128)(2,1)S(1)} %bitcast.312, f32[12,512]{1,0:T(8,128)S(1)} %log_add_fusion, f32[12,512,512]{1,2,0:T(8,128)} %copy-done.3, pred[512,512]{0,1:T(8,128)(4,1)S(1)} %broadcast_compare_fusion), kind=kOutput, calls=%fused_computation.130 | convolution fusion | flops 415236096 | bytes 14442496 | tf_op jit(solution)/shard_map/hqk,qhd->khd/dot_general | solution.py:260
  408.2 9.7 %multiply_reduce_fusion = (f32[12,512]{1,0:T(8,128)S(1)}, f32[12,512,512]{1,2,0:T(8,128)}) fusion(f32[12,512]{1,0:T(8,128)S(1)} %log_add_fusion, f32[12,512,512]{1,2,0:T(8,128)} %copy-done.3, pred[512,512]{0,1:T(8,128)(4,1)S(1)} %broadcast_compare_fusion, bf16[512,12,64]{0,2,1:T(8,128)(2,1)S(1)} %bitcast.313, bf16[512,3,12,64]{0,3,2,1:T(8,128)(2,1)} %bitcast.296), kind=kOutput, calls=%fused_computation.4 | convolution fusion | flops 418375680 | bytes 27049984 | tf_op jit(solution)/shard_map/qhd,khd->hqk/dot_general | solution.py:263
  417.9 7.3 %multiply_convert_fusion = bf16[12,512,512]{1,2,0:T(8,128)(2,1)S(1)} fusion(f32[12,512,512]{1,2,0:T(8,128)} %get-tuple-element.206, f32[12,512]{1,0:T(8,128)S(1)} %get-tuple-element.205, f32[12,512]{1,0:T(8,128)S(1)} %log_add_fusion, f32[12,512,512]{1,2,0:T(8,128)S(1)} %bitcast.291, pred[512,512]{0,1:T(8,128)(4,1)S(1)} %broadcast_compare_fusion), kind=kLoop, calls=%fused_computation.3 | loop fusion | flops 18874368 | bytes 31768576 | tf_op jit(solution)/shard_map/convert_element_type | solution.py:265
  434.3 5.0 convert_select_fusion.2
  439.9 6.0 convolution_convert_fusion.4.refs_0_
  481.9 6.0 deal.9
  487.9 6.0 deal.8
  500.5 14.4 %collective-permute-done.68 = bf16[512,768]{1,0:T(8,128)(2,1)S(1)} collective-permute-done((bf16[512,768]{1,0:T(8,128)(2,1)}, bf16[512,768]{1,0:T(8,128)(2,1)S(1)}, u32[]{:S(2)}, u32[]{:S(2)}) %collective-permute-start.68) | collective-permute-done | bytes 786464 | tf_op jit(solution)/shard_map/ppermute | solution.py:29
  561.0 15.3 %collective-permute-done.89 = bf16[1,240,768]{2,1,0:T(8,128)(2,1)} collective-permute-done((bf16[1,240,768]{2,1,0:T(8,128)(2,1)}, bf16[1,240,768]{2,1,0:T(8,128)(2,1)}, u32[]{:S(2)}, u32[]{:S(2)}) %collective-permute-start.89) | collective-permute-done | bytes 368672 | tf_op jit(solution)/shard_map/ppermute | solution.py:44
  587.3 5.5 collective-permute-done.90
  594.4 11.0 %collective-permute-done.84 = bf16[2,240,768]{2,1,0:T(8,128)(2,1)S(1)} collective-permute-done((bf16[2,240,768]{2,1,0:T(8,128)(2,1)S(1)}, bf16[2,240,768]{2,1,0:T(8,128)(2,1)S(1)}, u32[]{:S(2)}, u32[]{:S(2)}) %collective-permute-start.84) | collective-permute-done | bytes 737312 | tf_op jit(solution)/shard_map/ppermute | solution.py:44
  619.6 6.3 collective-permute-done.91
  627.6 6.3 collective-permute-done.85
  640.2 6.3 collective-permute-done.99
  646.6 7.9 %collective-permute-done.92 = bf16[2,240,768]{2,1,0:T(8,128)(2,1)S(1)} collective-permute-done((bf16[2,240,768]{2,1,0:T(8,128)(2,1)S(1)}, bf16[2,240,768]{2,1,0:T(8,128)(2,1)S(1)}, u32[]{:S(2)}, u32[]{:S(2)}) %collective-permute-start.92) | collective-permute-done | bytes 737312 | tf_op jit(solution)/shard_map/ppermute | solution.py:44
  654.5 7.9 %collective-permute-done.86 = bf16[2,240,768]{2,1,0:T(8,128)(2,1)S(1)} collective-permute-done((bf16[2,240,768]{2,1,0:T(8,128)(2,1)S(1)}, bf16[2,240,768]{2,1,0:T(8,128)(2,1)S(1)}, u32[]{:S(2)}, u32[]{:S(2)}) %collective-permute-start.86) | collective-permute-done | bytes 737312 | tf_op jit(solution)/shard_map/ppermute | solution.py:44
  (851 shorter events, 390.4 us)
Async XLA Ops:
  31.0 26.5 %collective-permute-start.36 = (bf16[2,144,768]{2,1,0:T(8,128)(2,1)S(1)}, bf16[2,144,768]{2,1,0:T(8,128)(2,1)}, u32[]{:S(2)}, u32[]{:S(2)}) collective-permute-start(bf16[2,144,768]{2,1,0:T(8,128)(2,1)S(1)} %pad_maximum_fusion.5.refs_0_), channel_id=1, source_target_pairs={{0,4},{1,3},{4,8},{5,1},{8,12},{9,5},{12,14},{13,9},{14,10},{15,13... | collective-permute-start | bytes 1327112 | tf_op jit(solution)/shard_map/ppermute | solution.py:44
  32.7 26.9 %collective-permute-start.27 = (bf16[2,192,768]{2,1,0:T(8,128)(2,1)S(1)}, bf16[2,192,768]{2,1,0:T(8,128)(2,1)}, u32[]{:S(2)}, u32[]{:S(2)}) collective-permute-start(bf16[2,192,768]{2,1,0:T(8,128)(2,1)S(1)} %pad_maximum_fusion.2.refs_0_), channel_id=1, source_target_pairs={{0,4},{1,3},{4,8},{5,1},{8,12},{9,5},{12,14},{13,9},{14,10},{15,13... | collective-permute-start | bytes 1769480 | tf_op jit(solution)/shard_map/ppermute | solution.py:44
  34.4 27.5 %collective-permute-start.54 = (bf16[2,192,768]{2,1,0:T(8,128)(2,1)S(1)}, bf16[2,192,768]{2,1,0:T(8,128)(2,1)}, u32[]{:S(2)}, u32[]{:S(2)}) collective-permute-start(bf16[2,192,768]{2,1,0:T(8,128)(2,1)S(1)} %pad_maximum_fusion.3.refs_0_), channel_id=1, source_target_pairs={{0,4},{1,3},{4,8},{5,1},{8,12},{9,5},{12,14},{13,9},{14,10},{15,13... | collective-permute-start | bytes 1769480 | tf_op jit(solution)/shard_map/ppermute | solution.py:44
  37.7 25.6 %collective-permute-start.6 = (bf16[2,144,768]{2,1,0:T(8,128)(2,1)}, bf16[2,144,768]{2,1,0:T(8,128)(2,1)S(1)}, u32[]{:S(2)}, u32[]{:S(2)}) collective-permute-start(bf16[2,144,768]{2,1,0:T(8,128)(2,1)} %collective-permute-done.2.refs_1_), channel_id=1, source_target_pairs={{0,1},{1,0},{2,3},{3,2},{4,5},{5,4},{6,7},{7,6},{8,9},{9,8},{10,11... | collective-permute-start | bytes 1327112 | tf_op jit(solution)/shard_map/ppermute | solution.py:29
  55.0 32.0 %collective-permute-start.45 = (bf16[2,240,768]{2,1,0:T(8,128)(2,1)S(1)}, bf16[2,240,768]{2,1,0:T(8,128)(2,1)}, u32[]{:S(2)}, u32[]{:S(2)}) collective-permute-start(bf16[2,240,768]{2,1,0:T(8,128)(2,1)S(1)} %pad_maximum_fusion.1.refs_0_), channel_id=1, source_target_pairs={{0,4},{1,3},{4,8},{5,1},{8,12},{9,5},{12,14},{13,9},{14,10},{15,13... | collective-permute-start | bytes 2211848 | tf_op jit(solution)/shard_map/ppermute | solution.py:44
  57.4 29.5 %collective-permute-start.17 = (bf16[2,240,768]{2,1,0:T(8,128)(2,1)S(1)}, bf16[2,240,768]{2,1,0:T(8,128)(2,1)}, u32[]{:S(2)}, u32[]{:S(2)}) collective-permute-start(bf16[2,240,768]{2,1,0:T(8,128)(2,1)S(1)} %pad_maximum_fusion.refs_0_), channel_id=1, source_target_pairs={{0,4},{1,3},{4,8},{5,1},{8,12},{9,5},{12,14},{13,9},{14,10},{15,13... | collective-permute-start | bytes 2211848 | tf_op jit(solution)/shard_map/ppermute | solution.py:44
  94.4 27.8 %collective-permute-start.58 = (bf16[2,192,768]{2,1,0:T(8,128)(2,1)}, bf16[2,192,768]{2,1,0:T(8,128)(2,1)}, u32[]{:S(2)}, u32[]{:S(2)}) collective-permute-start(bf16[2,192,768]{2,1,0:T(8,128)(2,1)} %collective-permute-done.54.refs_1_), channel_id=1, source_target_pairs={{0,1},{1,0},{2,3},{3,2},{4,5},{5,4},{6,7},{7,6},{8,9},{9,8},{10,11... | collective-permute-start | bytes 1769480 | tf_op jit(solution)/shard_map/ppermute | solution.py:29
  96.6 26.6 %collective-permute-start.55 = (bf16[2,192,768]{2,1,0:T(8,128)(2,1)}, bf16[2,192,768]{2,1,0:T(8,128)(2,1)}, u32[]{:S(2)}, u32[]{:S(2)}) collective-permute-start(bf16[2,192,768]{2,1,0:T(8,128)(2,1)} %collective-permute-done.54.refs_1_), channel_id=1, source_target_pairs={{0,4},{1,3},{4,8},{5,1},{8,12},{9,5},{12,14},{13,9},{14,10},{15,13... | collective-permute-start | bytes 1769480 | tf_op jit(solution)/shard_map/ppermute | solution.py:44
  99.1 28.9 %collective-permute-start.18 = (bf16[2,240,768]{2,1,0:T(8,128)(2,1)}, bf16[2,240,768]{2,1,0:T(8,128)(2,1)}, u32[]{:S(2)}, u32[]{:S(2)}) collective-permute-start(bf16[2,240,768]{2,1,0:T(8,128)(2,1)} %collective-permute-done.17.refs_1_), channel_id=1, source_target_pairs={{0,4},{1,3},{4,8},{5,1},{8,12},{9,5},{12,14},{13,9},{14,10},{15,13... | collective-permute-start | bytes 2211848 | tf_op jit(solution)/shard_map/ppermute | solution.py:44
  128.0 30.4 %collective-permute-start.19 = (bf16[2,240,768]{2,1,0:T(8,128)(2,1)}, bf16[2,240,768]{2,1,0:T(8,128)(2,1)}, u32[]{:S(2)}, u32[]{:S(2)}) collective-permute-start(bf16[2,240,768]{2,1,0:T(8,128)(2,1)} %collective-permute-done.18.refs_2_), channel_id=1, source_target_pairs={{0,4},{1,3},{4,8},{5,1},{8,12},{9,5},{12,14},{13,9},{14,10},{15,13... | collective-permute-start | bytes 2211848 | tf_op jit(solution)/shard_map/ppermute | solution.py:44
  141.0 24.8 %collective-permute-start.32 = (bf16[2,192,768]{2,1,0:T(8,128)(2,1)}, bf16[2,192,768]{2,1,0:T(8,128)(2,1)}, u32[]{:S(2)}, u32[]{:S(2)}) collective-permute-start(bf16[2,192,768]{2,1,0:T(8,128)(2,1)} %collective-permute-done.28.refs_2_), channel_id=1, source_target_pairs={{0,1},{1,0},{2,3},{3,2},{4,5},{5,4},{6,7},{7,6},{8,9},{9,8},{10,11... | collective-permute-start | bytes 1769480 | tf_op jit(solution)/shard_map/ppermute | solution.py:29
  141.5 24.3 %collective-permute-start.59 = (bf16[2,192,768]{2,1,0:T(8,128)(2,1)}, bf16[2,192,768]{2,1,0:T(8,128)(2,1)}, u32[]{:S(2)}, u32[]{:S(2)}) collective-permute-start(bf16[2,192,768]{2,1,0:T(8,128)(2,1)} %collective-permute-done.55.refs_2_), channel_id=1, source_target_pairs={{0,1},{1,0},{2,3},{3,2},{4,5},{5,4},{6,7},{7,6},{8,9},{9,8},{10,11... | collective-permute-start | bytes 1769480 | tf_op jit(solution)/shard_map/ppermute | solution.py:29
  196.8 55.6 %collective-permute-start.49 = (bf16[2,240,768]{2,1,0:T(8,128)(2,1)}, bf16[2,240,768]{2,1,0:T(8,128)(2,1)}, u32[]{:S(2)}, u32[]{:S(2)}) collective-permute-start(bf16[2,240,768]{2,1,0:T(8,128)(2,1)} %collective-permute-done.45.refs_1_), channel_id=1, source_target_pairs={{0,1},{1,0},{2,3},{3,2},{4,5},{5,4},{6,7},{7,6},{8,9},{9,8},{10,11... | collective-permute-start | bytes 2211848 | tf_op jit(solution)/shard_map/ppermute | solution.py:29
  197.3 55.1 %collective-permute-start.50 = (bf16[2,240,768]{2,1,0:T(8,128)(2,1)}, bf16[2,240,768]{2,1,0:T(8,128)(2,1)}, u32[]{:S(2)}, u32[]{:S(2)}) collective-permute-start(bf16[2,240,768]{2,1,0:T(8,128)(2,1)} %collective-permute-done.46.refs_2_), channel_id=1, source_target_pairs={{0,1},{1,0},{2,3},{3,2},{4,5},{5,4},{6,7},{7,6},{8,9},{9,8},{10,11... | collective-permute-start | bytes 2211848 | tf_op jit(solution)/shard_map/ppermute | solution.py:29
  197.4 55.1 %collective-permute-start.51 = (bf16[2,240,768]{2,1,0:T(8,128)(2,1)}, bf16[2,240,768]{2,1,0:T(8,128)(2,1)}, u32[]{:S(2)}, u32[]{:S(2)}) collective-permute-start(bf16[2,240,768]{2,1,0:T(8,128)(2,1)} %collective-permute-done.47.refs_3_), channel_id=1, source_target_pairs={{0,1},{1,0},{2,3},{3,2},{4,5},{5,4},{6,7},{7,6},{8,9},{9,8},{10,11... | collective-permute-start | bytes 2211848 | tf_op jit(solution)/shard_map/ppermute | solution.py:29
  197.9 54.6 %collective-permute-start.52 = (bf16[1,240,768]{2,1,0:T(8,128)(2,1)}, bf16[1,240,768]{2,1,0:T(8,128)(2,1)}, u32[]{:S(2)}, u32[]{:S(2)}) collective-permute-start(bf16[1,240,768]{2,1,0:T(8,128)(2,1)} %collective-permute-done.48.refs_4_), channel_id=1, source_target_pairs={{0,1},{1,0},{2,3},{3,2},{4,5},{5,4},{6,7},{7,6},{8,9},{9,8},{10,11... | collective-permute-start | bytes 1105928 | tf_op jit(solution)/shard_map/ppermute | solution.py:29
  297.5 199.4 %collective-permute-start.67 = (bf16[512,768]{1,0:T(8,128)(2,1)}, bf16[512,768]{1,0:T(8,128)(2,1)}, u32[]{:S(2)}, u32[]{:S(2)}) collective-permute-start(bf16[512,768]{1,0:T(8,128)(2,1)} %get-tuple-element.111), channel_id=1, source_target_pairs={{0,16},{16,0},{1,17},{17,1},{2,18},{18,2},{3,19},{19,3},{4,20},{20... | collective-permute-start | bytes 2359304 | tf_op jit(solution)/shard_map/ppermute | solution.py:29
  463.3 52.0 %collective-permute-start.75 = (bf16[8,144,768]{2,1,0:T(8,128)(2,1)}, bf16[8,144,768]{2,1,0:T(8,128)(2,1)}, u32[]{:S(2)}, u32[]{:S(2)}) collective-permute-start(bf16[8,144,768]{2,1,0:T(8,128)(2,1)} %get-tuple-element.33), channel_id=1, source_target_pairs={{0,1},{1,0},{2,3},{3,2},{4,5},{5,4},{6,7},{7,6},{8,9},{9,8},{10,11... | collective-permute-start | bytes 5308424 | tf_op jit(solution)/shard_map/ppermute | solution.py:29
  467.5 51.0 %collective-permute-start.69 = (bf16[8,144,768]{2,1,0:T(8,128)(2,1)}, bf16[8,144,768]{2,1,0:T(8,128)(2,1)}, u32[]{:S(2)}, u32[]{:S(2)}) collective-permute-start(bf16[8,144,768]{2,1,0:T(8,128)(2,1)} %get-tuple-element.31), channel_id=1, source_target_pairs={{0,1},{1,0},{2,3},{3,2},{4,5},{5,4},{6,7},{7,6},{8,9},{9,8},{10,11... | collective-permute-start | bytes 5308424 | tf_op jit(solution)/shard_map/ppermute | solution.py:29
  468.1 26.5 %collective-permute-start.112 = (f32[1,576]{1,0:T(1,128)S(1)}, f32[1,576]{1,0:T(1,128)S(1)}, u32[]{:S(2)}, u32[]{:S(2)}) collective-permute-start(f32[1,576]{1,0:T(1,128)S(1)} %broadcast_select_fusion.29), channel_id=1, source_target_pairs={{0,1},{1,0},{2,3},{3,2},{4,5},{5,4},{6,7},{7,6},{8,9},{9,8},{10,11... | collective-permute-start | bytes 6920 | tf_op jit(solution)/shard_map/ppermute | solution.py:29
  469.5 24.5 %collective-permute-start.66 = (f32[]{:T(128)}, f32[]{:T(128)}, u32[]{:S(2)}, u32[]{:S(2)}) collective-permute-start(f32[]{:T(128)} %div.177), channel_id=1, source_target_pairs={{0,16},{16,0},{1,17},{17,1},{2,18},{18,2},{3,19},{19,3},{4,20},{20... | collective-permute-start | bytes 20 | tf_op jit(solution)/shard_map/ppermute | solution.py:29
  494.0 38.3 %collective-permute-start.101 = (bf16[8,192,768]{2,1,0:T(8,128)(2,1)}, bf16[8,192,768]{2,1,0:T(8,128)(2,1)}, u32[]{:S(2)}, u32[]{:S(2)}) collective-permute-start(bf16[8,192,768]{2,1,0:T(8,128)(2,1)} %get-tuple-element.41), channel_id=1, source_target_pairs={{0,1},{1,0},{2,3},{3,2},{4,5},{5,4},{6,7},{7,6},{8,9},{9,8},{10,11... | collective-permute-start | bytes 7077896 | tf_op jit(solution)/shard_map/ppermute | solution.py:29
  496.9 55.1 %collective-permute-start.88 = (bf16[8,240,768]{2,1,0:T(8,128)(2,1)}, bf16[8,240,768]{2,1,0:T(8,128)(2,1)S(1)}, u32[]{:S(2)}, u32[]{:S(2)}) collective-permute-start(bf16[8,240,768]{2,1,0:T(8,128)(2,1)} %get-tuple-element.37), channel_id=1, source_target_pairs={{0,1},{1,0},{2,3},{3,2},{4,5},{5,4},{6,7},{7,6},{8,9},{9,8},{10,11... | collective-permute-start | bytes 8847368 | tf_op jit(solution)/shard_map/ppermute | solution.py:29
  515.2 39.5 %collective-permute-start.82 = (bf16[8,240,768]{2,1,0:T(8,128)(2,1)}, bf16[8,240,768]{2,1,0:T(8,128)(2,1)}, u32[]{:S(2)}, u32[]{:S(2)}) collective-permute-start(bf16[8,240,768]{2,1,0:T(8,128)(2,1)} %get-tuple-element.35), channel_id=1, source_target_pairs={{0,1},{1,0},{2,3},{3,2},{4,5},{5,4},{6,7},{7,6},{8,9},{9,8},{10,11... | collective-permute-start | bytes 8847368 | tf_op jit(solution)/shard_map/ppermute | solution.py:29
  547.0 35.2 %collective-permute-start.72 = (bf16[2,144,768]{2,1,0:T(8,128)(2,1)S(1)}, bf16[2,144,768]{2,1,0:T(8,128)(2,1)}, u32[]{:S(2)}, u32[]{:S(2)}) collective-permute-start(bf16[2,144,768]{2,1,0:T(8,128)(2,1)S(1)} %fusion.64), channel_id=1, source_target_pairs={{0,4},{1,3},{4,8},{5,1},{8,12},{9,5},{12,14},{13,9},{14,10},{15,13... | collective-permute-start | bytes 1327112 | tf_op jit(solution)/shard_map/ppermute | solution.py:44
  550.5 34.1 %collective-permute-start.103 = (bf16[2,192,768]{2,1,0:T(8,128)(2,1)S(1)}, bf16[2,192,768]{2,1,0:T(8,128)(2,1)}, u32[]{:S(2)}, u32[]{:S(2)}) collective-permute-start(bf16[2,192,768]{2,1,0:T(8,128)(2,1)S(1)} %get-tuple-element.171), channel_id=1, source_target_pairs={{0,4},{1,3},{4,8},{5,1},{8,12},{9,5},{12,14},{13,9},{14,10},{15,13... | collective-permute-start | bytes 1769480 | tf_op jit(solution)/shard_map/ppermute | solution.py:44
  552.0 34.0 %collective-permute-start.97 = (bf16[2,192,768]{2,1,0:T(8,128)(2,1)S(1)}, bf16[2,192,768]{2,1,0:T(8,128)(2,1)S(1)}, u32[]{:S(2)}, u32[]{:S(2)}) collective-permute-start(bf16[2,192,768]{2,1,0:T(8,128)(2,1)S(1)} %get-tuple-element.172), channel_id=1, source_target_pairs={{0,4},{1,3},{4,8},{5,1},{8,12},{9,5},{12,14},{13,9},{14,10},{15,13... | collective-permute-start | bytes 1769480 | tf_op jit(solution)/shard_map/ppermute | solution.py:44
  576.3 59.2 %collective-permute-start.79 = (bf16[2,144,768]{2,1,0:T(8,128)(2,1)S(1)}, bf16[2,144,768]{2,1,0:T(8,128)(2,1)S(1)}, u32[]{:S(2)}, u32[]{:S(2)}) collective-permute-start(bf16[2,144,768]{2,1,0:T(8,128)(2,1)S(1)} %fusion.62), channel_id=1, source_target_pairs={{0,4},{1,3},{4,8},{5,1},{8,12},{9,5},{12,14},{13,9},{14,10},{15,13... | collective-permute-start | bytes 1327112 | tf_op jit(solution)/shard_map/ppermute | solution.py:44
  583.3 55.7 %collective-permute-start.73 = (bf16[2,144,768]{2,1,0:T(8,128)(2,1)S(1)}, bf16[2,144,768]{2,1,0:T(8,128)(2,1)S(1)}, u32[]{:S(2)}, u32[]{:S(2)}) collective-permute-start(bf16[2,144,768]{2,1,0:T(8,128)(2,1)S(1)} %fusion.65), channel_id=1, source_target_pairs={{0,4},{1,3},{4,8},{5,1},{8,12},{9,5},{12,14},{13,9},{14,10},{15,13... | collective-permute-start | bytes 1327112 | tf_op jit(solution)/shard_map/ppermute | solution.py:44
  586.0 25.8 %collective-permute-start.104 = (bf16[2,192,768]{2,1,0:T(8,128)(2,1)S(1)}, bf16[2,192,768]{2,1,0:T(8,128)(2,1)S(1)}, u32[]{:S(2)}, u32[]{:S(2)}) collective-permute-start(bf16[2,192,768]{2,1,0:T(8,128)(2,1)S(1)} %fusion.53), channel_id=1, source_target_pairs={{0,4},{1,3},{4,8},{5,1},{8,12},{9,5},{12,14},{13,9},{14,10},{15,13... | collective-permute-start | bytes 1769480 | tf_op jit(solution)/shard_map/ppermute | solution.py:44
  592.8 25.3 %collective-permute-start.98 = (bf16[2,192,768]{2,1,0:T(8,128)(2,1)S(1)}, bf16[2,192,768]{2,1,0:T(8,128)(2,1)S(1)}, u32[]{:S(2)}, u32[]{:S(2)}) collective-permute-start(bf16[2,192,768]{2,1,0:T(8,128)(2,1)S(1)} %fusion.56), channel_id=1, source_target_pairs={{0,4},{1,3},{4,8},{5,1},{8,12},{9,5},{12,14},{13,9},{14,10},{15,13... | collective-permute-start | bytes 1769480 | tf_op jit(solution)/shard_map/ppermute | solution.py:44
  635.5 26.8 %collective-permute-start.86 = (bf16[2,240,768]{2,1,0:T(8,128)(2,1)S(1)}, bf16[2,240,768]{2,1,0:T(8,128)(2,1)S(1)}, u32[]{:S(2)}, u32[]{:S(2)}) collective-permute-start(bf16[2,240,768]{2,1,0:T(8,128)(2,1)S(1)} %fusion.45), channel_id=1, source_target_pairs={{0,4},{1,3},{4,8},{5,1},{8,12},{9,5},{12,14},{13,9},{14,10},{15,13... | collective-permute-start | bytes 2211848 | tf_op jit(solution)/shard_map/ppermute | solution.py:44
  (243 other events, 4381.7 us)

commit v2 on v1

v2 whole, which is shorter than its diff:
```python
from functools import partial

import jax
import jax.numpy as jnp
from jax import lax
from jax.experimental import pallas as pl
from jax.experimental.pallas import tpu as pltpu
from jax.sharding import PartitionSpec as P

D = 768
HEADS = 12
HEAD = 64
SEQ = 512
MICRO = 2
FF = 3072

bf16 = jnp.bfloat16
f32 = jnp.float32
highest = lax.Precision.HIGHEST
norm_eps = 1e-05
unit_eps = 1e-06
masked_value = -1000000000.0
contrast_scale = 10.0
vmem_limit = 20 * 2**20


def params():
    return pltpu.CompilerParams(vmem_limit_bytes=vmem_limit)


def cost(flops, size):
    return pl.CostEstimate(flops=int(10 * flops), bytes_accessed=int(10 * size), transcendentals=0)


def swapped(value, axis, mask):
    count = lax.axis_size(axis)
    return lax.ppermute(value, axis, [(i, i ^ mask) for i in range(count)])


def ring_order(chips):
    return list(range(0, chips, 2)) + list(range(chips - 1, 0, -2))


def ring_hop(value, backward=False):
    chips = lax.axis_size("dp") // 2
    order = ring_order(chips)
    pairs = []
    for place in range(chips):
        for core in range(2):
            step = 1 if core == 0 else -1
            pairs.append((order[place] * 2 + core, order[(place + step) % chips] * 2 + core))
    return lax.ppermute(value, "dp", pairs)


def ring_place():
    me = lax.axis_index("dp").astype(jnp.int32)
    chips = lax.axis_size("dp") // 2
    order = ring_order(chips)
    places = [order.index(chip) for chip in range(chips)]
    place = jnp.asarray(places, jnp.int32)[me // 2]
    core = me % 2
    return place, 1 - 2 * core, core


def owners(steps, cores):
    chips = lax.axis_size("dp") // 2
    place, way, core = ring_place()
    order = jnp.asarray(ring_order(chips), jnp.int32)
    found = order[(place + way * jnp.asarray(steps, jnp.int32)) % chips] * 2
    return found + (core + jnp.asarray(cores, jnp.int32)) % 2


def fast_ring():
    return lax.axis_size("dp") == 16


def gather_owners():
    steps = [0, 0, -1, -1, -2, -2, -3, -3, -4, 1, 1, 2, 2, 3, 3, 4]
    cores = [0, 1, 0, 1, 0, 1, 0, 1, 0, 1, 0, 1, 0, 1, 0, 1]
    return owners(steps, cores)


def assemble_kernel(counts, owner_ref, *refs):
    pieces, out_ref, sems = refs[: len(counts)], refs[-2], refs[-1]
    rows = pieces[0].shape[2]
    copies = []
    for piece, count in zip(pieces, counts):
        for k in range(count):
            start = pl.multiple_of(owner_ref[len(copies)] * rows, 16)
            copies.append(
                pltpu.make_async_copy(
                    piece.at[k], out_ref.at[:, pl.ds(start, rows), :], sems.at[len(copies)]
                )
            )
    for copy in copies:
        copy.start()
    for copy in copies:
        copy.wait()


def assemble(pieces, owner):
    counts = [piece.shape[0] for piece in pieces]
    total = sum(counts)
    blocks, rows = pieces[0].shape[1:3]
    return pl.pallas_call(
        partial(assemble_kernel, counts),
        out_shape=jax.ShapeDtypeStruct((blocks, total * rows, D), bf16),
        in_specs=[pl.BlockSpec(memory_space=pltpu.SMEM)]
        + [pl.BlockSpec(memory_space=pl.ANY)] * len(pieces),
        out_specs=pl.BlockSpec(memory_space=pltpu.VMEM),
        scratch_shapes=[pltpu.SemaphoreType.DMA((total,))],
        compiler_params=params(),
        cost_estimate=cost(0, 1e7),
        name="assemble",
    )(owner, *pieces)


unit_steps = [1, 1, 2, 2, 3, 3, 4, 0]


def slots():
    if not fast_ring():
        return jnp.arange(16, dtype=jnp.int32)
    core = ring_place()[2]
    both = jnp.arange(6, dtype=jnp.int32) % 2
    keep = owners(unit_steps, [0] * 8)
    send = owners([-step for step in unit_steps], [1] * 8)
    table = [keep[:6] // 2 * 2 + both, keep[6:], send[:6] // 2 * 2 + both, send[6:]]
    table = jnp.concatenate(table)
    index = jnp.arange(16, dtype=jnp.int32)
    return jnp.sum(jnp.where(table[None, :] == index[:, None], index[None, :], 0), axis=1)


def fold_kernel(one, core_ref, keep_ref, mate_ref, *refs):
    total = keep_ref[...].astype(f32) + mate_ref[...].astype(f32)
    if len(refs) > 1:
        there = refs[0][...].astype(f32)
        if one:
            there = jnp.where(pl.program_id(0) == core_ref[0], there, 0.0)
        total = total + there
    refs[-1][...] = total.astype(bf16)


def fold(core, keep, mate, first, there=None):
    rows, width = keep.shape[1:]
    count = 1 if there is None else 2
    one = there is not None and there.shape[0] == 1
    unit = pl.BlockSpec((1, rows, width), lambda i, _: (first + i, 0, 0))
    out = pl.BlockSpec((1, rows, width), lambda i, _: (i, 0, 0))
    arrived = pl.BlockSpec((1, rows, width), lambda i, _: (0, 0, 0)) if one else out
    return pl.pallas_call(
        partial(fold_kernel, one),
        grid_spec=pltpu.PrefetchScalarGridSpec(
            num_scalar_prefetch=1,
            grid=(count,),
            in_specs=[unit, unit] + ([] if there is None else [arrived]),
            out_specs=out,
        ),
        out_shape=jax.ShapeDtypeStruct((count, rows, width), bf16),
        compiler_params=params(),
        cost_estimate=cost(0, 0),
        name="fold",
    )(core, keep, mate, *([] if there is None else [there]))


def settle_kernel(place_ref, *refs):
    totals = []
    for layer in range(2):
        parts = refs[4 * layer : 4 * layer + 4]
        totals.append(sum(part[0].astype(f32) for part in parts))
    leading = place_ref[1] == 0
    keep_ref, send_ref = refs[8:]
    keep_ref[...] = jnp.where(leading, totals[0], totals[1])
    send_ref[...] = jnp.where(leading, totals[1], totals[0]).astype(bf16)


def settle(place, first, second):
    rows, width = first.keep.shape[1:]
    tile = rows // 3
    own = pl.BlockSpec((1, tile, width), lambda i, _: (7, i, 0))
    end = pl.BlockSpec((1, tile, width), lambda i, place: (place[0], i, 0))
    out = pl.BlockSpec((tile, width), lambda i, _: (i, 0))
    return pl.pallas_call(
        settle_kernel,
        grid_spec=pltpu.PrefetchScalarGridSpec(
            num_scalar_prefetch=1,
            grid=(3,),
            in_specs=[own, own, end, end] * 2,
            out_specs=[out, out],
        ),
        out_shape=[
            jax.ShapeDtypeStruct((rows, width), f32),
            jax.ShapeDtypeStruct((rows, width), bf16),
        ],
        compiler_params=params(),
        cost_estimate=cost(0, 0),
        name="settle",
    )(place, *first.parts(), *second.parts())


class Reduction:
    def __init__(self, core, keep, send):
        self.core, self.keep, self.send = core, keep, send
        self.moving = [swapped(send, "dp", 1)] if fast_ring() else []
        self.stage = 0

    def step(self):
        arrived = self.moving[0]
        if self.stage == 0:
            self.mate = arrived
            self.moving = [ring_hop(fold(self.core, self.keep, self.mate, 6))]
        elif self.stage < 4:
            first = 6 - 2 * self.stage
            self.moving = [ring_hop(fold(self.core, self.keep, self.mate, first, arrived))]
        elif self.stage == 4:
            self.near = arrived
            self.moving = [swapped(self.near, "dp", 1)]
        else:
            self.last = arrived
            self.moving = []
        self.stage += 1

    def parts(self):
        return self.keep, self.mate, self.near, self.last


class Settled:
    def __init__(self, place, first, second):
        self.keep, send = settle(place, first, second)
        self.moving = [swapped(send, "section", 1)]

    def step(self):
        self.value = self.keep + self.moving[0].astype(f32)
        self.moving = []


class Sent:
    def __init__(self, value, pairs):
        half = value.shape[0] // 2
        self.halves, self.pairs, self.arrived = [value[:half], value[half:]], pairs, []
        self.send()

    def send(self):
        half = self.halves[len(self.arrived)]
        self.moving = [lax.ppermute(half, "section", self.pairs)]

    def step(self):
        self.arrived += self.moving
        self.moving = []
        if len(self.arrived) < 2:
            self.send()

    def value(self):
        return jnp.concatenate(self.arrived)


class Sum:
    def __init__(self, value):
        self.value = value
        self.left = [("section", 1)]
        mask = 1
        while mask < lax.axis_size("dp"):
            self.left.append(("dp", mask))
            mask *= 2
        self.send()

    def send(self):
        self.moving = [swapped(self.value, *self.left[0])] if self.left else []

    def step(self):
        self.value = self.value + self.moving[0]
        self.left = self.left[1:]
        self.send()


class Gather:
    def __init__(self, shard):
        self.pieces, self.mates = [shard], []
        self.moving = [swapped(shard, "dp", 1)]
        self.stage = 0

    def step(self):
        if self.stage == 0:
            self.pieces = [jnp.stack([self.pieces[0], self.moving[0]])]
            self.moving = [ring_hop(self.pieces[0])]
        elif self.stage < 5:
            self.pieces.append(self.moving[0])
            self.mates += self.moving[1:]
            self.moving = [swapped(self.pieces[-1], "dp", 1)]
            if self.stage < 4:
                last = self.pieces[-1] if self.stage < 3 else self.pieces[-1][:1]
                self.moving = [ring_hop(last)] + self.moving
        else:
            self.mates += self.moving
            self.moving = []
        self.stage += 1

    def all(self):
        return self.pieces + self.mates


def onward(items, values=()):
    items = [item for item in items if item.moving]
    if items:
        values, moved = lax.optimization_barrier((values, [item.moving for item in items]))
        for item, moving in zip(items, moved):
            item.moving = moving
            item.step()
    return values


def tie(values, *others):
    return lax.optimization_barrier((values, others))[0]


def add_up(value, axis):
    mask = 1
    while mask < lax.axis_size(axis):
        value = value + swapped(value, axis, mask)
        mask *= 2
    return value


def gather_near(value):
    mask = lax.axis_size("dp") // 2
    while mask >= 1:
        value = jnp.concatenate([value, swapped(value, "dp", mask)])
        mask //= 2
    return value


def mm(a, b):
    return lax.dot_general(a, b, (((1,), (0,)), ((), ())), preferred_element_type=f32)


def mm_nt(a, b):
    return lax.dot_general(a, b, (((1,), (1,)), ((), ())), preferred_element_type=f32)


def mm_tn(a, b):
    return lax.dot_general(a, b, (((0,), (0,)), ((), ())), preferred_element_type=f32)


def full(shape):
    return pl.BlockSpec(shape, lambda i, *_: (0,) * len(shape))


def sds(shape, dtype):
    return jax.ShapeDtypeStruct(shape, dtype)


group = 256
groups = D // group
product = 2 * SEQ * D * D
token_block = (SEQ, D)
table_rows = 12
vec_spec = full((2 * table_rows, D))


def column_sum(value):
    return jnp.sum(value, axis=0, keepdims=True)


def attend_kernel(base, x_ref, wq_ref, wk_ref, wv_ref, vec_ref, seg_col_ref, seg_row_ref, *refs):
    q_ref, k_ref, v_ref, mixed_ref, lse_ref, mask_ref = refs
    i = pl.program_id(0)

    @pl.when(i == 0)
    def _():
        mask_ref[...] = jnp.where(seg_col_ref[...] == seg_row_ref[...], 0.0, masked_value)

    lanes = pl.ds(pl.multiple_of(i * group, group), group)
    x = x_ref[...]
    q = (mm(x, wq_ref[...]) + vec_ref[base + 2 : base + 3, lanes]).astype(bf16)
    k = mm(x, wk_ref[...]).astype(bf16)
    v = (mm(x, wv_ref[...]) + vec_ref[base + 3 : base + 4, lanes]).astype(bf16)
    q_ref[...] = q
    k_ref[...] = k
    v_ref[...] = v
    scaled = q * jnp.asarray(HEAD**-0.5, bf16)
    outs, lses = [], []
    for h in range(group // HEAD):
        c = slice(h * HEAD, (h + 1) * HEAD)
        scores = mm_nt(scaled[:, c], k[:, c]) + mask_ref[...]
        top = jnp.max(scores, axis=1, keepdims=True)
        raw = jnp.exp(scores - top)
        total = jnp.sum(raw, axis=1, keepdims=True)
        outs.append(mm(raw.astype(bf16), v[:, c]) / total)
        lses.append(top + jnp.log(total))
    mixed_ref[...] = jnp.concatenate(outs, axis=1).astype(bf16)
    lse_ref[...] = jnp.concatenate(lses + [jnp.zeros((SEQ, 128 - len(lses)), f32)], axis=1)


def attend(x, w_in, vec, base, seg_col, seg_row):
    def weight(b):
        return pl.BlockSpec((None, D, group), lambda i: (b, 0, i))

    out = pl.BlockSpec((SEQ, group), lambda i: (0, i))
    return pl.pallas_call(
        partial(attend_kernel, base),
        grid=(groups,),
        in_specs=[full(token_block)]
        + [weight(b) for b in range(3)]
        + [vec_spec, full((SEQ, 1)), full((1, SEQ))],
        out_specs=[out] * 4 + [pl.BlockSpec((None, SEQ, 128), lambda i: (i, 0, 0))],
        out_shape=[sds(token_block, bf16)] * 4 + [sds((groups, SEQ, 128), f32)],
        scratch_shapes=[pltpu.VMEM((SEQ, SEQ), f32)],
        compiler_params=params(),
        cost_estimate=cost(5 * product, 3e7),
        name="attend",
    )(x, w_in, w_in, w_in, vec, seg_col, seg_row)


def normalize(hidden):
    centered = hidden - jnp.mean(hidden, axis=1, keepdims=True)
    variance = jnp.mean(centered * centered, axis=1, keepdims=True)
    rstd = lax.rsqrt(variance + norm_eps)
    return centered * rstd, rstd


def gelu_both(x):
    base = 1.0 + 0.3275911 * 0.7071067811865476 * jnp.abs(x)
    t = pl.reciprocal(base, approx=True)
    t = t * (2.0 - base * t)
    bell = jnp.exp(x * x * -0.5)
    series = 1.421413741 + t * (-1.453152027 + t * 1.061405429)
    series = t * (0.254829592 + t * (-0.284496736 + t * series))
    tail = 0.5 * series * bell
    cdf = jnp.where(x >= 0, 1.0 - tail, tail)
    return x * cdf, cdf + x * bell * 0.3989422804014327


def widen_kernel(base, mixed_ref, x_ref, wo_ref, wi_ref, vec_ref, *refs):
    xhat_ref, rstd_ref, gelu_ref, dgelu_ref, normed_ref = refs
    i = pl.program_id(0)

    @pl.when(i == 0)
    def _():
        attended = mm(mixed_ref[...], wo_ref[...]) + vec_ref[base + 4 : base + 5, :]
        xhat, rstd = normalize(x_ref[...].astype(f32) + attended)
        xhat_ref[...] = xhat
        rstd_ref[...] = rstd
        normed = xhat * vec_ref[base : base + 1, :] + vec_ref[base + 5 : base + 6, :]
        normed_ref[...] = normed.astype(bf16)

    pre_act = mm(normed_ref[...], wi_ref[...]) + vec_ref[pl.ds(base + 8 + i, 1), :]
    value, slope = gelu_both(pre_act)
    gelu_ref[...] = value.astype(bf16)
    dgelu_ref[...] = slope.astype(bf16)


def widen(mixed, x, w_wide, vec, base):
    out = pl.BlockSpec(token_block, lambda i: (0, i))
    return pl.pallas_call(
        partial(widen_kernel, base),
        grid=(FF // D,),
        in_specs=[
            full(token_block),
            full(token_block),
            pl.BlockSpec((None, D, D), lambda i: (0, 0, 0)),
            pl.BlockSpec((None, D, D), lambda i: (1 + i, 0, 0)),
            vec_spec,
        ],
        out_specs=[full(token_block), full((SEQ, 1)), out, out],
        out_shape=[sds(token_block, f32), sds((SEQ, 1), f32)] + [sds((SEQ, FF), bf16)] * 2,
        scratch_shapes=[pltpu.VMEM(token_block, bf16)],
        compiler_params=params(),
        cost_estimate=cost(5 * product, 3e7),
        name="widen",
    )(mixed, x, w_wide, w_wide, vec)


def narrow_kernel(base, last, gelu_ref, wf_ref, xhat1_ref, vec_ref, *refs):
    if last:
        seg_row_ref, out_ref, xhat_ref, rstd_ref, pooled_ref, unit_ref, acc_ref = refs
    else:
        out_ref, xhat_ref, rstd_ref, acc_ref = refs
    i = pl.program_id(0)

    @pl.when(i == 0)
    def _():
        acc_ref[...] = mm(gelu_ref[...], wf_ref[...])

    @pl.when(i > 0)
    def _():
        acc_ref[...] += mm(gelu_ref[...], wf_ref[...])

    @pl.when(i == pl.num_programs(0) - 1)
    def _():
        normed = xhat1_ref[...] * vec_ref[base : base + 1, :] + vec_ref[base + 5 : base + 6, :]
        xhat, rstd = normalize(normed + (acc_ref[...] + vec_ref[base + 6 : base + 7, :]))
        xhat_ref[...] = xhat
        rstd_ref[...] = rstd
        out = xhat * vec_ref[base + 1 : base + 2, :] + vec_ref[base + 7 : base + 8, :]
        out_ref[...] = out.astype(bf16)
        if last:
            member = seg_row_ref[...] == lax.broadcasted_iota(jnp.int32, (8, SEQ), 0)
            count = jnp.sum(member.astype(f32), axis=1, keepdims=True)
            member = member.astype(bf16)
            high = out.astype(bf16)
            rest = out - high.astype(f32)
            middle = rest.astype(bf16)
            low = (rest - middle.astype(f32)).astype(bf16)
            pooled = mm(member, high) + mm(member, middle) + mm(member, low)
            pooled = pooled / jnp.maximum(count, 1.0)
            pooled_ref[...] = pooled
            norm = jnp.sum(pooled * pooled, axis=1, keepdims=True) + unit_eps
            unit_ref[...] = pooled * lax.rsqrt(norm)


def narrow(gelu, w_narrow, xhat1, vec, base, seg_row=None):
    last = seg_row is not None
    outs = [sds(token_block, bf16), sds(token_block, f32), sds((SEQ, 1), f32)]
    if last:
        outs += [sds((8, D), f32)] * 2
    return pl.pallas_call(
        partial(narrow_kernel, base, last),
        grid=(FF // D,),
        in_specs=[
            pl.BlockSpec(token_block, lambda i: (0, i)),
            pl.BlockSpec((None, D, D), lambda i: (0, i, 0)),
            full(token_block),
            vec_spec,
        ]
        + ([full((1, SEQ))] if last else []),
        out_specs=[full(out.shape) for out in outs],
        out_shape=outs,
        scratch_shapes=[pltpu.VMEM(token_block, f32)],
        compiler_params=params(),
        cost_estimate=cost(4 * product, 2e7),
        name="narrow",
    )(gelu, w_narrow, xhat1, vec, *([seg_row] if last else []))


def contrast_kernel(where_ref, table_ref, pooled_ref, groups_ref, partner_ref, seg_row_ref, *refs, total):
    loss_ref, gseg_ref = refs
    me, micro = where_ref[0], where_ref[1]
    dot = partial(lax.dot_general, precision=highest, preferred_element_type=f32)
    rows_nt = (((1,), (1,)), ((), ()))
    table = table_ref[...]
    count = table.shape[0]
    devices = count // 8
    segs = groups_ref.shape[1] // devices

    def sentence(shape, axis):
        index = lax.broadcasted_iota(jnp.int32, shape, axis)
        block, place = index >> 3, index & 7
        owner = jnp.zeros_like(block)
        far = devices // 2
        bit = 0
        while far >= 1:
            owner = owner | ((block >> bit) & 1) * far
            bit += 1
            far //= 2
        return jnp.where(place < segs, (owner ^ me) * segs + place, -1)

    ids_row, ids_col = sentence((1, count), 1), sentence((count, 1), 0)
    every = groups_ref.shape[1]
    groups = jnp.where(micro == 0, groups_ref[0:1, :], groups_ref[1:2, :]).astype(f32)
    groups = jnp.broadcast_to(groups, (8, every))
    hot_row = (lax.broadcasted_iota(jnp.int32, (every, 1), 0) == ids_row).astype(f32)
    hot_col = (lax.broadcasted_iota(jnp.int32, (1, every), 1) == ids_col).astype(f32)
    groups_row = dot(groups, hot_row, (((1,), (0,)), ((), ())))[0:1]
    groups_col = dot(hot_col, groups, rows_nt)[:, 0:1]
    logits = contrast_scale * dot(table, table, rows_nt)
    real = (ids_row >= 0) & (ids_col >= 0)
    allowed = real & (groups_col == groups_row) & (ids_col != ids_row)
    masked = jnp.where(allowed, logits, masked_value)
    top = jnp.max(masked, axis=0, keepdims=True)
    lse_row = top + jnp.log(column_sum(jnp.exp(masked - top)))
    mine = masked[:8]
    top = jnp.max(mine, axis=1, keepdims=True)
    raw = jnp.exp(mine - top)
    raw_total = jnp.sum(raw, axis=1, keepdims=True)
    across = jnp.exp(mine - lse_row)
    place = lax.broadcasted_iota(jnp.int32, (8, 1), 0)
    partner = jnp.zeros((8, 1), jnp.int32)
    for s in range(segs):
        partner = jnp.where(place == s, jnp.where(micro == 0, partner_ref[0, s], partner_ref[1, s]), partner)
    chosen = ((partner == ids_row) & (place < segs)).astype(f32)
    terms = top + jnp.log(raw_total) - jnp.sum(chosen * logits[:8], axis=1, keepdims=True)
    loss_ref[...] = column_sum(jnp.where(place < segs, terms, 0.0)) / total
    grad = raw / raw_total + across - 2.0 * chosen
    grad = contrast_scale * dot(grad, table, (((1,), (0,)), ((), ())))
    pooled = pooled_ref[...]
    scale = lax.rsqrt(jnp.sum(pooled * pooled, axis=1, keepdims=True) + unit_eps)
    dots = jnp.sum(grad * pooled, axis=1, keepdims=True)
    grad = scale * grad - pooled * (scale * scale * scale * dots)
    member = (seg_row_ref[...] == lax.broadcasted_iota(jnp.int32, (8, SEQ), 0)).astype(f32)
    gseg_ref[...] = grad / jnp.maximum(jnp.sum(member, axis=1, keepdims=True), 1.0)


def contrast(where, table, pooled, group_ids, partner, seg_row, total):
    vmem = pl.BlockSpec(memory_space=pltpu.VMEM)
    smem = pl.BlockSpec(memory_space=pltpu.SMEM)
    return pl.pallas_call(
        partial(contrast_kernel, total=total),
        out_shape=[sds((1, 1), f32), sds((8, D), f32)],
        in_specs=[smem, vmem, vmem, vmem, smem, vmem],
        out_specs=[vmem] * 2,
        compiler_params=params(),
        name="contrast",
    )(where, table, pooled, group_ids, partner, seg_row)


def norm_back(grad, xhat, rstd, gain):
    scaled = grad * gain
    mean = jnp.mean(scaled, axis=1, keepdims=True)
    along = jnp.mean(scaled * xhat, axis=1, keepdims=True)
    return rstd * (scaled - mean - xhat * along)


def put(slot, keep_ref, send_ref, index, value):
    @pl.when(slot < 8)
    def _():
        keep_ref[(slot,) + index] = value

    @pl.when(slot >= 8)
    def _():
        send_ref[(slot - 8,) + index] = value


def back_out_kernel(base, last, slot_ref, *refs):
    if last:
        cot_ref, seg_col_ref, gseg_ref, *refs = refs
    else:
        cot_ref, *refs = refs
    xhat_ref, rstd_ref, vec_ref, gelu_ref, gsum_ref, gbranch_ref, small_ref, keep_ref, send_ref = refs
    i = pl.program_id(0)

    @pl.when(i == 0)
    def _():
        grad = cot_ref[...].astype(f32)
        if last:
            for s in range(4):
                grad = grad + jnp.where(seg_col_ref[...] == s, gseg_ref[s : s + 1, :], 0.0)
        xhat = xhat_ref[...]
        grad_sum = norm_back(grad, xhat, rstd_ref[...], vec_ref[base + 1 : base + 2, :])
        gsum_ref[...] = grad_sum
        low = grad_sum.astype(bf16)
        gbranch_ref[...] = low
        small_ref[...] = jnp.zeros((16, D), f32)
        small_ref[1:2, :] = column_sum(grad * xhat)
        small_ref[6:7, :] = column_sum(low.astype(f32))
        small_ref[7:8, :] = column_sum(grad)

    rows = FF // 16
    grad_weight = mm_tn(gelu_ref[...], gbranch_ref[...]).astype(bf16)
    for j in range(4):
        put(slot_ref[4 * i + j], keep_ref, send_ref, (), grad_weight[j * rows : (j + 1) * rows])


def back_out(slot, cot, xhat2, rstd2, vec, base, gelu, seg_col=None, gseg=None):
    last = gseg is not None
    ins = [cot] + ([seg_col, gseg] if last else []) + [xhat2, rstd2, vec, gelu]
    outs = [sds(token_block, f32), sds(token_block, bf16), sds((16, D), f32)]
    outs += [sds((8, FF // 16, D), bf16)] * 2
    return pl.pallas_call(
        partial(back_out_kernel, base, last),
        grid_spec=pltpu.PrefetchScalarGridSpec(
            num_scalar_prefetch=1,
            grid=(FF // D,),
            in_specs=[full(a.shape) for a in ins[:-1]]
            + [pl.BlockSpec(token_block, lambda i, *_: (0, i))],
            out_specs=[full(out.shape) for out in outs],
        ),
        out_shape=outs,
        compiler_params=params(),
        cost_estimate=cost(4 * product, 2e7),
        name="back_out",
    )(slot, *ins)


def back_pre_kernel(base, slot_ref, *refs):
    gbranch_ref, wf_ref, dgelu_ref, xhat_ref, vec_ref, small_in_ref, *refs = refs
    gpre_ref, small_ref, keep_ref, send_ref, normed_ref = refs
    i = pl.program_id(0)
    rows = D // 16

    @pl.when(i == 0)
    def _():
        normed = xhat_ref[...] * vec_ref[base : base + 1, :] + vec_ref[base + 5 : base + 6, :]
        normed_ref[...] = normed.astype(bf16)
        small_ref[...] = small_in_ref[...]

    grad_gelu = mm_nt(gbranch_ref[...], wf_ref[...])
    grad_pre = (grad_gelu * dgelu_ref[...].astype(f32)).astype(bf16)
    gpre_ref[...] = grad_pre
    small_ref[pl.ds(8 + i, 1), :] = column_sum(grad_pre.astype(f32))
    grad_weight = mm_tn(normed_ref[...], grad_pre).astype(bf16)
    row = pl.multiple_of(rows * i, 16)
    for d in range(16):
        value = grad_weight[d * rows : (d + 1) * rows]
        put(slot_ref[d], keep_ref, send_ref, (pl.ds(row, rows),), value)


def back_pre(slot, gbranch, w_narrow, dgelu, xhat1, vec, base, small):
    outs = [sds((SEQ, FF), bf16), sds((16, D), f32)] + [sds((8, 4 * D // 16, D), bf16)] * 2
    return pl.pallas_call(
        partial(back_pre_kernel, base),
        grid_spec=pltpu.PrefetchScalarGridSpec(
            num_scalar_prefetch=1,
            grid=(FF // D,),
            in_specs=[
                full(token_block),
                pl.BlockSpec((None, D, D), lambda i, *_: (0, i, 0)),
                pl.BlockSpec(token_block, lambda i, *_: (0, i)),
                full(token_block),
                vec_spec,
                full((16, D)),
            ],
            out_specs=[pl.BlockSpec(token_block, lambda i, *_: (0, i))]
            + [full(out.shape) for out in outs[1:]],
            scratch_shapes=[pltpu.VMEM(token_block, bf16)],
        ),
        out_shape=outs,
        compiler_params=params(),
        cost_estimate=cost(8 * product, 3e7),
        name="back_pre",
    )(slot, gbranch, w_narrow, dgelu, xhat1, vec, small)


def back_mid_kernel(base, slot_ref, *refs):
    gsum_ref, gpre_ref, wi_ref, xhat_ref, rstd_ref, mixed_ref, wo_ref, vec_ref, *refs = refs
    small_in_ref, ghid_ref, gmixed_ref, small_ref, keep_ref, send_ref, acc_ref = refs
    i = pl.program_id(0)
    rows = D // 16

    @pl.when(i == 0)
    def _():
        acc_ref[...] = gsum_ref[...]
        small_ref[...] = small_in_ref[...]

    acc_ref[...] += mm_nt(gpre_ref[...], wi_ref[...])

    @pl.when(i == pl.num_programs(0) - 1)
    def _():
        grad = acc_ref[...]
        xhat = xhat_ref[...]
        grad_hidden = norm_back(grad, xhat, rstd_ref[...], vec_ref[base : base + 1, :])
        ghid_ref[...] = grad_hidden
        low = grad_hidden.astype(bf16)
        gmixed_ref[...] = mm_nt(low, wo_ref[...]).astype(bf16)
        small_ref[0:1, :] = column_sum(grad * xhat)
        small_ref[4:5, :] = column_sum(low.astype(f32))
        small_ref[5:6, :] = column_sum(grad)
        grad_out = mm_tn(mixed_ref[...], low).astype(bf16)
        for d in range(16):
            put(slot_ref[d], keep_ref, send_ref, (), grad_out[d * rows : (d + 1) * rows])


def back_mid(slot, gsum, gpre, w_wide, xhat1, rstd1, mixed, vec, base, small):
    outs = [sds(token_block, f32), sds(token_block, bf16), sds((16, D), f32)]
    outs += [sds((8, 4 * D // 16, D), bf16)] * 2
    return pl.pallas_call(
        partial(back_mid_kernel, base),
        grid_spec=pltpu.PrefetchScalarGridSpec(
            num_scalar_prefetch=1,
            grid=(FF // D,),
            in_specs=[
                full(token_block),
                pl.BlockSpec(token_block, lambda i, *_: (0, i)),
                pl.BlockSpec((None, D, D), lambda i, *_: (1 + i, 0, 0)),
                full(token_block),
                full((SEQ, 1)),
                full(token_block),
                pl.BlockSpec((None, D, D), lambda i, *_: (0, 0, 0)),
                vec_spec,
                full((16, D)),
            ],
            out_specs=[full(out.shape) for out in outs[:3]]
            + [pl.BlockSpec((8, D // 16, D), lambda i, *_: (0, 3, 0))] * 2,
            scratch_shapes=[pltpu.VMEM(token_block, f32)],
        ),
        out_shape=outs,
        compiler_params=params(),
        cost_estimate=cost(6 * product, 3e7),
        name="back_mid",
    )(slot, gsum, gpre, w_wide, xhat1, rstd1, mixed, w_wide, vec, small)


def attend_back_kernel(first, n_chunk, slot_ref, *refs):
    x_ref, q_ref, k_ref, v_ref, gm_ref, lse_ref, wq_ref, wk_ref, wv_ref, *refs = refs
    ghid_ref, seg_col_ref, seg_row_ref, small_in_ref, *refs = refs
    gx_ref, low_ref, small_ref, keep_ref, send_ref, mask_ref = refs[n_chunk:]
    i = pl.program_id(0)
    rows = D // 16

    @pl.when(i == 0)
    def _():
        mask_ref[...] = jnp.where(seg_col_ref[...] == seg_row_ref[...], 0.0, masked_value)
        gx_ref[...] = ghid_ref[...]
        small_ref[...] = small_in_ref[...]

    q, k, v, gm = q_ref[...], k_ref[...], v_ref[...], gm_ref[...]
    scaled = q * jnp.asarray(HEAD**-0.5, bf16)
    lse = jnp.transpose(lse_ref[...])
    parts = [[], [], []]
    for h in range(group // HEAD):
        c = slice(h * HEAD, (h + 1) * HEAD)
        probs = jnp.exp(mm_nt(k[:, c], scaled[:, c]) + mask_ref[...] - lse[h : h + 1, :])
        grad_probs = mm_nt(v[:, c], gm[:, c])
        parts[2].append(mm(probs.astype(bf16), gm[:, c]))
        dots = column_sum(grad_probs * probs)
        grad_scores = (probs * (grad_probs - dots)).astype(bf16)
        parts[1].append(mm(grad_scores, scaled[:, c]))
        parts[0].append(mm_tn(grad_scores, k[:, c]) * HEAD**-0.5)
    grads = [jnp.concatenate(part, axis=1).astype(bf16) for part in parts]
    x = x_ref[...]
    for b, grad in enumerate(grads):
        grad_weight = mm_tn(x, grad).astype(bf16)
        for d in range(16):
            index = (slice(b * rows, (b + 1) * rows),)
            put(slot_ref[d], keep_ref, send_ref, index, grad_weight[d * rows : (d + 1) * rows])
    lanes = pl.ds(pl.multiple_of((first + i) * group, group), group)
    small_ref[2:3, lanes] = column_sum(grads[0].astype(f32))
    small_ref[3:4, lanes] = column_sum(grads[2].astype(f32))
    gx_ref[...] += (
        mm_nt(grads[0], wq_ref[...]) + mm_nt(grads[1], wk_ref[...]) + mm_nt(grads[2], wv_ref[...])
    )

    @pl.when(i == pl.num_programs(0) - 1)
    def _():
        low_ref[...] = gx_ref[...].astype(bf16)


def attend_back(slot, x, q, k, v, gm, lse, w_in, ghid, seg_col, seg_row, small, first, count, chunk):
    def weight(b):
        return pl.BlockSpec((None, D, group), lambda i, *_: (b, 0, first + i))

    heads = pl.BlockSpec((SEQ, group), lambda i, *_: (0, first + i))
    units = pl.BlockSpec((8, 3 * D // 16, group), lambda i, *_: (0, 0, first + i))
    outs = [sds(token_block, f32), sds(token_block, bf16), sds((16, D), f32)]
    outs += [sds((8, 4 * D // 16, D), bf16)] * 2
    ins = [x, q, k, v, gm, lse, w_in, w_in, w_in, ghid, seg_col, seg_row, small]
    return pl.pallas_call(
        partial(attend_back_kernel, first, len(chunk)),
        grid_spec=pltpu.PrefetchScalarGridSpec(
            num_scalar_prefetch=1,
            grid=(count,),
            in_specs=[full(token_block)]
            + [heads] * 4
            + [pl.BlockSpec((None, SEQ, 128), lambda i, *_: (first + i, 0, 0))]
            + [weight(b) for b in range(3)]
            + [full(token_block), full((SEQ, 1)), full((1, SEQ)), full((16, D))]
            + [pl.BlockSpec(memory_space=pl.ANY)] * len(chunk),
            out_specs=[full(out.shape) for out in outs[:3]] + [units] * 2,
            scratch_shapes=[pltpu.VMEM((SEQ, SEQ), f32)],
        ),
        out_shape=outs,
        input_output_aliases={len(ins) + 1 + n: 3 + n for n in range(len(chunk))},
        compiler_params=params(),
        cost_estimate=cost(6 * count * product, 3e7),
        name="attend_back",
    )(slot, *ins, *chunk)


def blocked(shard):
    rows, columns = shard.shape
    return shard.reshape(rows, columns // D, D).transpose(1, 0, 2)


def unblocked(shard):
    blocks, rows, columns = shard.shape
    return shard.transpose(1, 0, 2).reshape(rows, blocks * columns)


class Cross:
    def __init__(self, shard):
        self.shard = shard
        self.moving = [swapped(shard, "section", 1)]

    def step(self):
        self.other = self.moving[0]
        self.moving = []

    def layer(self, layer):
        return jnp.where(lax.axis_index("section") == layer, self.shard, self.other)


def gather_plain(attn_in, attn_out, ff_in, ff_out):
    weights = [[], []]
    for shard in (attn_in, attn_out, ff_in, ff_out):
        both = lax.all_gather(shard.astype(bf16), ("section", "dp"), axis=0, tiled=True)
        half = both.shape[0] // 2
        for layer in range(2):
            weights[layer].append(blocked(both[layer * half : (layer + 1) * half]))
    return [[w[0], jnp.concatenate([w[1], w[2]]), w[3]] for w in weights]


def local(
    tokens,
    out_cotangent,
    lengths,
    partner,
    group_ids,
    attn_in,
    attn_out,
    ff_in,
    ff_out,
    norm_gains,
    biases,
    ff_bias,
):
    section = lax.axis_index("section").astype(jnp.int32)
    me = lax.axis_index("dp").astype(jnp.int32)
    leading = section == 0
    n_dp = lax.axis_size("dp")
    rows_in = D // n_dp
    rows_out = FF // n_dp
    segs = lengths.shape[-1]

    def pick(stack):
        return lax.dynamic_index_in_dim(stack, section, 0, keepdims=False)

    vectors = jnp.concatenate(
        [norm_gains[0].reshape(-1), biases[0].reshape(-1), ff_bias[0].reshape(-1)]
    ).astype(bf16)

    def vector_table(every):
        rows = every[:, :, : 8 * rows_in].reshape(n_dp, 2, 8, rows_in)
        rows = rows.transpose(1, 2, 0, 3).reshape(2, 8, D)
        bias = every[:, :, 8 * rows_in :].transpose(1, 0, 2).reshape(2, 4, D)
        return jnp.concatenate([rows, bias], axis=1).reshape(2 * table_rows, D).astype(f32)

    my_tokens = pick(tokens)[0]
    my_cotangent = pick(out_cotangent)[0]
    row_ends = jnp.cumsum(pick(lengths)[0], dtype=jnp.int32)
    places = jnp.arange(SEQ, dtype=jnp.int32)
    segment = jnp.sum((places[:, None] >= row_ends[None, :]).astype(jnp.int32), axis=-1)
    seg_col, seg_row = segment[:, None], segment[None, :]
    slot = slots()

    running = []
    if fast_ring():
        owner = gather_owners()
        cross_in = Cross(blocked(attn_in[0].astype(bf16)))
        cross_vec = Cross(vectors)
        onward([cross_in, cross_vec])
        table = jnp.stack([cross_vec.layer(0), cross_vec.layer(1)])
        table = jnp.pad(table, ((0, 14), (0, D - table.shape[1])))
        gather_vec = Gather(table[None])
        in0 = Gather(cross_in.layer(0))
        late = tie((attn_out, ff_in, ff_out), cross_in.other)
        wide_shard = [late[0][0].astype(bf16)[None], blocked(late[1][0].astype(bf16))]
        cross_wide = Cross(jnp.concatenate(wide_shard))
        onward([in0, gather_vec])
        onward([in0, gather_vec, cross_wide])
        wide_gather0 = Gather(cross_wide.layer(0))
        cross_narrow = Cross(tie(late[2], cross_wide.other)[0].astype(bf16)[None])
        onward([in0, gather_vec, wide_gather0])
        onward([in0, gather_vec, wide_gather0, cross_narrow])
        narrow_gather0 = Gather(cross_narrow.layer(0))
        onward([in0, gather_vec, wide_gather0, narrow_gather0])
        in1 = Gather(tie(cross_in.layer(1), narrow_gather0.pieces[0]))
        onward([in0, gather_vec, wide_gather0, narrow_gather0, in1])
        vec = assemble(gather_vec.all(), owner).reshape(n_dp, 16, D)
        vec = vector_table(vec[:, :2, : vectors.shape[0]])
        w_in0 = assemble(in0.all(), owner)
        q0, k0, v0, mixed0, lse0 = attend(my_tokens, w_in0, vec, 0, seg_col, seg_row)
        mixed0 = onward([wide_gather0, narrow_gather0, in1], mixed0)
        wide_gather1 = Gather(tie(cross_wide.layer(1), mixed0))
        onward([wide_gather0, narrow_gather0, in1, wide_gather1])
        w_wide0 = assemble(wide_gather0.all(), owner)
        wide0 = widen(mixed0, my_tokens, w_wide0, vec, 0)
        gelu0 = onward([narrow_gather0, in1, wide_gather1], wide0[2])
        narrow_gather1 = Gather(tie(cross_narrow.layer(1), gelu0))
        onward([narrow_gather0, in1, wide_gather1, narrow_gather1])
        w_narrow0 = assemble(narrow_gather0.all(), owner)
        middle, *tail0 = narrow(gelu0, w_narrow0, wide0[0], vec, 0)
        middle = onward([in1, wide_gather1, narrow_gather1], middle)
        w_in1 = assemble(in1.all(), owner)
        middle_sent = Sent(middle, [(1, 0)])
        q1, k1, v1, mixed1, lse1 = attend(middle, w_in1, vec, table_rows, seg_col, seg_row)
        mixed1 = onward([wide_gather1, narrow_gather1, middle_sent], mixed1)
        onward([wide_gather1, narrow_gather1, middle_sent])
        w_wide1 = assemble(wide_gather1.all(), owner)
        wide1 = widen(mixed1, middle, w_wide1, vec, table_rows)
        gelu1 = onward([narrow_gather1], wide1[2])
        onward([narrow_gather1])
        w_narrow1 = assemble(narrow_gather1.all(), owner)
        weights = [(w_in0, w_wide0, w_narrow0), (w_in1, w_wide1, w_narrow1)]
    else:
        weights = gather_plain(attn_in[0], attn_out[0], ff_in[0], ff_out[0])
        both = lax.all_gather(vectors, ("section", "dp")).reshape(2, n_dp, -1)
        vec = vector_table(both.transpose(1, 0, 2))
        q0, k0, v0, mixed0, lse0 = attend(my_tokens, weights[0][0], vec, 0, seg_col, seg_row)
        wide0 = widen(mixed0, my_tokens, weights[0][1], vec, 0)
        middle, *tail0 = narrow(wide0[2], weights[0][2], wide0[0], vec, 0)
        middle_sent = Sent(middle, [(1, 0)])
        q1, k1, v1, mixed1, lse1 = attend(middle, weights[1][0], vec, table_rows, seg_col, seg_row)
        wide1 = widen(mixed1, middle, weights[1][1], vec, table_rows)
        gelu1 = wide1[2]
        w_narrow1 = weights[1][2]
    final_low, *tail1, pooled, unit = narrow(
        gelu1, w_narrow1, wide1[0], vec, table_rows, seg_row
    )
    final_sent = Sent(final_low, [(0, 1)])
    running += [middle_sent, final_sent]

    table = gather_near(unit)
    total = MICRO * n_dp * segs
    where = jnp.stack([me, section])
    loss, grad_segs = contrast(where, table, pooled, group_ids, partner, seg_row, total)

    chunks = {}
    core = (me % 2)[None]

    def backward(layer, rows, heads, wide, tail, cot, segs_grad):
        base = layer * table_rows
        w_in, w_wide, w_narrow = weights[layer]
        q, k, v, mixed, lse = heads
        xhat1, rstd1, gelu, dgelu = wide
        grad_sum, grad_branch, small, keep, send = back_out(
            slot, cot, *tail, vec, base, gelu, *segs_grad
        )
        grad_branch = onward(running, grad_branch)
        chunks[layer, 2] = Reduction(core, keep, send)
        running.append(chunks[layer, 2])
        grad_pre, small, keep, send = back_pre(
            slot, grad_branch, w_narrow, dgelu, xhat1, vec, base, small
        )
        grad_pre = onward(running, grad_pre)
        chunks[layer, 1] = Reduction(core, keep, send)
        running.append(chunks[layer, 1])
        grad_x, grad_mixed, small, *chunk = back_mid(
            slot, grad_sum, grad_pre, w_wide, xhat1, rstd1, mixed, vec, base, small
        )
        grad_mixed = onward(running, grad_mixed)
        ins = (slot, rows, q, k, v, grad_mixed, lse, w_in)
        for first in range(groups):
            grad_x, grad_low, small, *chunk = attend_back(
                *ins, grad_x, seg_col, seg_row, small, first, 1, chunk
            )
            grad_x, grad_low = onward(running, (grad_x, grad_low))
        chunks[layer, 0] = Reduction(core, *chunk)
        running.append(chunks[layer, 0])
        return grad_x, grad_low, small

    heads = (q1, k1, v1, mixed1, lse1)
    grad_middle, grad_middle_low, small1 = backward(
        1, middle, heads, wide1, tail1, my_cotangent, (seg_col, grad_segs)
    )
    small1 = Sum(lax.dynamic_update_slice(small1, loss, (12, 0)))
    middle_grad_sent = Sent(grad_middle_low, [(0, 1)])
    running += [small1, middle_grad_sent]
    heads = (q0, k0, v0, mixed0, lse0)
    grad_tokens, grad_tokens_low, small0 = backward(
        0, my_tokens, heads, wide0, tail0, grad_middle_low, ()
    )
    small0 = Sum(small0)
    tokens_grad_sent = Sent(grad_tokens_low, [(1, 0)])
    running += [small0, tokens_grad_sent]

    settled = {}
    while True:
        for chunk in (2, 1, 0):
            ends = [chunks[layer, chunk] for layer in range(2)]
            if chunk not in settled and all(end.stage == 6 for end in ends):
                settled[chunk] = Settled(jnp.stack([me % 2, section]), *ends)
                running.append(settled[chunk])
        if not any(item.moving for item in running):
            break
        onward(running)

    if fast_ring():
        own_ff_out = settled[2].value
        own_ff_in = unblocked(settled[1].value.reshape(4, rows_in, D))
        own_attn_in = unblocked(settled[0].value[: 3 * rows_in].reshape(3, rows_in, D))
        own_attn_out = settled[0].value[3 * rows_in :]
    else:

        def natural(layer, name, blocks):
            item = chunks[layer, name]
            both = jnp.concatenate([item.keep, item.send])
            both = both.reshape(16, blocks, -1, D)
            return both.transpose(1, 0, 2, 3).reshape(blocks, -1, D)

        whole = [[], [], [], []]
        for layer in range(2):
            parts = natural(layer, 0, 4)
            whole[0].append(unblocked(parts[:3]))
            whole[1].append(parts[3])
            whole[2].append(unblocked(natural(layer, 1, 4)))
            whole[3].append(natural(layer, 2, 1)[0])
        own_attn_in, own_attn_out, own_ff_in, own_ff_out = (
            lax.psum_scatter(
                jnp.concatenate(pair).astype(f32), ("section", "dp"), scatter_dimension=0, tiled=True
            )
            for pair in whole
        )

    contrast_loss = small1.value[12, 0]
    small = jnp.where(leading, small0.value, small1.value)
    own_rows = lax.dynamic_slice(small, (0, me * rows_in), (8, rows_in))
    spot = me * rows_out
    own_bias = lax.dynamic_slice(small, (8 + spot // D, spot % D), (1, rows_out))

    hidden_states = jnp.where(
        leading,
        jnp.stack([middle, middle_sent.value()]),
        jnp.stack([final_sent.value(), final_low]),
    )
    hidden_grads = jnp.where(
        leading,
        jnp.stack([grad_tokens, tokens_grad_sent.value().astype(f32)]),
        jnp.stack([middle_grad_sent.value().astype(f32), grad_middle]),
    )
    return (
        contrast_loss,
        hidden_states[None, :, None],
        hidden_grads[None, :, None],
        own_attn_in[None],
        own_attn_out[None],
        own_ff_in[None],
        own_ff_out[None],
        own_rows[None, :2],
        own_rows[None, 2:],
        own_bias,
    )


def solution(mesh):
    return jax.shard_map(
        local,
        mesh=mesh,
        in_specs=(
            P(None, "dp", None, None),
            P(None, "dp", None, None),
            P(None, "dp", None),
            P(None, "dp"),
            P(),
            P("section", "dp", None),
            P("section", "dp", None),
            P("section", "dp", None),
            P("section", "dp", None),
            P("section", None, "dp"),
            P("section", None, "dp"),
            P("section", "dp"),
        ),
        out_specs=(
            P(),
            P("section", None, "dp", None, None),
            P("section", None, "dp", None, None),
            P("section", "dp", None),
            P("section", "dp", None),
            P("section", "dp", None),
            P("section", "dp", None),
            P("section", None, "dp"),
            P("section", None, "dp"),
            P("section", "dp"),
        ),
        check_vma=False,
    )
```

time: 699 us -> 571 us (0.82)
  matrix products: 191 us -> 0 us
  Pallas kernels: 63.4 us -> 172 us
  other arithmetic: 80.6 us -> 23.6 us
  local copies, waits for them, and re-layouts: 49 us -> 81.8 us
  waiting for transfers between devices: 200 us -> 178 us
    dot_general x40 -> x0, matrix products: 191 us -> none  [the longest x2 39.7 us: layer_forward(): jnp.dot(normed.astype(bf16), ff_in, preferred_element_type=f32) + ff_bias]
    pallas_call x12 -> x53, Pallas kernels: 63.4 us -> 172 us  [the longest x6 49.3 us: attend_back(): pl.pallas_call(partial(attend_back_kernel, first, len(chunk)), grid_spec=...]
    ppermute x48 -> x52, waiting for transfers between devices: 143 us -> 94.1 us  [ring_hop(): return lax.ppermute(value, 'dp', pairs)]
    unnamed x340 -> x367, local copies, waits for them, and re-layouts: 11.5 us -> 58.3 us
    convert_element_type x28 -> x5, other arithmetic: 27 us -> 1.83 us  [the longest x1 1.11 us: local(): cross_in = Cross(blocked(attn_in[0].astype(bf16)))]
    ppermute x0 -> x8, waiting for transfers between devices: none -> 17.4 us  [send(): self.moving = [lax.ppermute(half, 'section', self.pairs)]]
    ppermute x0 -> x8, starting transfers between devices: none -> 14.3 us  [send(): self.moving = [lax.ppermute(half, 'section', self.pairs)]]
    add x16 -> x12, other arithmetic: 14.4 us -> 0.19 us  [the longest x2 0.11 us: step(): self.value = self.keep + self.moving[0].astype(f32)]
  transfers between devices with their start and end apart: 113 -> 128, of which waited for: 40 -> 42; matrix products, arithmetic and copies ran while one was open for 40% -> 7% of each run, Pallas kernels for 8% -> 27%
where the time goes in v2:
time: 571 us; the launch traced here: 562 us
  waiting for transfers between devices  178 us (31%)
  Pallas kernels  172 us (30%)
  starting transfers between devices  103 us (18%)
  local copies, waits for them, and re-layouts  81.8 us (14%)
  other arithmetic  23.6 us (4%)
    ppermute x52, waiting for transfers between devices, ring_hop(): return lax.ppermute(value, 'dp', pairs)  94.1 us
    ppermute x68, waiting for transfers between devices, swapped(): return lax.ppermute(value, axis, [(i, i ^ mask) for i in range(count)])  66.7 us
    unnamed x367, local copies, waits for them, and re-layouts  58.3 us
    ppermute x52, starting transfers between devices, ring_hop(): return lax.ppermute(value, 'dp', pairs)  57.7 us
    pallas_call x6, Pallas kernels, attend_back(): pl.pallas_call(partial(attend_back_kernel, first, len(chunk)), grid_spec=...  49.3 us
    ppermute x68, starting transfers between devices, swapped(): return lax.ppermute(value, axis, [(i, i ^ mask) for i in range(count)])  31.4 us
    pallas_call x2, Pallas kernels, widen(): pl.pallas_call(partial(widen_kernel, base), grid=(FF // D,), in_specs=[fu...  19.9 us
    ppermute x8, waiting for transfers between devices, send(): self.moving = [lax.ppermute(half, 'section', self.pairs)]  17.4 us
  transfers between devices with their start and end apart: 128, of which 42 were waited for; matrix products, arithmetic and copies ran while one was open for 7% of the time, Pallas kernels for 27%

profile of v2, /device:TPU:0, one launch (start us, length us, event | category | flops | bytes accessed | tf_op | source)
XLA Modules:
  0.0 561.8 jit_solution(13824897544954966975)
XLA Ops:
  39.5 6.6 %collective-permute-done.17 = bf16[1,192,768]{2,1,0:T(8,128)(2,1)S(1)} collective-permute-done((bf16[1,192,768]{2,1,0:T(8,128)(2,1)S(1)}, bf16[1,192,768]{2,1,0:T(8,128)(2,1)S(1)}, u32[]{:S(2)}, u32[]{:S(2)}) %collective-permute-start.17) | collective-permute-done | bytes 294944 | tf_op jit(solution)/shard_map/ppermute | solution.py:37
  56.1 8.4 %collective-permute-done.20.refs_4_ = bf16[1,1,16,768]{3,2,1,0:T(8,128)(2,1)S(1)} collective-permute-done((bf16[1,1,16,768]{3,2,1,0:T(8,128)(2,1)S(1)}, bf16[1,1,16,768]{3,2,1,0:T(8,128)(2,1)S(1)}, u32[]{:S(2)}, u32[]{:S(2)}) %collective-permute-start.20) | collective-permute-done | bytes 24608 | tf_op jit(solution)/shard_map/ppermute | solution.py:52
  82.6 7.8 %collective-permute-done.29.refs_1_ = bf16[2,1,192,768]{3,2,1,0:T(8,128)(2,1)} collective-permute-done((bf16[2,1,192,768]{3,2,1,0:T(8,128)(2,1)S(1)}, bf16[2,1,192,768]{3,2,1,0:T(8,128)(2,1)}, u32[]{:S(2)}, u32[]{:S(2)}) %collective-permute-start.29) | collective-permute-done | bytes 589856 | tf_op jit(solution)/shard_map/ppermute | solution.py:52
  117.0 8.7 %attend.2 = (bf16[512,768]{1,0:T(8,128)(2,1)S(1)}, bf16[512,768]{1,0:T(8,128)(2,1)S(1)}, bf16[512,768]{1,0:T(8,128)(2,1)S(1)}, bf16[512,768]{1,0:T(8,128)(2,1)S(1)}, f32[3,512,128]{2,1,0:T(8,128)S(1)}) custom-call(bf16[512,768]{1,0:T(8,128)(2,1)S(1)} %get-tuple-element.533.x_ref.refs_0_, ...), custom_call_target="tpu_custom_call" | custom-call | flops 30198988800 | bytes 300000000 | tf_op jit(solution)/shard_map/attend/pallas_call | solution.py:399
  134.3 10.1 %collective-permute-done.39.refs_2_ = bf16[2,3,48,768]{3,2,1,0:T(8,128)(2,1)S(1)} collective-permute-done((bf16[2,3,48,768]{3,2,1,0:T(8,128)(2,1)}, bf16[2,3,48,768]{3,2,1,0:T(8,128)(2,1)S(1)}, u32[]{:S(2)}, u32[]{:S(2)}) %collective-permute-start.39) | collective-permute-done | bytes 442400 | tf_op jit(solution)/shard_map/ppermute | solution.py:52
  153.2 10.0 %widen.2 = (f32[512,768]{1,0:T(8,128)S(1)}, f32[512,1]{1,0:T(8,128)S(1)}, bf16[512,3072]{1,0:T(8,128)(2,1)S(1)}, bf16[512,3072]{1,0:T(8,128)(2,1)S(1)}) custom-call(bf16[512,768]{1,0:T(8,128)(2,1)S(1)} %get-tuple-element.280.mixed_ref.refs_5_, bf16[512,768]{1,0:T(8,128)(2,1)S(1)} %copy-done.38, ...), custom_call_target="tpu_custom_call" | custom-call | flops 30198988800 | bytes 300000000 | tf_op jit(solution)/shard_map/widen/pallas_call | solution.py:454
  177.3 7.8 %collective-permute-done.48.refs_4_ = bf16[1,3,48,768]{3,2,1,0:T(8,128)(2,1)} collective-permute-done((bf16[1,3,48,768]{3,2,1,0:T(8,128)(2,1)}, bf16[1,3,48,768]{3,2,1,0:T(8,128)(2,1)}, u32[]{:S(2)}, u32[]{:S(2)}) %collective-permute-start.48) | collective-permute-done | bytes 221216 | tf_op jit(solution)/shard_map/ppermute | solution.py:52
  214.2 8.7 %attend.3 = (bf16[512,768]{1,0:T(8,128)(2,1)S(1)}, bf16[512,768]{1,0:T(8,128)(2,1)S(1)}, bf16[512,768]{1,0:T(8,128)(2,1)S(1)}, bf16[512,768]{1,0:T(8,128)(2,1)S(1)}, f32[3,512,128]{2,1,0:T(8,128)S(1)}) custom-call(bf16[512,768]{1,0:T(8,128)(2,1)S(1)} %get-tuple-element.307.x_ref.refs_0_, ...), custom_call_target="tpu_custom_call" | custom-call | flops 30198988800 | bytes 300000000 | tf_op jit(solution)/shard_map/attend/pallas_call | solution.py:399
  226.1 11.8 %collective-permute-done.65 = bf16[256,768]{1,0:T(8,128)(2,1)S(1)} collective-permute-done((bf16[256,768]{1,0:T(8,128)(2,1)S(1)}, bf16[256,768]{1,0:T(8,128)(2,1)S(1)}, u32[]{:S(2)}, u32[]{:S(2)}) %collective-permute-start.65) | collective-permute-done | bytes 393248 | tf_op jit(solution)/shard_map/ppermute | solution.py:245
  242.3 10.0 %widen.3 = (f32[512,768]{1,0:T(8,128)S(1)}, f32[512,1]{1,0:T(8,128)S(1)}, bf16[512,3072]{1,0:T(8,128)(2,1)S(1)}, bf16[512,3072]{1,0:T(8,128)(2,1)S(1)}) custom-call(bf16[512,768]{1,0:T(8,128)(2,1)S(1)} %get-tuple-element.318.mixed_ref.refs_5_, bf16[512,768]{1,0:T(8,128)(2,1)S(1)} %get-tuple-element.307.x_ref.refs_0_, ...), custom_call_target="tpu_custom_call" | custom-call | flops 30198988800 | bytes 300000000 | tf_op jit(solution)/shard_map/widen/pallas_call | solution.py:454
  277.5 6.4 %back_out.2 = (f32[512,768]{1,0:T(8,128)S(1)}, bf16[512,768]{1,0:T(8,128)(2,1)S(1)}, f32[16,768]{1,0:T(8,128)S(1)}, bf16[8,192,768]{2,1,0:T(8,128)(2,1)S(1)}, bf16[8,192,768]{2,1,0:T(8,128)(2,1)S(1)}) custom-call(s32[16]{0:T(128)S(1)} %select_reduce_fusion.slot_ref, bf16[512,768]{1,0:T(8,128)(2,1)S(1)} %copy-done.40, s32[512,1]{1,0:T(8,128)S(1)} %copy-done.82, ...), custom_call_target="tpu_custom_call" | custom-call | flops 24159191040 | bytes 200000000 | tf_op jit(solution)/shard_map/back_out/pallas_call | solution.py:658
  284.1 8.3 %back_pre.2 = (bf16[512,3072]{1,0:T(8,128)(2,1)S(1)}, f32[16,768]{1,0:T(8,128)S(1)}, bf16[8,192,768]{2,1,0:T(8,128)(2,1)S(1)}, bf16[8,192,768]{2,1,0:T(8,128)(2,1)S(1)}) custom-call(s32[16]{0:T(128)S(1)} %select_reduce_fusion.slot_ref, bf16[512,768]{1,0:T(8,128)(2,1)S(1)} %get-tuple-element.341.refs_0_, bf16[1,3072,768]{2,1,0:T(8,128)(2,1)S(1)} %assemble.13.wf_ref.refs_1_, ...), custom_call_target="tpu_custom_call" | custom-call | flops 48318382080 | bytes 300000000 | tf_op jit(solution)/shard_map/back_pre/pallas_call | solution.py:699
  295.0 6.8 %back_mid.2 = (f32[512,768]{1,0:T(8,128)S(1)}, bf16[512,768]{1,0:T(8,128)(2,1)S(1)}, f32[16,768]{1,0:T(8,128)S(1)}, bf16[8,192,768]{2,1,0:T(8,128)(2,1)S(1)}, bf16[8,192,768]{2,1,0:T(8,128)(2,1)S(1)}) custom-call(s32[16]{0:T(128)S(1)} %select_reduce_fusion.slot_ref, f32[512,768]{1,0:T(8,128)S(1)} %get-tuple-element.338.refs_0_, ...), custom_call_target="tpu_custom_call" | custom-call | flops 36238786560 | bytes 300000000 | tf_op jit(solution)/shard_map/back_mid/pallas_call | solution.py:755
  304.7 8.4 %attend_back.6 = (f32[512,768]{1,0:T(8,128)S(1)}, bf16[512,768]{1,0:T(8,128)(2,1)}, f32[16,768]{1,0:T(8,128)S(1)}, bf16[8,192,768]{2,1,0:T(8,128)(2,1)S(1)}, bf16[8,192,768]{2,1,0:T(8,128)(2,1)S(1)}) custom-call(s32[16]{0:T(128)S(1)} %select_reduce_fusion.slot_ref, ...), custom_call_target="tpu_custom_call", output_to_operand_aliasing={{3}: (14, {}), {4}: (15, {})} | custom-call | flops 36238786560 | bytes 300000000 | tf_op jit(solution)/shard_map/attend_back/pallas_call | solution.py:836
  317.7 8.8 %attend_back.7 = (f32[512,768]{1,0:T(8,128)S(1)}, bf16[512,768]{1,0:T(8,128)(2,1)}, f32[16,768]{1,0:T(8,128)S(1)}, bf16[8,192,768]{2,1,0:T(8,128)(2,1)S(1)}, bf16[8,192,768]{2,1,0:T(8,128)(2,1)S(1)}) custom-call(s32[16]{0:T(128)S(1)} %select_reduce_fusion.slot_ref, ...), custom_call_target="tpu_custom_call", output_to_operand_aliasing={{3}: (14, {}), {4}: (15, {})} | custom-call | flops 36238786560 | bytes 300000000 | tf_op jit(solution)/shard_map/attend_back/pallas_call | solution.py:836
  326.4 5.2 collective-permute-done.80.refs_0_
  335.5 7.5 %attend_back.8 = (f32[512,768]{1,0:T(8,128)S(1)}, bf16[512,768]{1,0:T(8,128)(2,1)S(1)}, f32[16,768]{1,0:T(8,128)S(1)}, bf16[8,192,768]{2,1,0:T(8,128)(2,1)S(1)}, bf16[8,192,768]{2,1,0:T(8,128)(2,1)S(1)}) custom-call(s32[16]{0:T(128)S(1)} %select_reduce_fusion.slot_ref, ...), custom_call_target="tpu_custom_call", output_to_operand_aliasing={{3}: (14, {}), {4}: (15, {})} | custom-call | flops 36238786560 | bytes 300000000 | tf_op jit(solution)/shard_map/attend_back/pallas_call | solution.py:836
  360.0 5.8 %back_out.3 = (f32[512,768]{1,0:T(8,128)S(1)}, bf16[512,768]{1,0:T(8,128)(2,1)S(1)}, f32[16,768]{1,0:T(8,128)S(1)}, bf16[8,192,768]{2,1,0:T(8,128)(2,1)S(1)}, bf16[8,192,768]{2,1,0:T(8,128)(2,1)S(1)}) custom-call(s32[16]{0:T(128)S(1)} %select_reduce_fusion.slot_ref, bf16[512,768]{1,0:T(8,128)(2,1)S(1)} %get-tuple-element.380.refs_0_, ...), custom_call_target="tpu_custom_call" | custom-call | flops 24159191040 | bytes 200000000 | tf_op jit(solution)/shard_map/back_out/pallas_call | solution.py:658
  373.3 8.3 %back_pre.3 = (bf16[512,3072]{1,0:T(8,128)(2,1)S(1)}, f32[16,768]{1,0:T(8,128)S(1)}, bf16[8,192,768]{2,1,0:T(8,128)(2,1)S(1)}, bf16[8,192,768]{2,1,0:T(8,128)(2,1)S(1)}) custom-call(s32[16]{0:T(128)S(1)} %select_reduce_fusion.slot_ref, bf16[512,768]{1,0:T(8,128)(2,1)S(1)} %get-tuple-element.388.refs_0_, bf16[1,3072,768]{2,1,0:T(8,128)(2,1)S(1)} %bitcast.87, ...), custom_call_target="tpu_custom_call" | custom-call | flops 48318382080 | bytes 300000000 | tf_op jit(solution)/shard_map/back_pre/pallas_call | solution.py:699
  387.3 6.8 %back_mid.3 = (f32[512,768]{1,0:T(8,128)S(1)}, bf16[512,768]{1,0:T(8,128)(2,1)S(1)}, f32[16,768]{1,0:T(8,128)S(1)}, bf16[8,192,768]{2,1,0:T(8,128)(2,1)S(1)}, bf16[8,192,768]{2,1,0:T(8,128)(2,1)S(1)}) custom-call(s32[16]{0:T(128)S(1)} %select_reduce_fusion.slot_ref, f32[512,768]{1,0:T(8,128)S(1)} %copy-done.119, bf16[512,3072]{1,0:T(8,128)(2,1)S(1)} %copy-done.117, ...), custom_call_target="tpu_custom_call" | custom-call | flops 36238786560 | bytes 300000000 | tf_op jit(solution)/shard_map/back_mid/pallas_call | solution.py:755
  402.0 8.6 %attend_back.9 = (f32[512,768]{1,0:T(8,128)S(1)}, bf16[512,768]{1,0:T(8,128)(2,1)}, f32[16,768]{1,0:T(8,128)S(1)}, bf16[8,192,768]{2,1,0:T(8,128)(2,1)S(1)}, bf16[8,192,768]{2,1,0:T(8,128)(2,1)S(1)}) custom-call(s32[16]{0:T(128)S(1)} %select_reduce_fusion.slot_ref, bf16[512,768]{1,0:T(8,128)(2,1)S(1)} %copy-done.39, ...), custom_call_target="tpu_custom_call", output_to_operand_aliasing={{3}: (14, {}), {4}: (15, {})} | custom-call | flops 36238786560 | bytes 300000000 | tf_op jit(solution)/shard_map/attend_back/pallas_call | solution.py:836
  410.9 6.3 %collective-permute-done.98.refs_0_ = bf16[2,192,768]{2,1,0:T(8,128)(2,1)S(1)} collective-permute-done((bf16[2,192,768]{2,1,0:T(8,128)(2,1)S(1)}, bf16[2,192,768]{2,1,0:T(8,128)(2,1)S(1)}, u32[]{:S(2)}, u32[]{:S(2)}) %collective-permute-start.98) | collective-permute-done | bytes 589856 | tf_op jit(solution)/shard_map/ppermute | solution.py:52
  422.7 8.4 %attend_back.10 = (f32[512,768]{1,0:T(8,128)S(1)}, bf16[512,768]{1,0:T(8,128)(2,1)}, f32[16,768]{1,0:T(8,128)S(1)}, bf16[8,192,768]{2,1,0:T(8,128)(2,1)S(1)}, bf16[8,192,768]{2,1,0:T(8,128)(2,1)S(1)}) custom-call(s32[16]{0:T(128)S(1)} %select_reduce_fusion.slot_ref, bf16[512,768]{1,0:T(8,128)(2,1)S(1)} %copy-done.39, ...), custom_call_target="tpu_custom_call", output_to_operand_aliasing={{3}: (14, {}), {4}: (15, {})} | custom-call | flops 36238786560 | bytes 300000000 | tf_op jit(solution)/shard_map/attend_back/pallas_call | solution.py:836
  433.8 6.3 %collective-permute-done.102.refs_6_ = bf16[2,192,768]{2,1,0:T(8,128)(2,1)S(1)} collective-permute-done((bf16[2,192,768]{2,1,0:T(8,128)(2,1)S(1)}, bf16[2,192,768]{2,1,0:T(8,128)(2,1)S(1)}, u32[]{:S(2)}, u32[]{:S(2)}) %collective-permute-start.102) | collective-permute-done | bytes 589856 | tf_op jit(solution)/shard_map/ppermute | solution.py:52
  440.1 7.7 %attend_back.11 = (f32[512,768]{1,0:T(8,128)S(1)}, bf16[512,768]{1,0:T(8,128)(2,1)S(1)}, f32[16,768]{1,0:T(8,128)S(1)}, bf16[8,192,768]{2,1,0:T(8,128)(2,1)S(1)}, bf16[8,192,768]{2,1,0:T(8,128)(2,1)S(1)}) custom-call(s32[16]{0:T(128)S(1)} %select_reduce_fusion.slot_ref, ...), custom_call_target="tpu_custom_call", output_to_operand_aliasing={{3}: (14, {}), {4}: (15, {})} | custom-call | flops 36238786560 | bytes 300000000 | tf_op jit(solution)/shard_map/attend_back/pallas_call | solution.py:836
  452.8 6.4 %collective-permute-done.108.refs_0_ = bf16[2,192,768]{2,1,0:T(8,128)(2,1)S(1)} collective-permute-done((bf16[2,192,768]{2,1,0:T(8,128)(2,1)S(1)}, bf16[2,192,768]{2,1,0:T(8,128)(2,1)S(1)}, u32[]{:S(2)}, u32[]{:S(2)}) %collective-permute-start.108) | collective-permute-done | bytes 589856 | tf_op jit(solution)/shard_map/ppermute | solution.py:52
  459.2 6.3 %collective-permute-done.107.refs_2_ = bf16[2,192,768]{2,1,0:T(8,128)(2,1)S(1)} collective-permute-done((bf16[2,192,768]{2,1,0:T(8,128)(2,1)S(1)}, bf16[2,192,768]{2,1,0:T(8,128)(2,1)S(1)}, u32[]{:S(2)}, u32[]{:S(2)}) %collective-permute-start.107) | collective-permute-done | bytes 589856 | tf_op jit(solution)/shard_map/ppermute | solution.py:52
  472.4 10.5 %collective-permute-done.112 = f32[16,768]{1,0:T(8,128)S(1)} collective-permute-done((f32[16,768]{1,0:T(8,128)S(1)}, f32[16,768]{1,0:T(8,128)S(1)}, u32[]{:S(2)}, u32[]{:S(2)}) %collective-permute-start.112) | collective-permute-done | bytes 49184 | tf_op jit(solution)/shard_map/ppermute | solution.py:37
  491.2 5.6 collective-permute-done.117
  496.8 5.9 %collective-permute-done.118 = bf16[192,768]{1,0:T(8,128)(2,1)S(1)} collective-permute-done((bf16[192,768]{1,0:T(8,128)(2,1)S(1)}, bf16[192,768]{1,0:T(8,128)(2,1)S(1)}, u32[]{:S(2)}, u32[]{:S(2)}) %collective-permute-start.118) | collective-permute-done | bytes 294944 | tf_op jit(solution)/shard_map/ppermute | solution.py:37
  506.6 7.7 %collective-permute-done.120 = f32[16,768]{1,0:T(8,128)S(1)} collective-permute-done((f32[16,768]{1,0:T(8,128)S(1)}, f32[16,768]{1,0:T(8,128)S(1)}, u32[]{:S(2)}, u32[]{:S(2)}) %collective-permute-start.120) | collective-permute-done | bytes 49184 | tf_op jit(solution)/shard_map/ppermute | solution.py:37
  552.9 6.4 %collective-permute-done.127 = bf16[192,768]{1,0:T(8,128)(2,1)S(1)} collective-permute-done((bf16[192,768]{1,0:T(8,128)(2,1)S(1)}, bf16[192,768]{1,0:T(8,128)(2,1)S(1)}, u32[]{:S(2)}, u32[]{:S(2)}) %collective-permute-start.127) | collective-permute-done | bytes 294944 | tf_op jit(solution)/shard_map/ppermute | solution.py:37
  (754 shorter events, 310.6 us)
Async XLA Ops:
  34.4 18.2 %collective-permute-start.16 = (bf16[2,5,48,768]{3,2,1,0:T(8,128)(2,1)S(1)}, bf16[2,5,48,768]{3,2,1,0:T(8,128)(2,1)}, u32[]{:S(2)}, u32[]{:S(2)}) collective-permute-start(bf16[2,5,48,768]{3,2,1,0:T(8,128)(2,1)S(1)} %pad_maximum_fusion.refs_0_), channel_id=1, source_target_pairs={{0,4},{1,3},{4,8},{5,1},{8,12},{9,5},{12,14},{13,9},{14,10},{15,13... | collective-permute-start | bytes 2211848 | tf_op jit(solution)/shard_map/ppermute | solution.py:52
  35.0 16.8 %collective-permute-start.12 = (bf16[2,3,48,768]{3,2,1,0:T(8,128)(2,1)S(1)}, bf16[2,3,48,768]{3,2,1,0:T(8,128)(2,1)S(1)}, u32[]{:S(2)}, u32[]{:S(2)}) collective-permute-start(bf16[2,3,48,768]{3,2,1,0:T(8,128)(2,1)S(1)} %collective-permute-done.7.refs_2_), channel_id=1, source_target_pairs={{0,4},{1,3},{4,8},{5,1},{8,12},{9,5},{12,14},{13,9},{14,10},{15,13... | collective-permute-start | bytes 1327112 | tf_op jit(solution)/shard_map/ppermute | solution.py:52
  52.6 19.7 %collective-permute-start.22 = (bf16[2,5,48,768]{3,2,1,0:T(8,128)(2,1)}, bf16[2,5,48,768]{3,2,1,0:T(8,128)(2,1)}, u32[]{:S(2)}, u32[]{:S(2)}) collective-permute-start(bf16[2,5,48,768]{3,2,1,0:T(8,128)(2,1)} %collective-permute-done.16.refs_1_), channel_id=1, source_target_pairs={{0,4},{1,3},{4,8},{5,1},{8,12},{9,5},{12,14},{13,9},{14,10},{15,13... | collective-permute-start | bytes 2211848 | tf_op jit(solution)/shard_map/ppermute | solution.py:52
  53.1 19.2 %collective-permute-start.23 = (bf16[2,5,48,768]{3,2,1,0:T(8,128)(2,1)}, bf16[2,5,48,768]{3,2,1,0:T(8,128)(2,1)}, u32[]{:S(2)}, u32[]{:S(2)}) collective-permute-start(bf16[2,5,48,768]{3,2,1,0:T(8,128)(2,1)} %collective-permute-done.16.refs_1_), channel_id=1, source_target_pairs={{0,1},{1,0},{2,3},{3,2},{4,5},{5,4},{6,7},{7,6},{8,9},{9,8},{10,11... | collective-permute-start | bytes 2211848 | tf_op jit(solution)/shard_map/ppermute | solution.py:37
  53.6 17.9 %collective-permute-start.19 = (bf16[2,3,48,768]{3,2,1,0:T(8,128)(2,1)S(1)}, bf16[2,3,48,768]{3,2,1,0:T(8,128)(2,1)S(1)}, u32[]{:S(2)}, u32[]{:S(2)}) collective-permute-start(bf16[2,3,48,768]{3,2,1,0:T(8,128)(2,1)S(1)} %collective-permute-done.12.refs_3_), channel_id=1, source_target_pairs={{0,1},{1,0},{2,3},{3,2},{4,5},{5,4},{6,7},{7,6},{8,9},{9,8},{10,11... | collective-permute-start | bytes 1327112 | tf_op jit(solution)/shard_map/ppermute | solution.py:37
  72.3 18.1 %collective-permute-start.27 = (bf16[2,5,48,768]{3,2,1,0:T(8,128)(2,1)}, bf16[2,5,48,768]{3,2,1,0:T(8,128)(2,1)}, u32[]{:S(2)}, u32[]{:S(2)}) collective-permute-start(bf16[2,5,48,768]{3,2,1,0:T(8,128)(2,1)} %collective-permute-done.22.refs_2_), channel_id=1, source_target_pairs={{0,4},{1,3},{4,8},{5,1},{8,12},{9,5},{12,14},{13,9},{14,10},{15,13... | collective-permute-start | bytes 2211848 | tf_op jit(solution)/shard_map/ppermute | solution.py:52
  72.8 17.6 %collective-permute-start.28 = (bf16[2,5,48,768]{3,2,1,0:T(8,128)(2,1)}, bf16[2,5,48,768]{3,2,1,0:T(8,128)(2,1)}, u32[]{:S(2)}, u32[]{:S(2)}) collective-permute-start(bf16[2,5,48,768]{3,2,1,0:T(8,128)(2,1)} %collective-permute-done.22.refs_2_), channel_id=1, source_target_pairs={{0,1},{1,0},{2,3},{3,2},{4,5},{5,4},{6,7},{7,6},{8,9},{9,8},{10,11... | collective-permute-start | bytes 2211848 | tf_op jit(solution)/shard_map/ppermute | solution.py:37
  74.0 16.3 %collective-permute-start.29 = (bf16[2,1,192,768]{3,2,1,0:T(8,128)(2,1)S(1)}, bf16[2,1,192,768]{3,2,1,0:T(8,128)(2,1)}, u32[]{:S(2)}, u32[]{:S(2)}) collective-permute-start(bf16[2,1,192,768]{3,2,1,0:T(8,128)(2,1)S(1)} %pad_maximum_fusion.2.refs_0_), channel_id=1, source_target_pairs={{0,4},{1,3},{4,8},{5,1},{8,12},{9,5},{12,14},{13,9},{14,10},{15,13... | collective-permute-start | bytes 1769480 | tf_op jit(solution)/shard_map/ppermute | solution.py:52
  99.6 29.7 %collective-permute-start.32 = (bf16[2,5,48,768]{3,2,1,0:T(8,128)(2,1)}, bf16[2,5,48,768]{3,2,1,0:T(8,128)(2,1)}, u32[]{:S(2)}, u32[]{:S(2)}) collective-permute-start(bf16[2,5,48,768]{3,2,1,0:T(8,128)(2,1)} %collective-permute-done.27.refs_3_), channel_id=1, source_target_pairs={{0,1},{1,0},{2,3},{3,2},{4,5},{5,4},{6,7},{7,6},{8,9},{9,8},{10,11... | collective-permute-start | bytes 2211848 | tf_op jit(solution)/shard_map/ppermute | solution.py:37
  99.6 29.7 %collective-permute-start.33 = (bf16[2,1,192,768]{3,2,1,0:T(8,128)(2,1)}, bf16[2,1,192,768]{3,2,1,0:T(8,128)(2,1)}, u32[]{:S(2)}, u32[]{:S(2)}) collective-permute-start(bf16[2,1,192,768]{3,2,1,0:T(8,128)(2,1)} %collective-permute-done.29.refs_1_), channel_id=1, source_target_pairs={{0,4},{1,3},{4,8},{5,1},{8,12},{9,5},{12,14},{13,9},{14,10},{15,13... | collective-permute-start | bytes 1769480 | tf_op jit(solution)/shard_map/ppermute | solution.py:52
  100.1 29.1 %collective-permute-start.34 = (bf16[2,1,192,768]{3,2,1,0:T(8,128)(2,1)}, bf16[2,1,192,768]{3,2,1,0:T(8,128)(2,1)}, u32[]{:S(2)}, u32[]{:S(2)}) collective-permute-start(bf16[2,1,192,768]{3,2,1,0:T(8,128)(2,1)} %collective-permute-done.29.refs_1_), channel_id=1, source_target_pairs={{0,1},{1,0},{2,3},{3,2},{4,5},{5,4},{6,7},{7,6},{8,9},{9,8},{10,11... | collective-permute-start | bytes 1769480 | tf_op jit(solution)/shard_map/ppermute | solution.py:37
  102.1 27.2 %collective-permute-start.35 = (bf16[2,3,48,768]{3,2,1,0:T(8,128)(2,1)S(1)}, bf16[2,3,48,768]{3,2,1,0:T(8,128)(2,1)}, u32[]{:S(2)}, u32[]{:S(2)}) collective-permute-start(bf16[2,3,48,768]{3,2,1,0:T(8,128)(2,1)S(1)} %pad_maximum_fusion.5.refs_0_), channel_id=1, source_target_pairs={{0,4},{1,3},{4,8},{5,1},{8,12},{9,5},{12,14},{13,9},{14,10},{15,13... | collective-permute-start | bytes 1327112 | tf_op jit(solution)/shard_map/ppermute | solution.py:52
  107.0 22.3 %collective-permute-start.31 = (bf16[1,5,48,768]{3,2,1,0:T(8,128)(2,1)}, bf16[1,5,48,768]{3,2,1,0:T(8,128)(2,1)S(1)}, u32[]{:S(2)}, u32[]{:S(2)}) collective-permute-start(bf16[1,5,48,768]{3,2,1,0:T(8,128)(2,1)} %slice.89), channel_id=1, source_target_pairs={{0,4},{1,3},{4,8},{5,1},{8,12},{9,5},{12,14},{13,9},{14,10},{15,13... | collective-permute-start | bytes 1105928 | tf_op jit(solution)/shard_map/ppermute | solution.py:52
  145.3 24.8 %collective-permute-start.43 = (bf16[2,1,192,768]{3,2,1,0:T(8,128)(2,1)S(1)}, bf16[2,1,192,768]{3,2,1,0:T(8,128)(2,1)S(1)}, u32[]{:S(2)}, u32[]{:S(2)}) collective-permute-start(bf16[2,1,192,768]{3,2,1,0:T(8,128)(2,1)S(1)} %collective-permute-done.37.refs_3_), channel_id=1, source_target_pairs={{0,1},{1,0},{2,3},{3,2},{4,5},{5,4},{6,7},{7,6},{8,9},{9,8},{10,11... | collective-permute-start | bytes 1769480 | tf_op jit(solution)/shard_map/ppermute | solution.py:37
  145.3 23.9 %collective-permute-start.44 = (bf16[2,3,48,768]{3,2,1,0:T(8,128)(2,1)S(1)}, bf16[2,3,48,768]{3,2,1,0:T(8,128)(2,1)S(1)}, u32[]{:S(2)}, u32[]{:S(2)}) collective-permute-start(bf16[2,3,48,768]{3,2,1,0:T(8,128)(2,1)S(1)} %collective-permute-done.39.refs_2_), channel_id=1, source_target_pairs={{0,4},{1,3},{4,8},{5,1},{8,12},{9,5},{12,14},{13,9},{14,10},{15,13... | collective-permute-start | bytes 1327112 | tf_op jit(solution)/shard_map/ppermute | solution.py:52
  146.8 22.5 %collective-permute-start.45 = (bf16[2,3,48,768]{3,2,1,0:T(8,128)(2,1)S(1)}, bf16[2,3,48,768]{3,2,1,0:T(8,128)(2,1)S(1)}, u32[]{:S(2)}, u32[]{:S(2)}) collective-permute-start(bf16[2,3,48,768]{3,2,1,0:T(8,128)(2,1)S(1)} %collective-permute-done.39.refs_2_), channel_id=1, source_target_pairs={{0,1},{1,0},{2,3},{3,2},{4,5},{5,4},{6,7},{7,6},{8,9},{9,8},{10,11... | collective-permute-start | bytes 1327112 | tf_op jit(solution)/shard_map/ppermute | solution.py:37
  147.6 23.3 %collective-permute-start.46 = (bf16[2,5,48,768]{3,2,1,0:T(8,128)(2,1)S(1)}, bf16[2,5,48,768]{3,2,1,0:T(8,128)(2,1)}, u32[]{:S(2)}, u32[]{:S(2)}) collective-permute-start(bf16[2,5,48,768]{3,2,1,0:T(8,128)(2,1)S(1)} %pad_maximum_fusion.1.refs_0_), channel_id=1, source_target_pairs={{0,4},{1,3},{4,8},{5,1},{8,12},{9,5},{12,14},{13,9},{14,10},{15,13... | collective-permute-start | bytes 2211848 | tf_op jit(solution)/shard_map/ppermute | solution.py:52
  148.7 20.5 %collective-permute-start.42 = (bf16[1,1,192,768]{3,2,1,0:T(8,128)(2,1)S(1)}, bf16[1,1,192,768]{3,2,1,0:T(8,128)(2,1)S(1)}, u32[]{:S(2)}, u32[]{:S(2)}) collective-permute-start(bf16[1,1,192,768]{3,2,1,0:T(8,128)(2,1)S(1)} %slice.90), channel_id=1, source_target_pairs={{0,4},{1,3},{4,8},{5,1},{8,12},{9,5},{12,14},{13,9},{14,10},{15,13... | collective-permute-start | bytes 884744 | tf_op jit(solution)/shard_map/ppermute | solution.py:52
  170.9 18.0 %collective-permute-start.50 = (bf16[2,5,48,768]{3,2,1,0:T(8,128)(2,1)}, bf16[2,5,48,768]{3,2,1,0:T(8,128)(2,1)}, u32[]{:S(2)}, u32[]{:S(2)}) collective-permute-start(bf16[2,5,48,768]{3,2,1,0:T(8,128)(2,1)} %collective-permute-done.46.refs_1_), channel_id=1, source_target_pairs={{0,4},{1,3},{4,8},{5,1},{8,12},{9,5},{12,14},{13,9},{14,10},{15,13... | collective-permute-start | bytes 2211848 | tf_op jit(solution)/shard_map/ppermute | solution.py:52
  172.0 16.9 %collective-permute-start.51 = (bf16[2,5,48,768]{3,2,1,0:T(8,128)(2,1)}, bf16[2,5,48,768]{3,2,1,0:T(8,128)(2,1)S(1)}, u32[]{:S(2)}, u32[]{:S(2)}) collective-permute-start(bf16[2,5,48,768]{3,2,1,0:T(8,128)(2,1)} %collective-permute-done.46.refs_1_), channel_id=1, source_target_pairs={{0,1},{1,0},{2,3},{3,2},{4,5},{5,4},{6,7},{7,6},{8,9},{9,8},{10,11... | collective-permute-start | bytes 2211848 | tf_op jit(solution)/shard_map/ppermute | solution.py:37
  189.8 18.0 %collective-permute-start.54 = (bf16[2,5,48,768]{3,2,1,0:T(8,128)(2,1)}, bf16[2,5,48,768]{3,2,1,0:T(8,128)(2,1)S(1)}, u32[]{:S(2)}, u32[]{:S(2)}) collective-permute-start(bf16[2,5,48,768]{3,2,1,0:T(8,128)(2,1)} %collective-permute-done.50.refs_2_), channel_id=1, source_target_pairs={{0,4},{1,3},{4,8},{5,1},{8,12},{9,5},{12,14},{13,9},{14,10},{15,13... | collective-permute-start | bytes 2211848 | tf_op jit(solution)/shard_map/ppermute | solution.py:52
  190.9 17.0 %collective-permute-start.55 = (bf16[2,5,48,768]{3,2,1,0:T(8,128)(2,1)}, bf16[2,5,48,768]{3,2,1,0:T(8,128)(2,1)S(1)}, u32[]{:S(2)}, u32[]{:S(2)}) collective-permute-start(bf16[2,5,48,768]{3,2,1,0:T(8,128)(2,1)} %collective-permute-done.50.refs_2_), channel_id=1, source_target_pairs={{0,1},{1,0},{2,3},{3,2},{4,5},{5,4},{6,7},{7,6},{8,9},{9,8},{10,11... | collective-permute-start | bytes 2211848 | tf_op jit(solution)/shard_map/ppermute | solution.py:37
  266.3 17.8 %collective-permute-start.73 = (bf16[256,768]{1,0:T(8,128)(2,1)S(1)}, bf16[256,768]{1,0:T(8,128)(2,1)S(1)}, u32[]{:S(2)}, u32[]{:S(2)}) collective-permute-start(bf16[256,768]{1,0:T(8,128)(2,1)S(1)} %get-tuple-element.517), channel_id=1, source_target_pairs={{0,16},{1,17},{2,18},{3,19},{4,20},{5,21},{6,22},{7,23},{8,24},{9,... | collective-permute-start | bytes 1179656 | tf_op jit(solution)/shard_map/ppermute | solution.py:245
  267.8 25.1 %collective-permute-start.74 = (bf16[256,768]{1,0:T(8,128)(2,1)S(1)}, bf16[256,768]{1,0:T(8,128)(2,1)S(1)}, u32[]{:S(2)}, u32[]{:S(2)}) collective-permute-start(bf16[256,768]{1,0:T(8,128)(2,1)S(1)} %get-tuple-element.516), channel_id=1, source_target_pairs={{0,16},{1,17},{2,18},{3,19},{4,20},{5,21},{6,22},{7,23},{8,24},{9,... | collective-permute-start | bytes 1179656 | tf_op jit(solution)/shard_map/ppermute | solution.py:245
  347.7 19.3 %collective-permute-start.87 = (f32[16,768]{1,0:T(8,128)S(1)}, f32[16,768]{1,0:T(8,128)S(1)}, u32[]{:S(2)}, u32[]{:S(2)}) collective-permute-start(f32[16,768]{1,0:T(8,128)S(1)} %dynamic_update_slice.3), channel_id=1, source_target_pairs={{0,16},{16,0},{1,17},{17,1},{2,18},{18,2},{3,19},{19,3},{4,20},{20... | collective-permute-start | bytes 147464 | tf_op jit(solution)/shard_map/ppermute | solution.py:37
  347.8 23.9 %collective-permute-start.86 = (bf16[8,192,768]{2,1,0:T(8,128)(2,1)}, bf16[8,192,768]{2,1,0:T(8,128)(2,1)S(1)}, u32[]{:S(2)}, u32[]{:S(2)}) collective-permute-start(bf16[8,192,768]{2,1,0:T(8,128)(2,1)} %copy-done.105), channel_id=1, source_target_pairs={{0,1},{1,0},{2,3},{3,2},{4,5},{5,4},{6,7},{7,6},{8,9},{9,8},{10,11... | collective-permute-start | bytes 7077896 | tf_op jit(solution)/shard_map/ppermute | solution.py:37
  353.8 17.0 %collective-permute-start.85 = (bf16[2,192,768]{2,1,0:T(8,128)(2,1)S(1)}, bf16[2,192,768]{2,1,0:T(8,128)(2,1)S(1)}, u32[]{:S(2)}, u32[]{:S(2)}) collective-permute-start(bf16[2,192,768]{2,1,0:T(8,128)(2,1)S(1)} %fold.31), channel_id=1, source_target_pairs={{0,4},{1,3},{4,8},{5,1},{8,12},{9,5},{12,14},{13,9},{14,10},{15,13... | collective-permute-start | bytes 1769480 | tf_op jit(solution)/shard_map/ppermute | solution.py:52
  400.4 16.9 %collective-permute-start.98 = (bf16[2,192,768]{2,1,0:T(8,128)(2,1)S(1)}, bf16[2,192,768]{2,1,0:T(8,128)(2,1)S(1)}, u32[]{:S(2)}, u32[]{:S(2)}) collective-permute-start(bf16[2,192,768]{2,1,0:T(8,128)(2,1)S(1)} %fold.35), channel_id=1, source_target_pairs={{0,4},{1,3},{4,8},{5,1},{8,12},{9,5},{12,14},{13,9},{14,10},{15,13... | collective-permute-start | bytes 1769480 | tf_op jit(solution)/shard_map/ppermute | solution.py:52
  421.5 18.6 %collective-permute-start.102 = (bf16[2,192,768]{2,1,0:T(8,128)(2,1)S(1)}, bf16[2,192,768]{2,1,0:T(8,128)(2,1)S(1)}, u32[]{:S(2)}, u32[]{:S(2)}) collective-permute-start(bf16[2,192,768]{2,1,0:T(8,128)(2,1)S(1)} %fold.38), channel_id=1, source_target_pairs={{0,4},{1,3},{4,8},{5,1},{8,12},{9,5},{12,14},{13,9},{14,10},{15,13... | collective-permute-start | bytes 1769480 | tf_op jit(solution)/shard_map/ppermute | solution.py:52
  449.0 33.9 %collective-permute-start.111 = (bf16[8,192,768]{2,1,0:T(8,128)(2,1)S(1)}, bf16[8,192,768]{2,1,0:T(8,128)(2,1)S(1)}, u32[]{:S(2)}, u32[]{:S(2)}) collective-permute-start(bf16[8,192,768]{2,1,0:T(8,128)(2,1)S(1)} %get-tuple-element.447), channel_id=1, source_target_pairs={{0,1},{1,0},{2,3},{3,2},{4,5},{5,4},{6,7},{7,6},{8,9},{9,8},{10,11... | collective-permute-start | bytes 7077896 | tf_op jit(solution)/shard_map/ppermute | solution.py:37
  466.4 16.5 %collective-permute-start.110 = (bf16[2,192,768]{2,1,0:T(8,128)(2,1)S(1)}, bf16[2,192,768]{2,1,0:T(8,128)(2,1)S(1)}, u32[]{:S(2)}, u32[]{:S(2)}) collective-permute-start(bf16[2,192,768]{2,1,0:T(8,128)(2,1)S(1)} %fold.43), channel_id=1, source_target_pairs={{0,4},{1,3},{4,8},{5,1},{8,12},{9,5},{12,14},{13,9},{14,10},{15,13... | collective-permute-start | bytes 1769480 | tf_op jit(solution)/shard_map/ppermute | solution.py:52
  482.9 19.8 %collective-permute-start.114 = (bf16[2,192,768]{2,1,0:T(8,128)(2,1)S(1)}, bf16[2,192,768]{2,1,0:T(8,128)(2,1)S(1)}, u32[]{:S(2)}, u32[]{:S(2)}) collective-permute-start(bf16[2,192,768]{2,1,0:T(8,128)(2,1)S(1)} %collective-permute-done.110.refs_2_), channel_id=1, source_target_pairs={{0,1},{1,0},{2,3},{3,2},{4,5},{5,4},{6,7},{7,6},{8,9},{9,8},{10,11... | collective-permute-start | bytes 1769480 | tf_op jit(solution)/shard_map/ppermute | solution.py:37
  (277 other events, 2709.4 us)

commit v3 on v0

v3 whole, which is shorter than its diff:
```python
from functools import partial

import jax
import jax.numpy as jnp
from jax import lax
from jax.experimental import pallas as pl
from jax.experimental.pallas import tpu as pltpu
from jax.sharding import PartitionSpec as P

D = 768
HEADS = 12
HEAD = 64
SEQ = 512
MICRO = 2
FF = 3072

bf16 = jnp.bfloat16
f32 = jnp.float32
highest = lax.Precision.HIGHEST
norm_eps = 1e-05
unit_eps = 1e-06
masked_value = -1000000000.0
contrast_scale = 10.0
vmem_limit = 16 * 2**20
slot_vmem = 36 * 2**20


def params(size=vmem_limit):
    return pltpu.CompilerParams(vmem_limit_bytes=size)


def cost(flops, size):
    return pl.CostEstimate(flops=int(10 * flops), bytes_accessed=int(10 * size), transcendentals=0)


def swapped(value, axis, mask):
    count = lax.axis_size(axis)
    return lax.ppermute(value, axis, [(i, i ^ mask) for i in range(count)])


def ring_order(chips):
    return list(range(0, chips, 2)) + list(range(chips - 1, 0, -2))


def ring_hop(value, backward=False):
    chips = lax.axis_size("dp") // 2
    order = ring_order(chips)
    pairs = []
    for place in range(chips):
        for core in range(2):
            step = 1 if core == 0 else -1
            pairs.append((order[place] * 2 + core, order[(place + step) % chips] * 2 + core))
    return lax.ppermute(value, "dp", pairs)


def ring_place(me):
    chips = lax.axis_size("dp") // 2
    order = ring_order(chips)
    places = [order.index(chip) for chip in range(chips)]
    place = jnp.asarray(places, jnp.int32)[me // 2]
    core = me % 2
    return place, 1 - 2 * core, core


def owners(me, steps, cores):
    chips = lax.axis_size("dp") // 2
    place, way, core = ring_place(me)
    order = jnp.asarray(ring_order(chips), jnp.int32)
    found = order[(place + way * jnp.asarray(steps, jnp.int32)) % chips] * 2
    return found + (core + jnp.asarray(cores, jnp.int32)) % 2


def fast_ring():
    return lax.axis_size("dp") == 16


def gather_owners(me):
    steps = [0, 0, -1, -1, -2, -2, -3, -3, -4, 1, 1, 2, 2, 3, 3, 4]
    cores = [0, 1, 0, 1, 0, 1, 0, 1, 0, 1, 0, 1, 0, 1, 0, 1]
    return owners(me, steps, cores)


def assemble_kernel(counts, owner_ref, *refs):
    pieces, out_ref, sems = refs[: len(counts)], refs[-2], refs[-1]
    rows = pieces[0].shape[2]
    copies = []
    for piece, count in zip(pieces, counts):
        for k in range(count):
            start = pl.multiple_of(owner_ref[len(copies)] * rows, 16)
            copies.append(
                pltpu.make_async_copy(
                    piece.at[k], out_ref.at[:, pl.ds(start, rows), :], sems.at[len(copies)]
                )
            )
    for copy in copies:
        copy.start()
    for copy in copies:
        copy.wait()


def assemble(pieces, owner):
    counts = [piece.shape[0] for piece in pieces]
    total = sum(counts)
    blocks, rows = pieces[0].shape[1:3]
    return pl.pallas_call(
        partial(assemble_kernel, counts),
        out_shape=jax.ShapeDtypeStruct((blocks, total * rows, D), bf16),
        in_specs=[pl.BlockSpec(memory_space=pltpu.SMEM)]
        + [pl.BlockSpec(memory_space=pl.ANY)] * len(pieces),
        out_specs=pl.BlockSpec(memory_space=pltpu.VMEM),
        scratch_shapes=[pltpu.SemaphoreType.DMA((total,))],
        compiler_params=params(),
        cost_estimate=cost(0, 1e7),
        name="assemble",
    )(owner, *[pltpu.with_memory_space_constraint(piece, pltpu.HBM) for piece in pieces])


unit_steps = [1, 1, 2, 2, 3, 3, 4, 0]


def slots(me):
    if not fast_ring():
        return jnp.arange(16, dtype=jnp.int32)
    both = jnp.arange(6, dtype=jnp.int32) % 2
    keep = owners(me, unit_steps, [0] * 8)
    send = owners(me, [-step for step in unit_steps], [1] * 8)
    table = [keep[:6] // 2 * 2 + both, keep[6:], send[:6] // 2 * 2 + both, send[6:]]
    table = jnp.concatenate(table)
    index = jnp.arange(16, dtype=jnp.int32)
    return jnp.sum(jnp.where(table[None, :] == index[:, None], index[None, :], 0), axis=1)


def fold_first_kernel(keep_ref, mate_ref, out_ref, own_ref):
    total = keep_ref[...].astype(f32) + mate_ref[...].astype(f32)
    out_ref[...] = total[:1].astype(bf16)
    own_ref[...] = total[1]


def fold_first(keep, mate):
    rows, width = keep.shape[1:]
    tile = rows // 2
    units = pl.BlockSpec((2, tile, width), lambda i: (3, i, 0))
    return pl.pallas_call(
        fold_first_kernel,
        grid=(2,),
        in_specs=[units, units],
        out_specs=[
            pl.BlockSpec((1, tile, width), lambda i: (0, i, 0)),
            pl.BlockSpec((tile, width), lambda i: (i, 0)),
        ],
        out_shape=[
            jax.ShapeDtypeStruct((1, rows, width), bf16),
            jax.ShapeDtypeStruct((rows, width), f32),
        ],
        compiler_params=params(),
        cost_estimate=cost(0, 0),
        name="fold_first",
    )(keep, mate)


def fold_kernel(one, core_ref, keep_ref, mate_ref, there_ref, out_ref):
    there = there_ref[...].astype(f32)
    if one:
        there = jnp.where(pl.program_id(0) == core_ref[0], there, 0.0)
    total = keep_ref[...].astype(f32) + mate_ref[...].astype(f32) + there
    out_ref[...] = total.astype(bf16)


def fold(core, keep, mate, first, there):
    rows, width = keep.shape[1:]
    one = there.shape[0] == 1
    unit = pl.BlockSpec((1, rows, width), lambda i, _: (first + i, 0, 0))
    out = pl.BlockSpec((1, rows, width), lambda i, _: (i, 0, 0))
    arrived = pl.BlockSpec((1, rows, width), lambda i, _: (0, 0, 0)) if one else out
    return pl.pallas_call(
        partial(fold_kernel, one),
        grid_spec=pltpu.PrefetchScalarGridSpec(
            num_scalar_prefetch=1, grid=(2,), in_specs=[unit, unit, arrived], out_specs=out
        ),
        out_shape=jax.ShapeDtypeStruct((2, rows, width), bf16),
        compiler_params=params(),
        cost_estimate=cost(0, 0),
        name="fold",
    )(core, keep, mate, there)


class Reduction:
    def __init__(self, core, keep, send):
        self.core, self.keep, self.send = core, keep, send
        self.moving = [swapped(send, "dp", 1)] if fast_ring() else []
        self.stage = 0

    def step(self):
        arrived = self.moving[0]
        if self.stage == 0:
            self.mate = arrived
            first, self.own = fold_first(self.keep, self.mate)
            self.moving = [ring_hop(first)]
        elif self.stage < 4:
            first = 6 - 2 * self.stage
            self.moving = [ring_hop(fold(self.core, self.keep, self.mate, first, arrived))]
        elif self.stage == 4:
            self.near = arrived
            self.moving = [swapped(self.near, "dp", 1)]
        else:
            self.last = arrived
            self.moving = []
        self.stage += 1

    def value(self):
        def mine(pair):
            return lax.dynamic_index_in_dim(pair, self.core[0], 0, keepdims=False).astype(f32)

        return self.own + mine(self.near) + mine(self.last)


class Sent:
    def __init__(self, value, pairs):
        self.moving = [lax.ppermute(value, "section", pairs)]

    def step(self):
        self.arrived = self.moving[0]
        self.moving = []

    def value(self):
        return self.arrived


class Near:
    def __init__(self, value):
        self.value, self.mask = value, lax.axis_size("dp") // 2
        self.send()

    def send(self):
        self.moving = [swapped(self.value, "dp", self.mask)] if self.mask else []

    def step(self):
        self.value = jnp.concatenate([self.value, self.moving[0]])
        self.mask //= 2
        self.send()


class Sum:
    def __init__(self, value):
        self.value, self.mask = value, lax.axis_size("dp") // 2
        self.send()

    def send(self):
        self.moving = [swapped(self.value, "dp", self.mask)] if self.mask else []

    def step(self):
        self.value = self.value + self.moving[0]
        self.mask //= 2
        self.send()


class Swapped:
    def __init__(self, value):
        self.own, self.moving = value, [swapped(value, "section", 1)]

    def step(self):
        self.both = self.own + self.moving[0]
        self.moving = []


class Gather:
    def __init__(self, shard):
        self.pieces, self.mates = [shard], []
        self.moving = [swapped(shard, "dp", 1)]
        self.stage = 0

    def step(self):
        if self.stage == 0:
            self.pieces = [jnp.stack([self.pieces[0], self.moving[0]])]
            self.moving = [ring_hop(self.pieces[0])]
        elif self.stage < 5:
            self.pieces.append(self.moving[0])
            self.mates += self.moving[1:]
            self.moving = [swapped(self.pieces[-1], "dp", 1)]
            if self.stage < 4:
                last = self.pieces[-1] if self.stage < 3 else self.pieces[-1][:1]
                self.moving = [ring_hop(last)] + self.moving
        else:
            self.mates += self.moving
            self.moving = []
        self.stage += 1

    def all(self):
        return self.pieces + self.mates


class Order:
    def __init__(self, start):
        self.token = start

    def onward(self, items, values=()):
        for item in items:
            if item.moving:
                item.moving, self.token = lax.optimization_barrier((item.moving, self.token))
                item.step()
        values, self.token = lax.optimization_barrier((values, self.token))
        return values


def tie(values, *others):
    return lax.optimization_barrier((values, others))[0]


def add_up(value, axis):
    mask = 1
    while mask < lax.axis_size(axis):
        value = value + swapped(value, axis, mask)
        mask *= 2
    return value


def mm(a, b):
    return lax.dot_general(a, b, (((1,), (0,)), ((), ())), preferred_element_type=f32)


def mm_nt(a, b):
    return lax.dot_general(a, b, (((1,), (1,)), ((), ())), preferred_element_type=f32)


def mm_tn(a, b):
    return lax.dot_general(a, b, (((0,), (0,)), ((), ())), preferred_element_type=f32)


def full(shape):
    return pl.BlockSpec(shape, lambda i, *_: (0,) * len(shape))


def sds(shape, dtype):
    return jax.ShapeDtypeStruct(shape, dtype)


def far(shape, dtype):
    return pltpu.HBM(shape, dtype)


group = 256
groups = D // group
product = 2 * SEQ * D * D
token_block = (SEQ, D)
table_rows = 12
loss_row = 12
entries = MICRO + 1
everything = pl.BlockSpec(memory_space=pl.ANY)


def far(shape, dtype):
    return pltpu.HBM(shape, dtype)


def tokens_buffer(width, dtype):
    return far((entries, SEQ, width), dtype)


def busy(i, m):
    return jnp.where(m[0] < MICRO, i, 0)


def at_entry(block, *where):
    place = where[0] if where else (lambda i: (0,) * len(block))
    return pl.BlockSpec((None, *block), lambda i, m: (m[0], *place(busy(i, m))))


def at_micro(block):
    return pl.BlockSpec((None, *block), lambda i, m: (jnp.minimum(m[0], MICRO - 1),) + (0,) * len(block))


def column_sum(value):
    return jnp.sum(value, axis=0, keepdims=True)


class Slot:
    def __init__(self, entry, ahead=False):
        self.entry, self.ahead = entry, ahead


def in_place(value):
    if value.ndim > 2 and value.shape[0] in (MICRO, entries):
        return pltpu.with_memory_space_constraint(value, pltpu.HBM)
    return value


def slot_call(kernel, m, grid, ins, in_specs, outs, out_specs, before, scratch, size, name, kept=None):
    first = len(outs) - len(before)
    aliases = {1 + len(ins) + n: first + n for n in range(len(before))}
    if kept is not None:
        aliases[1 + kept[0]] = kept[1]
    return pl.pallas_call(
        kernel,
        grid_spec=pltpu.PrefetchScalarGridSpec(
            num_scalar_prefetch=1,
            grid=(grid,),
            in_specs=in_specs + [everything] * len(before),
            out_specs=out_specs,
            scratch_shapes=scratch,
        ),
        out_shape=outs,
        input_output_aliases=aliases,
        compiler_params=params(slot_vmem),
        cost_estimate=cost(0, 0) if m.ahead else cost(size * product, 3e7),
        name=name,
    )(m.entry, *[in_place(value) for value in ins], *[in_place(value) for value in before])


def attend_kernel(n_before, m_ref, *refs):
    x_ref, wq_ref, wk_ref, wv_ref, vec_ref, seg_col_ref, seg_row_ref, *refs = refs
    q_ref, k_ref, v_ref, mixed_ref, lse_ref, mask_ref = refs[n_before:]
    i = pl.program_id(0)

    @pl.when(m_ref[0] < MICRO)
    def _():
        @pl.when(i == 0)
        def _():
            mask_ref[...] = jnp.where(seg_col_ref[...] == seg_row_ref[...], 0.0, masked_value)

        lanes = pl.ds(pl.multiple_of(i * group, group), group)
        x = x_ref[...]
        q = (mm(x, wq_ref[...]) + vec_ref[2:3, lanes]).astype(bf16)
        k = mm(x, wk_ref[...]).astype(bf16)
        v = (mm(x, wv_ref[...]) + vec_ref[3:4, lanes]).astype(bf16)
        q_ref[...] = q
        k_ref[...] = k
        v_ref[...] = v
        scaled = q * jnp.asarray(HEAD**-0.5, bf16)
        outs, lses = [], []
        for h in range(group // HEAD):
            c = slice(h * HEAD, (h + 1) * HEAD)
            scores = mm_nt(scaled[:, c], k[:, c]) + mask_ref[...]
            top = jnp.max(scores, axis=1, keepdims=True)
            raw = jnp.exp(scores - top)
            total = jnp.sum(raw, axis=1, keepdims=True)
            outs.append(mm(raw.astype(bf16), v[:, c]) / total)
            lses.append(top + jnp.log(total))
        mixed_ref[...] = jnp.concatenate(outs, axis=1).astype(bf16)
        lse_ref[...] = jnp.concatenate(lses + [jnp.zeros((SEQ, 128 - len(lses)), f32)], axis=1)


vec_spec = full((table_rows, D))


def attend(m, x, w_in, vec, seg_col, seg_row, before):
    def weight(b):
        return pl.BlockSpec((None, D, group), lambda i, m: (b, 0, busy(i, m)))

    heads = at_entry((SEQ, group), lambda i: (0, i))
    return slot_call(
        partial(attend_kernel, len(before)),
        m,
        groups,
        [x, w_in, w_in, w_in, vec, seg_col, seg_row],
        [full(token_block)]
        + [weight(b) for b in range(3)]
        + [vec_spec, at_entry((SEQ, 1)), at_entry((1, SEQ))],
        [tokens_buffer(D, bf16)] * 4 + [far((entries, groups, SEQ, 128), f32)],
        [heads] * 4 + [at_entry((None, SEQ, 128), lambda i: (i, 0, 0))],
        before,
        [pltpu.VMEM((SEQ, SEQ), f32)],
        5,
        "attend",
    )


def normalize(hidden):
    centered = hidden - jnp.mean(hidden, axis=1, keepdims=True)
    variance = jnp.mean(centered * centered, axis=1, keepdims=True)
    rstd = lax.rsqrt(variance + norm_eps)
    return centered * rstd, rstd


def gelu_both(x):
    cdf = 0.5 + 0.5 * lax.erf(x * 0.7071067811865476)
    return x * cdf, cdf + x * (jnp.exp(x * x * -0.5) * 0.3989422804014327)


def forward_kernel(last, n_before, m_ref, mixed_ref, x_ref, wo_ref, wi_ref, wf_ref, vec_ref, *refs):
    seg_row_ref, *refs = refs
    refs = refs[n_before:]
    if last:
        pooled_ref, unit_ref, *refs = refs
    else:
        out_ref, *refs = refs
    xhat1_ref, rstd1_ref, gelu_ref, dgelu_ref, state_ref, xhat2_ref, rstd2_ref, *refs = refs
    normed_ref, acc_ref = refs
    i = pl.program_id(0)

    @pl.when(m_ref[0] < MICRO)
    def _():
        @pl.when(i == 0)
        def _():
            attended = mm(mixed_ref[...], wo_ref[...]) + vec_ref[4:5, :]
            xhat, rstd = normalize(x_ref[...].astype(f32) + attended)
            xhat1_ref[...] = xhat.astype(bf16)
            rstd1_ref[...] = rstd
            normed = xhat * vec_ref[0:1, :] + vec_ref[5:6, :]
            normed_ref[...] = normed.astype(bf16)
            acc_ref[...] = normed + vec_ref[6:7, :]

        pre_act = mm(normed_ref[...], wi_ref[...]) + vec_ref[pl.ds(8 + i, 1), :]
        value, slope = gelu_both(pre_act)
        value = value.astype(bf16)
        gelu_ref[...] = value
        dgelu_ref[...] = slope.astype(bf16)
        acc_ref[...] += mm(value, wf_ref[...])

        @pl.when(i == pl.num_programs(0) - 1)
        def _():
            xhat, rstd = normalize(acc_ref[...])
            xhat2_ref[...] = xhat.astype(bf16)
            rstd2_ref[...] = rstd
            out = xhat * vec_ref[1:2, :] + vec_ref[7:8, :]
            state_ref[...] = out.astype(bf16)
            if not last:
                out_ref[...] = out.astype(bf16)
            else:
                member = seg_row_ref[...] == lax.broadcasted_iota(jnp.int32, (8, SEQ), 0)
                count = jnp.sum(member.astype(f32), axis=1, keepdims=True)
                member = member.astype(bf16)
                high = out.astype(bf16)
                rest = out - high.astype(f32)
                middle = rest.astype(bf16)
                low = (rest - middle.astype(f32)).astype(bf16)
                pooled = mm(member, high) + mm(member, middle) + mm(member, low)
                pooled = pooled / jnp.maximum(count, 1.0)
                pooled_ref[...] = pooled
                norm = jnp.sum(pooled * pooled, axis=1, keepdims=True) + unit_eps
                unit_ref[...] = pooled * lax.rsqrt(norm)

    if last:

        @pl.when(m_ref[0] >= MICRO)
        def _():
            pooled_ref[...] = jnp.zeros((8, D), f32)
            unit_ref[...] = jnp.zeros((8, D), f32)


def forward(m, mixed, x, w_wide, w_narrow, vec, seg_row, last, before):
    part = at_entry(token_block, lambda i: (0, i))
    now = [sds((8, D), f32)] * 2 if last else [sds(token_block, bf16)]
    row = sds((entries, SEQ, 1), f32)
    outs = now + [tokens_buffer(D, bf16), row] + [tokens_buffer(FF, bf16)] * 2
    outs += [tokens_buffer(D, bf16), tokens_buffer(D, bf16), row]
    return slot_call(
        partial(forward_kernel, last, len(before)),
        m,
        FF // D,
        [mixed, x, w_wide, w_wide, w_narrow, vec, seg_row],
        [
            at_entry(token_block),
            full(token_block),
            pl.BlockSpec((None, D, D), lambda i, m: (0, 0, 0)),
            pl.BlockSpec((None, D, D), lambda i, m: (1 + busy(i, m), 0, 0)),
            pl.BlockSpec((None, D, D), lambda i, m: (0, busy(i, m), 0)),
            vec_spec,
            at_entry((1, SEQ)),
        ],
        outs,
        [full(out.shape) for out in now]
        + [at_entry(token_block), at_entry((SEQ, 1)), part, part]
        + [at_entry(token_block), at_entry(token_block), at_entry((SEQ, 1))],
        before,
        [pltpu.VMEM(token_block, bf16), pltpu.VMEM(token_block, f32)],
        9,
        "forward",
    )


def contrast_kernel(me_ref, table_ref, pooled_ref, groups_ref, partner_ref, seg_row_ref, *refs, micro, total):
    loss_ref, gseg_ref = refs
    me = me_ref[0]
    dot = partial(lax.dot_general, precision=highest, preferred_element_type=f32)
    rows_nt = (((1,), (1,)), ((), ()))
    table = table_ref[...].reshape(-1, D)
    count = table.shape[0]
    devices = count // 8
    every = groups_ref.shape[1]
    segs = every // devices

    def sentence(shape, axis):
        index = lax.broadcasted_iota(jnp.int32, shape, axis)
        block, place = index >> 3, index & 7
        owner = jnp.zeros_like(block)
        far_one = devices // 2
        bit = 0
        while far_one >= 1:
            owner = owner | ((block >> bit) & 1) * far_one
            bit += 1
            far_one //= 2
        return jnp.where(place < segs, (owner ^ me) * segs + place, -1)

    ids_row, ids_col = sentence((1, count), 1), sentence((count, 1), 0)
    ids = groups_ref[micro : micro + 1, :].astype(f32)
    ids = jnp.broadcast_to(ids, (8, every))
    hot_row = (lax.broadcasted_iota(jnp.int32, (every, 1), 0) == ids_row).astype(f32)
    hot_col = (lax.broadcasted_iota(jnp.int32, (1, every), 1) == ids_col).astype(f32)
    groups_row = dot(ids, hot_row, (((1,), (0,)), ((), ())))[0:1]
    groups_col = dot(hot_col, ids, rows_nt)[:, 0:1]
    logits = contrast_scale * dot(table, table, rows_nt)
    real = (ids_row >= 0) & (ids_col >= 0)
    allowed = real & (groups_col == groups_row) & (ids_col != ids_row)
    masked = jnp.where(allowed, logits, masked_value)
    top = jnp.max(masked, axis=0, keepdims=True)
    lse_row = top + jnp.log(column_sum(jnp.exp(masked - top)))
    mine = masked[:8]
    top = jnp.max(mine, axis=1, keepdims=True)
    raw = jnp.exp(mine - top)
    raw_total = jnp.sum(raw, axis=1, keepdims=True)
    across = jnp.exp(mine - lse_row)
    place = lax.broadcasted_iota(jnp.int32, (8, 1), 0)
    partner = jnp.zeros((8, 1), jnp.int32)
    for s in range(segs):
        partner = jnp.where(place == s, partner_ref[micro, s], partner)
    chosen = ((partner == ids_row) & (place < segs)).astype(f32)
    terms = top + jnp.log(raw_total) - jnp.sum(chosen * logits[:8], axis=1, keepdims=True)
    loss = column_sum(jnp.where(place < segs, terms, 0.0)) / total
    loss_ref[...] = jnp.broadcast_to(loss, (1, D))
    grad = raw / raw_total + across - 2.0 * chosen
    grad = contrast_scale * dot(grad, table, (((1,), (0,)), ((), ())))
    pooled = pooled_ref[...]
    scale = lax.rsqrt(jnp.sum(pooled * pooled, axis=1, keepdims=True) + unit_eps)
    dots = jnp.sum(grad * pooled, axis=1, keepdims=True)
    grad = scale * grad - pooled * (scale * scale * scale * dots)
    member = (seg_row_ref[...] == lax.broadcasted_iota(jnp.int32, (8, SEQ), 0)).astype(f32)
    gseg_ref[...] = grad / jnp.maximum(jnp.sum(member, axis=1, keepdims=True), 1.0)


def contrast(me, table, pooled, group_ids, partner, seg_row, micro, total):
    smem = pl.BlockSpec(memory_space=pltpu.SMEM)
    return pl.pallas_call(
        partial(contrast_kernel, micro=micro, total=total),
        grid=(1,),
        out_shape=[sds((1, D), f32), sds((8, D), f32)],
        in_specs=[
            smem,
            full(table.shape),
            full((8, D)),
            full(group_ids.shape),
            smem,
            pl.BlockSpec((None, 1, SEQ), lambda i: (micro, 0, 0)),
        ],
        out_specs=[full((1, D)), full((8, D))],
        compiler_params=params(slot_vmem),
        name="contrast",
    )(me, table, pooled, group_ids, partner, seg_row)


def norm_back(grad, xhat, rstd, gain):
    scaled = grad * gain
    mean = jnp.mean(scaled, axis=1, keepdims=True)
    along = jnp.mean(scaled * xhat, axis=1, keepdims=True)
    return rstd * (scaled - mean - xhat * along)


def ff_back_kernel(last, n_before, m_ref, cot_ref, *refs):
    if last:
        seg_col_ref, gseg_ref, loss_ref, *refs = refs
    xhat2_ref, rstd2_ref, vec_ref, wf_ref, dgelu_ref, wi_ref, xhat1_ref, rstd1_ref, *refs = refs
    wo_ref, small_in_ref, *refs = refs
    ghid_ref, gmixed_ref, small_ref, gbranch_ref, gpre_ref, gatt_ref, acc_ref = refs[n_before:]
    i = pl.program_id(0)

    @pl.when(i == 0)
    def _():
        small_ref[...] = small_in_ref[...]

    @pl.when(m_ref[0] < MICRO)
    def _():
        @pl.when(i == 0)
        def _():
            grad = cot_ref[...].astype(f32)
            if last:
                for s in range(4):
                    grad = grad + jnp.where(seg_col_ref[...] == s, gseg_ref[s : s + 1, :], 0.0)
            xhat = xhat2_ref[...].astype(f32)
            grad_sum = norm_back(grad, xhat, rstd2_ref[...], vec_ref[1:2, :])
            acc_ref[...] = grad_sum
            low = grad_sum.astype(bf16)
            gbranch_ref[...] = low
            if last:
                small_ref[loss_row : loss_row + 1, :] += loss_ref[...]
            small_ref[1:2, :] += column_sum(grad * xhat)
            small_ref[6:7, :] += column_sum(low.astype(f32))
            small_ref[7:8, :] += column_sum(grad)

        grad_gelu = mm_nt(gbranch_ref[...], wf_ref[...])
        grad_pre = (grad_gelu * dgelu_ref[...].astype(f32)).astype(bf16)
        gpre_ref[...] = grad_pre
        small_ref[pl.ds(8 + i, 1), :] += column_sum(grad_pre.astype(f32))
        acc_ref[...] += mm_nt(grad_pre, wi_ref[...])

        @pl.when(i == pl.num_programs(0) - 1)
        def _():
            grad = acc_ref[...]
            xhat = xhat1_ref[...].astype(f32)
            grad_hidden = norm_back(grad, xhat, rstd1_ref[...], vec_ref[0:1, :])
            ghid_ref[...] = grad_hidden
            low = grad_hidden.astype(bf16)
            gatt_ref[...] = low
            gmixed_ref[...] = mm_nt(low, wo_ref[...]).astype(bf16)
            small_ref[0:1, :] += column_sum(grad * xhat)
            small_ref[4:5, :] += column_sum(low.astype(f32))
            small_ref[5:6, :] += column_sum(grad)


def ff_back(m, cot, segs, xhat2, rstd2, vec, w_narrow, dgelu, w_wide, xhat1, rstd1, small, before):
    last = len(segs) > 0
    part = at_entry(token_block, lambda i: (0, i))
    return slot_call(
        partial(ff_back_kernel, last, len(before)),
        m,
        FF // D,
        [cot, *segs, xhat2, rstd2, vec, w_narrow, dgelu, w_wide, xhat1, rstd1, w_wide, small],
        (
            [at_micro(token_block), at_entry((SEQ, 1)), full((8, D)), full((1, D))]
            if last
            else [full(token_block)]
        )
        + [
            at_entry(token_block),
            at_entry((SEQ, 1)),
            vec_spec,
            pl.BlockSpec((None, D, D), lambda i, m: (0, busy(i, m), 0)),
            part,
            pl.BlockSpec((None, D, D), lambda i, m: (1 + busy(i, m), 0, 0)),
            at_entry(token_block),
            at_entry((SEQ, 1)),
            pl.BlockSpec((None, D, D), lambda i, m: (0, 0, 0)),
            full((16, D)),
        ],
        [sds(token_block, f32), sds(token_block, bf16), sds((16, D), f32)]
        + [tokens_buffer(D, bf16), tokens_buffer(FF, bf16), far((entries, 4, SEQ, D), bf16)],
        [full(token_block), full(token_block), full((16, D))]
        + [at_entry(token_block), part, at_entry((None, SEQ, D), lambda i: (3, 0, 0))],
        before,
        [pltpu.VMEM(token_block, f32)],
        12,
        "ff_back",
    )


def attend_back_kernel(first, n_total, n_before, m_ref, *refs):
    q_ref, k_ref, v_ref, gm_ref, lse_ref, wq_ref, wk_ref, wv_ref, *refs = refs
    totals, refs = refs[:n_total], refs[n_total:]
    seg_col_ref, seg_row_ref, small_in_ref, *refs = refs
    low_ref, small_ref, gx_ref, gqkv_ref, mask_ref = refs[n_before:]
    i = pl.program_id(0)
    active = m_ref[0] < MICRO

    @pl.when(i == 0)
    def _():
        small_ref[...] = small_in_ref[...]

    @pl.when((i == 0) & active)
    def _():
        mask_ref[...] = jnp.where(seg_col_ref[...] == seg_row_ref[...], 0.0, masked_value)
        gx_ref[...] = totals[0][...]

    @pl.when((i == 0) & jnp.logical_not(active))
    def _():
        gx_ref[...] = totals[-1][...]

    @pl.when(active)
    def _():
        q, k, v, gm = q_ref[...], k_ref[...], v_ref[...], gm_ref[...]
        scaled = q * jnp.asarray(HEAD**-0.5, bf16)
        lse = jnp.transpose(lse_ref[...])
        parts = [[], [], []]
        for h in range(group // HEAD):
            c = slice(h * HEAD, (h + 1) * HEAD)
            probs = jnp.exp(mm_nt(k[:, c], scaled[:, c]) + mask_ref[...] - lse[h : h + 1, :])
            grad_probs = mm_nt(v[:, c], gm[:, c])
            parts[2].append(mm(probs.astype(bf16), gm[:, c]))
            dots = column_sum(grad_probs * probs)
            grad_scores = (probs * (grad_probs - dots)).astype(bf16)
            parts[1].append(mm(grad_scores, scaled[:, c]))
            parts[0].append(mm_tn(grad_scores, k[:, c]) * HEAD**-0.5)
        grads = [jnp.concatenate(part, axis=1).astype(bf16) for part in parts]
        for b, grad in enumerate(grads):
            gqkv_ref[b] = grad
        lanes = pl.ds(pl.multiple_of((first + i) * group, group), group)
        small_ref[2:3, lanes] += column_sum(grads[0].astype(f32))
        small_ref[3:4, lanes] += column_sum(grads[2].astype(f32))
        gx_ref[...] += (
            mm_nt(grads[0], wq_ref[...]) + mm_nt(grads[1], wk_ref[...]) + mm_nt(grads[2], wv_ref[...])
        )

        @pl.when(i == pl.num_programs(0) - 1)
        def _():
            low_ref[...] = gx_ref[...].astype(bf16)


def attend_back(m, q, k, v, gm, lse, w_in, totals, seg_col, seg_row, small, first, count, before):
    def weight(b):
        return pl.BlockSpec((None, D, group), lambda i, m: (b, 0, first + busy(i, m)))

    heads = at_entry((SEQ, group), lambda i: (0, first + i))
    buffer = at_micro(token_block)
    total_specs = [buffer] if first else [full(token_block), buffer][: len(totals)]
    return slot_call(
        partial(attend_back_kernel, first, len(totals), len(before)),
        m,
        count,
        [q, k, v, gm, lse, w_in, w_in, w_in, *totals, seg_col, seg_row, small],
        [heads] * 3
        + [pl.BlockSpec((SEQ, group), lambda i, m: (0, first + busy(i, m)))]
        + [at_entry((None, SEQ, 128), lambda i: (first + i, 0, 0))]
        + [weight(b) for b in range(3)]
        + total_specs
        + [at_entry((SEQ, 1)), at_entry((1, SEQ)), full((16, D))],
        [sds(token_block, bf16), sds((16, D), f32)]
        + [far((MICRO, SEQ, D), f32), far((entries, 4, SEQ, D), bf16)],
        [full(token_block), full((16, D)), buffer]
        + [at_entry((3, SEQ, group), lambda i: (0, 0, first + i))],
        before,
        [pltpu.VMEM((SEQ, SEQ), f32)],
        6 * count,
        "attend_back",
        (7 + len(totals), 2) if first or len(totals) > 1 else None,
    )


def put(slot, keep_ref, send_ref, index, value):
    @pl.when(slot < 8)
    def _():
        keep_ref[(slot,) + index] = value

    @pl.when(slot >= 8)
    def _():
        send_ref[(slot - 8,) + index] = value


def weight_call(kernel, slot, ins, in_specs, scratch, name):
    outs = [sds((8, FF // 16, D), bf16)] * 2
    return pl.pallas_call(
        kernel,
        grid_spec=pltpu.PrefetchScalarGridSpec(
            num_scalar_prefetch=1,
            grid=(4,),
            in_specs=in_specs,
            out_specs=[full(out.shape) for out in outs],
            scratch_shapes=scratch,
        ),
        out_shape=outs,
        compiler_params=params(),
        cost_estimate=cost(8 * product, 3e7),
        name=name,
    )(slot, *[in_place(value) for value in ins])


def weight_out_kernel(slot_ref, gelu_ref, gbranch_ref, keep_ref, send_ref):
    i = pl.program_id(0)
    rows = FF // 16
    total = sum(mm_tn(gelu_ref[m], gbranch_ref[m]) for m in range(MICRO)).astype(bf16)
    for j in range(4):
        put(slot_ref[4 * i + j], keep_ref, send_ref, (), total[j * rows : (j + 1) * rows])


def weight_wide_kernel(slot_ref, xhat_ref, vec_ref, gpre_ref, keep_ref, send_ref, normed_ref):
    i = pl.program_id(0)
    rows = D // 16

    @pl.when(i == 0)
    def _():
        for m in range(MICRO):
            normed = (xhat_ref[m].astype(f32) * vec_ref[0:1, :] + vec_ref[5:6, :]).astype(bf16)
            normed_ref[:, m * SEQ : (m + 1) * SEQ] = jnp.transpose(normed)

    total = mm(normed_ref[...], gpre_ref[...].reshape(MICRO * SEQ, D)).astype(bf16)
    row = pl.multiple_of(rows * i, 16)
    for d in range(16):
        put(slot_ref[d], keep_ref, send_ref, (pl.ds(row, rows),), total[d * rows : (d + 1) * rows])


def weight_attn_kernel(slot_ref, x_ref, mixed_ref, grad_ref, keep_ref, send_ref, left_ref):
    i = pl.program_id(0)
    rows = D // 16

    def turn(ref):
        for m in range(MICRO):
            left_ref[:, m * SEQ : (m + 1) * SEQ] = jnp.transpose(ref[m])

    @pl.when(i == 0)
    def _():
        turn(x_ref)

    @pl.when(i == 3)
    def _():
        turn(mixed_ref)

    total = mm(left_ref[...], grad_ref[...].reshape(MICRO * SEQ, D)).astype(bf16)
    row = pl.multiple_of(rows * i, 16)
    for d in range(16):
        put(slot_ref[d], keep_ref, send_ref, (pl.ds(row, rows),), total[d * rows : (d + 1) * rows])


both_blocks = (MICRO, SEQ, D)
both_parts = pl.BlockSpec(both_blocks, lambda i, _: (0, 0, i))


def weight_out(slot, gelu, gbranch):
    specs = [both_parts, full(both_blocks)]
    return weight_call(weight_out_kernel, slot, [gelu, gbranch], specs, [], "weight_out")


def weight_wide(slot, xhat1, vec, gpre):
    specs = [full(both_blocks), vec_spec, both_parts]
    scratch = [pltpu.VMEM((D, MICRO * SEQ), bf16)]
    return weight_call(weight_wide_kernel, slot, [xhat1, vec, gpre], specs, scratch, "weight_wide")


def weight_attn(slot, x, mixed, grads):
    grad_spec = pl.BlockSpec((MICRO, None, SEQ, D), lambda i, _: (0, i, 0, 0))
    specs = [full(both_blocks), full(both_blocks), grad_spec]
    scratch = [pltpu.VMEM((D, MICRO * SEQ), bf16)]
    return weight_call(weight_attn_kernel, slot, [x, mixed, grads], specs, scratch, "weight_attn")


def blocked(shard):
    rows, columns = shard.shape
    return shard.reshape(rows, columns // D, D).transpose(1, 0, 2)


def unblocked(shard):
    blocks, rows, columns = shard.shape
    return shard.transpose(1, 0, 2).reshape(rows, blocks * columns)


def gather_plain(shard):
    return blocked(lax.all_gather(shard.astype(bf16), "dp", axis=0, tiled=True))


def local(
    tokens,
    out_cotangent,
    lengths,
    partner,
    group_ids,
    attn_in,
    attn_out,
    ff_in,
    ff_out,
    norm_gains,
    biases,
    ff_bias,
):
    section = lax.axis_index("section").astype(jnp.int32)
    me = lax.axis_index("dp").astype(jnp.int32)
    leading = section == 0
    n_dp = lax.axis_size("dp")
    rows_in = D // n_dp
    rows_out = FF // n_dp
    segs = lengths.shape[-1]

    vectors = jnp.concatenate(
        [norm_gains[0].reshape(-1), biases[0].reshape(-1), ff_bias[0].reshape(-1)]
    ).astype(bf16)

    def vector_table(every):
        rows = every[:, : 8 * rows_in].reshape(n_dp, 8, rows_in).transpose(1, 0, 2).reshape(8, D)
        return jnp.concatenate([rows, every[:, 8 * rows_in :].reshape(4, D)]).astype(f32)

    spare = jnp.int32(MICRO)

    def entry(micro, layer):
        return jnp.where(section == layer, jnp.int32(micro), spare)[None]

    def segment_forms(lengths):
        row_ends = jnp.cumsum(lengths[:, 0], axis=-1, dtype=jnp.int32)
        places = jnp.arange(SEQ, dtype=jnp.int32)
        segment = jnp.sum((places[None, :, None] >= row_ends[:, None, :]).astype(jnp.int32), axis=-1)
        segment = jnp.concatenate([segment, segment[:1]])
        return segment[:, :, None], segment[:, None, :]

    order = Order(lengths[0, 0, 0])
    onward = order.onward

    first = Slot(entry(0, 0))
    x = tokens[0, 0]
    if fast_ring():
        in_gather = Gather(blocked(attn_in[0].astype(bf16)))
        table = jnp.pad(vectors[None], ((0, 15), (0, D - vectors.shape[0])))
        vec_gather = Gather(table[None])
        onward([in_gather, vec_gather])
        onward([in_gather, vec_gather])
        late = tie((attn_out, ff_in, ff_out, lengths, me), in_gather.pieces[1])
        wide_shard = [late[0][0].astype(bf16)[None], blocked(late[1][0].astype(bf16))]
        wide_gather = Gather(jnp.concatenate(wide_shard))
        seg_col, seg_row = segment_forms(late[3])
        owner, slot = gather_owners(late[4]), slots(late[4])
        onward([in_gather, vec_gather])
        onward([wide_gather])
        onward([in_gather, vec_gather])
        narrow_gather = Gather(tie(late[2], in_gather.pieces[3])[0].astype(bf16)[None])
        onward([in_gather, vec_gather])
        onward([wide_gather])
        onward([narrow_gather])
        onward([in_gather, vec_gather])
        vec = assemble(vec_gather.all(), owner).reshape(n_dp, 16, D)
        vec = vector_table(vec[:, 0, : vectors.shape[0]])
        w_in = assemble(in_gather.all(), owner)
        heads = attend(first, x, w_in, vec, seg_col, seg_row, [])
        heads = onward([wide_gather, narrow_gather], heads)
        onward([wide_gather, narrow_gather])
        onward([wide_gather])
        onward([narrow_gather])
        onward([wide_gather])
        w_wide = assemble(wide_gather.all(), owner)
        onward([narrow_gather])
        onward([narrow_gather])
        w_narrow = assemble(narrow_gather.all(), owner)
    else:
        w_in = gather_plain(attn_in[0])
        w_wide = jnp.concatenate([gather_plain(attn_out[0]), gather_plain(ff_in[0])])
        w_narrow = gather_plain(ff_out[0])
        vec = vector_table(lax.all_gather(vectors, "dp"))
        seg_col, seg_row = segment_forms(lengths)
        slot = slots(me)
        heads = attend(first, x, w_in, vec, seg_col, seg_row, [])
    out, *stored = forward(first, heads[3], x, w_wide, w_narrow, vec, seg_row, False, [])
    pairs = [(0, 1)]
    sent0 = Sent(out, pairs)

    second = Slot(entry(1, 0), True)
    x = tokens[1, 0]
    heads = attend(second, x, w_in, vec, seg_col, seg_row, heads)
    out, *stored = forward(second, heads[3], x, w_wide, w_narrow, vec, seg_row, False, stored)
    heads, stored, out = onward([sent0], (heads, stored, out))
    sent1 = Sent(out, pairs)

    third = Slot(entry(0, 1), True)
    x = received0 = sent0.value()
    heads = attend(third, x, w_in, vec, seg_col, seg_row, heads)
    pooled0, unit0, *stored = forward(
        third, heads[3], x, w_wide, w_narrow, vec, seg_row, True, stored
    )
    near0 = Near(unit0)
    heads, stored = onward([sent1], (heads, stored))

    fourth = Slot(entry(1, 1))
    x = received1 = sent1.value()
    heads = attend(fourth, x, w_in, vec, seg_col, seg_row, heads)
    heads = onward([near0], heads)
    pooled1, unit1, *stored = forward(
        fourth, heads[3], x, w_wide, w_narrow, vec, seg_row, True, stored
    )
    q, k, v, mixed, lse = heads
    xhat1, rstd1, gelu, dgelu, states, xhat2, rstd2 = stored

    total = MICRO * n_dp * segs

    def contrasted(near, pooled, micro):
        while near.moving:
            onward([near])
        table = near.value.reshape(-1, D)
        loss, grad_segs = contrast(
            me[None], table, pooled, group_ids, partner, seg_row, micro, total
        )
        return seg_col, grad_segs, loss

    near1 = Near(unit1)
    segs0 = contrasted(near0, pooled0, 0)

    cots = out_cotangent[:, 0]
    grads = []
    hidden_grads = []
    small = jnp.zeros((16, D), f32)

    def ff_slot(m, cot, segs_in, small):
        grad_hidden, grad_mixed, small, *buffers = ff_back(
            m, cot, segs_in, xhat2, rstd2, vec, w_narrow, dgelu, w_wide, xhat1, rstd1, small, grads
        )
        return grad_hidden, grad_mixed, small, buffers

    def heads_slot(m, grad_hidden, grad_mixed, small, buffers, items, calls):
        total, all_grads = grad_hidden, buffers[2]
        for first, count in calls:
            low, small, total, all_grads = attend_back(
                m,
                *(q, k, v, grad_mixed, lse, w_in),
                [total] if first else [total] + hidden_grads,
                *(seg_col, seg_row, small, first, count, [all_grads]),
            )
            total, all_grads, low, small = onward(items(), (total, all_grads, low, small))
        return low, small, [total], [buffers[0], buffers[1], all_grads]

    all_heads = ((0, groups),)
    pairs = [(1, 0)]
    m = Slot(entry(0, 1))
    state = ff_slot(m, cots, segs0, small)
    state = onward([near1], state)
    two_calls = ((0, 2), (2, 1))
    low, small, hidden_grads, grads = heads_slot(m, *state, lambda: [near1], two_calls)
    sent0 = Sent(low, pairs)

    m = Slot(entry(1, 1), True)
    state = ff_slot(m, cots, contrasted(near1, pooled1, 1), small)
    low, small, hidden_grads, grads = heads_slot(m, *state, lambda: [sent0], all_heads)
    sent1 = Sent(low, pairs)

    m = Slot(entry(0, 0), True)
    state = ff_slot(m, sent0.value(), (), small)
    states_out, state = onward([], (states[None, :MICRO, None], state))
    low, small, hidden_grads, grads = heads_slot(m, *state, lambda: [sent1], all_heads)

    m = Slot(entry(1, 0))
    core = (me % 2)[None]
    running = []

    def reduction(chunk):
        running.append(Reduction(core, *chunk))
        return running[-1]

    *state, buffers = ff_slot(m, sent1.value(), (), small)
    chunk_out = weight_out(slot, gelu, buffers[0])
    reduced_out = reduction(chunk_out)
    chunk_wide = weight_wide(slot, xhat1, vec, buffers[1])
    state, buffers = onward(running, (state, buffers))
    reduced_wide = reduction(chunk_wide)
    one_by_one = [(first, 1) for first in range(groups)]
    low, small, hidden_grads, grads = heads_slot(m, *state, buffers, lambda: running, one_by_one)
    inputs = jnp.where(leading, tokens[:, 0], jnp.stack([received0, received1]))
    chunk_attn = weight_attn(slot, inputs, mixed, grads[2])
    reduced_attn = reduction(chunk_attn)
    small = Sum(small)
    running += [small]
    loss = None
    while True:
        if loss is None and not small.moving:
            loss = Swapped(small.value[loss_row : loss_row + 1, :128])
            running.append(loss)
        if not any(item.moving for item in running):
            break
        onward([reduced_attn])
        onward([item for item in running if item is not reduced_attn])

    if fast_ring():
        own_ff_out = reduced_out.value()
        own_ff_in = unblocked(reduced_wide.value().reshape(4, rows_in, D))
        own_attn = reduced_attn.value()
        own_attn_in = unblocked(own_attn[: 3 * rows_in].reshape(3, rows_in, D))
        own_attn_out = own_attn[3 * rows_in :]
    else:

        def natural(chunk, blocks):
            both = jnp.concatenate(chunk).reshape(16, blocks, -1, D)
            return both.transpose(1, 0, 2, 3).reshape(blocks, -1, D)

        attn = natural(chunk_attn, 4)
        whole = [unblocked(attn[:3]), attn[3], unblocked(natural(chunk_wide, 4))]
        whole.append(natural(chunk_out, 1)[0])
        own_attn_in, own_attn_out, own_ff_in, own_ff_out = (
            lax.psum_scatter(grad.astype(f32), "dp", scatter_dimension=0, tiled=True)
            for grad in whole
        )

    contrast_loss = jnp.where(order.token < 0, 0.0, loss.both[0, 0])
    small = small.value
    own_rows = lax.dynamic_slice(small, (0, me * rows_in), (8, rows_in))
    spot = me * rows_out
    own_bias = lax.dynamic_slice(small, (8 + spot // D, spot % D), (1, rows_out))
    return (
        contrast_loss,
        states_out,
        hidden_grads[0][None, :, None],
        own_attn_in[None],
        own_attn_out[None],
        own_ff_in[None],
        own_ff_out[None],
        own_rows[None, :2],
        own_rows[None, 2:],
        own_bias,
    )


def solution(mesh):
    return jax.shard_map(
        local,
        mesh=mesh,
        in_specs=(
            P(None, "dp", None, None),
            P(None, "dp", None, None),
            P(None, "dp", None),
            P(None, "dp"),
            P(),
            P("section", "dp", None),
            P("section", "dp", None),
            P("section", "dp", None),
            P("section", "dp", None),
            P("section", None, "dp"),
            P("section", None, "dp"),
            P("section", "dp"),
        ),
        out_specs=(
            P(),
            P("section", None, "dp", None, None),
            P("section", None, "dp", None, None),
            P("section", "dp", None),
            P("section", "dp", None),
            P("section", "dp", None),
            P("section", "dp", None),
            P("section", None, "dp"),
            P("section", None, "dp"),
            P("section", "dp"),
        ),
        check_vma=False,
    )
```

time: 1270 us -> 468 us (0.37)
  waiting for transfers between devices: 511 us -> 150 us
  matrix products: 359 us -> 0 us
  blocking collectives: 212 us -> 0 us
  Pallas kernels: 0 us -> 196 us
  other arithmetic: 88 us -> 18.9 us
  starting transfers between devices: 11.9 us -> 60.9 us
  local copies, waits for them, and re-layouts: 66.2 us -> 30.7 us
  between operations: 20.6 us -> 4.16 us
    dot_general x66 -> x0, matrix products: 359 us -> none  [the longest x3 48.4 us: layer_forward(): jnp.dot(normed.astype(jnp.bfloat16), ff_in, preferred_element_type=jnp.fl...]
    reduce_scatter x4 -> x0, waiting for transfers between devices: 317 us -> none  [the longest x1 116 us: local(): lax.psum_scatter(accum[2], 'dp', scatter_dimension=0, tiled=True)]
    pallas_call x0 -> x40, Pallas kernels: none -> 196 us  [the longest x19 148 us: slot_call(): pl.pallas_call(kernel, grid_spec=pltpu.PrefetchScalarGridSpec(num_scalar_...]
    ppermute x4 -> x71, waiting for transfers between devices: 40.9 us -> 150 us  [the longest x28 66.2 us: ring_hop(): return lax.ppermute(value, 'dp', pairs)]
    unnamed x2 -> x0, blocking collectives: 91.3 us -> none
    unnamed x14 -> x0, waiting for transfers between devices: 86.1 us -> none
    all_gather x4 -> x0, blocking collectives: 82.8 us -> none  [the longest x2 37.7 us: contrast_part(): table = lax.all_gather(unit_local, 'dp', axis=0, tiled=True)]
    all_gather x4 -> x0, waiting for transfers between devices: 67 us -> none  [the longest x1 47.5 us: local(): lax.all_gather(ff_out[0].astype(jnp.bfloat16), 'dp', axis=0, tiled=True)]
  transfers between devices with their start and end apart: 15 -> 71, of which waited for: 9 -> 31; matrix products, arithmetic and copies ran while one was open for 13% -> 6% of each run, Pallas kernels for 0% -> 31%
where the time goes in v3:
time: 468 us; the launch traced here: 460 us
  Pallas kernels  196 us (42%)
  waiting for transfers between devices  150 us (32%)
  starting transfers between devices  60.9 us (13%)
  local copies, waits for them, and re-layouts  30.7 us (7%)
  other arithmetic  18.9 us (4%)
    pallas_call x19, Pallas kernels, slot_call(): pl.pallas_call(kernel, grid_spec=pltpu.PrefetchScalarGridSpec(num_scalar_...  148 us
    ppermute x28, waiting for transfers between devices, ring_hop(): return lax.ppermute(value, 'dp', pairs)  66.2 us
    ppermute x4, waiting for transfers between devices, __init__(): self.moving = [lax.ppermute(value, 'section', pairs)]  59 us
    ppermute x28, starting transfers between devices, ring_hop(): return lax.ppermute(value, 'dp', pairs)  34.8 us
    pallas_call x3, Pallas kernels, weight_call(): pl.pallas_call(kernel, grid_spec=pltpu.PrefetchScalarGridSpec(num_scalar_...  29.3 us
    ppermute x39, waiting for transfers between devices, swapped(): return lax.ppermute(value, axis, [(i, i ^ mask) for i in range(count)])  24.5 us
    ppermute x39, starting transfers between devices, swapped(): return lax.ppermute(value, axis, [(i, i ^ mask) for i in range(count)])  20.4 us
    unnamed x166, local copies, waits for them, and re-layouts  16.3 us
  transfers between devices with their start and end apart: 71, of which 31 were waited for; matrix products, arithmetic and copies ran while one was open for 6% of the time, Pallas kernels for 31%

profile of v3, /device:TPU:0, one launch (start us, length us, event | category | flops | bytes accessed | tf_op | source)
XLA Modules:
  0.0 460.3 jit_solution(3085005436734855565)
XLA Ops:
  39.0 5.1 %collective-permute-done.13.refs_3_ = bf16[2,1,16,768]{3,2,1,0:T(8,128)(2,1)S(1)} collective-permute-done((bf16[2,1,16,768]{3,2,1,0:T(8,128)(2,1)S(1)}, bf16[2,1,16,768]{3,2,1,0:T(8,128)(2,1)S(1)}, u32[]{:S(2)}, u32[]{:S(2)}) %collective-permute-start.13) | collective-permute-done | bytes 49184 | tf_op jit(solution)/shard_map/ppermute | solution.py:53
  71.5 11.1 %attend.4 = (bf16[3,512,768]{2,1,0:T(8,128)(2,1)}, bf16[3,512,768]{2,1,0:T(8,128)(2,1)}, bf16[3,512,768]{2,1,0:T(8,128)(2,1)}, bf16[3,512,768]{2,1,0:T(8,128)(2,1)}, f32[3,3,512,128]{3,2,1,0:T(8,128)}) custom-call(s32[1]{0:T(128)} %bitcast.8.m_ref, bf16[512,768]{1,0:T(8,128)(2,1)S(1)} %get-tuple-element.724.refs_0_.x_ref, bf16[3,768,768]{2,1,0:T(8,128)(2,1)} %copy-done, ...), custom_call_target="tpu_custom_call" | custom-call | flops 30198988800 | bytes 300000000 | tf_op jit(solution)/shard_map/attend/pallas_call | solution.py:392
  82.6 3.7 collective-permute-done.24.refs_3_
  90.0 10.7 %collective-permute-done.26.refs_4_ = bf16[1,5,48,768]{3,2,1,0:T(8,128)(2,1)S(1)} collective-permute-done((bf16[1,5,48,768]{3,2,1,0:T(8,128)(2,1)S(1)}, bf16[1,5,48,768]{3,2,1,0:T(8,128)(2,1)S(1)}, u32[]{:S(2)}, u32[]{:S(2)}) %collective-permute-start.26) | collective-permute-done | bytes 368672 | tf_op jit(solution)/shard_map/ppermute | solution.py:53
  103.4 5.1 %collective-permute-done.33.refs_4_ = bf16[1,1,192,768]{3,2,1,0:T(8,128)(2,1)S(1)} collective-permute-done((bf16[1,1,192,768]{3,2,1,0:T(8,128)(2,1)S(1)}, bf16[1,1,192,768]{3,2,1,0:T(8,128)(2,1)S(1)}, u32[]{:S(2)}, u32[]{:S(2)}) %collective-permute-start.33) | collective-permute-done | bytes 294944 | tf_op jit(solution)/shard_map/ppermute | solution.py:53
  112.8 3.7 assemble.7.wf_ref.refs_6_.refs_3_
  116.6 13.1 %forward.4 = (bf16[512,768]{1,0:T(8,128)(2,1)S(1)}, bf16[3,512,768]{2,1,0:T(8,128)(2,1)}, f32[3,512,1]{2,1,0:T(8,128)S(1)}, bf16[3,512,3072]{2,1,0:T(8,128)(2,1)...) custom-call(s32[1]{0:T(128)} %bitcast.8.m_ref, ...), custom_call_target="tpu_custom_call" | custom-call | flops 54358179840 | bytes 300000000 | tf_op jit(solution)/shard_map/forward/pallas_call | solution.py:392
  132.9 11.2 %attend.5 = (bf16[3,512,768]{2,1,0:T(8,128)(2,1)}, bf16[3,512,768]{2,1,0:T(8,128)(2,1)}, bf16[3,512,768]{2,1,0:T(8,128)(2,1)}, bf16[3,512,768]{2,1,0:T(8,128)(2,1)}, f32[3,3,512,128]{3,2,1,0:T(8,128)}) custom-call(s32[1]{0:T(128)} %bitcast.23.m_ref, ...), custom_call_target="tpu_custom_call", output_to_operand_aliasing={{0}: (8, {}), {1}: (9, {}), {2}: (10, {}), {3}: (11, {}), {... | custom-call | tf_op jit(solution)/shard_map/attend/pallas_call | solution.py:392
  144.2 12.8 %forward.5 = (bf16[512,768]{1,0:T(8,128)(2,1)S(1)}, bf16[3,512,768]{2,1,0:T(8,128)(2,1)}, f32[3,512,1]{2,1,0:T(8,128)}, bf16[3,512,3072]{2,1,0:T(8,128)(2,1)}, b...) custom-call(s32[1]{0:T(128)} %bitcast.23.m_ref, ...), custom_call_target="tpu_custom_call", output_to_operand_aliasing={{1}: (8, {}), {2}: (9, {}), {3}: (10, {}), {4}: (11, {}), {... | custom-call | tf_op jit(solution)/shard_map/forward/pallas_call | solution.py:392
  169.7 6.3 %collective-permute-done.37.refs_0_.x_ref = bf16[512,768]{1,0:T(8,128)(2,1)S(1)} collective-permute-done((bf16[512,768]{1,0:T(8,128)(2,1)S(1)}, bf16[512,768]{1,0:T(8,128)(2,1)S(1)}, u32[]{:S(2)}, u32[]{:S(2)}) %collective-permute-start.37) | collective-permute-done | bytes 786464 | tf_op jit(solution)/shard_map/ppermute | solution.py:219
  187.3 3.9 collective-permute-done.41
  195.8 3.7 ff_back.4
  199.5 4.0 attend_back.7
  206.1 3.7 attend_back.8
  215.3 4.1 ff_back.5
  219.3 4.6 %attend_back.9 = (bf16[512,768]{1,0:T(8,128)(2,1)}, f32[16,768]{1,0:T(8,128)S(1)}, f32[2,512,768]{2,1,0:T(8,128)}, bf16[3,4,512,768]{3,2,1,0:T(8,128)(2,1)}) custom-call(s32[1]{0:T(128)} %bitcast.26.m_ref, bf16[3,512,768]{2,1,0:T(8,128)(2,1)} %get-tuple-element.494.refs_0_, ...), custom_call_target="tpu_custom_call", output_to_operand_aliasing={{3}: (14, {}), {2}: (10, {})} | custom-call | tf_op jit(solution)/shard_map/attend_back/pallas_call | solution.py:392
  224.0 52.7 %collective-permute-done.46.cot_ref = bf16[512,768]{1,0:T(8,128)(2,1)S(1)} collective-permute-done((bf16[512,768]{1,0:T(8,128)(2,1)S(1)}, bf16[512,768]{1,0:T(8,128)(2,1)S(1)}, u32[]{:S(2)}, u32[]{:S(2)}) %collective-permute-start.46) | collective-permute-done | bytes 786464 | tf_op jit(solution)/shard_map/ppermute | solution.py:219
  286.0 12.6 %ff_back.6 = (f32[512,768]{1,0:T(8,128)S(1)}, bf16[512,768]{1,0:T(8,128)(2,1)S(1)}, f32[16,768]{1,0:T(8,128)S(1)}, bf16[3,512,768]{2,1,0:T(8,128)(2,1)}, bf16[3,...) custom-call(s32[1]{0:T(128)} %bitcast.8.m_ref, ...), custom_call_target="tpu_custom_call", output_to_operand_aliasing={{3}: (12, {}), {4}: (13, {}), {5}: (14, {})} | custom-call | tf_op jit(solution)/shard_map/ff_back/pallas_call | solution.py:392
  298.6 17.1 %attend_back.10 = (bf16[512,768]{1,0:T(8,128)(2,1)}, f32[16,768]{1,0:T(8,128)S(1)}, f32[2,512,768]{2,1,0:T(8,128)}, bf16[3,4,512,768]{3,2,1,0:T(8,128)(2,1)}) custom-call(s32[1]{0:T(128)} %bitcast.8.m_ref, bf16[3,512,768]{2,1,0:T(8,128)(2,1)} %get-tuple-element.494.refs_0_, ...), custom_call_target="tpu_custom_call", output_to_operand_aliasing={{3}: (14, {}), {2}: (10, {})} | custom-call | tf_op jit(solution)/shard_map/attend_back/pallas_call | solution.py:392
  315.8 12.8 %ff_back.7 = (f32[512,768]{1,0:T(8,128)S(1)}, bf16[512,768]{1,0:T(8,128)(2,1)S(1)}, f32[16,768]{1,0:T(8,128)S(1)}, bf16[3,512,768]{2,1,0:T(8,128)(2,1)}, bf16[3,...) custom-call(s32[1]{0:T(128)} %bitcast.23.m_ref, ...), custom_call_target="tpu_custom_call", output_to_operand_aliasing={{3}: (12, {}), {4}: (13, {}), {5}: (14, {})} | custom-call | flops 72477573120 | bytes 300000000 | tf_op jit(solution)/shard_map/ff_back/pallas_call | solution.py:392
  328.6 8.8 %weight_out.1 = (bf16[8,192,768]{2,1,0:T(8,128)(2,1)S(1)}, bf16[8,192,768]{2,1,0:T(8,128)(2,1)S(1)}) custom-call(s32[16]{0:T(128)S(1)} %select_reduce_fusion.slot_ref, bf16[3,512,3072]{2,1,0:T(8,128)(2,1)} %get-tuple-element.606.gelu_ref, bf16[3,512,768]{2,1,0:T(8,128)(2,1)} %get-tuple-element.603.gbranch_ref), custom_call_target="tpu_custom_call" | custom-call | flops 48318382080 | bytes 300000000 | tf_op jit(solution)/shard_map/weight_out/pallas_call | solution.py:837
  337.5 9.8 %weight_wide.1 = (bf16[8,192,768]{2,1,0:T(8,128)(2,1)S(1)}, bf16[8,192,768]{2,1,0:T(8,128)(2,1)S(1)}) custom-call(s32[16]{0:T(128)S(1)} %select_reduce_fusion.slot_ref, bf16[3,512,768]{2,1,0:T(8,128)(2,1)} %get-tuple-element.520.refs_9_.refs_6_.xhat_ref, f32[12,768]{1,0:T(8,128)S(1)} %maximum_convert_fusion.refs_4_.vec_ref.refs_5_.refs_2_, ...), custom_call_target="tpu_custom_call" | custom-call | flops 48318382080 | bytes 300000000 | tf_op jit(solution)/shard_map/weight_wide/pallas_call | solution.py:837
  349.6 8.2 %attend_back.11 = (bf16[512,768]{1,0:T(8,128)(2,1)}, f32[16,768]{1,0:T(8,128)S(1)}, f32[2,512,768]{2,1,0:T(8,128)}, bf16[3,4,512,768]{3,2,1,0:T(8,128)(2,1)}) custom-call(s32[1]{0:T(128)} %bitcast.23.m_ref, bf16[3,512,768]{2,1,0:T(8,128)(2,1)} %get-tuple-element.494.refs_0_, ...), custom_call_target="tpu_custom_call", output_to_operand_aliasing={{3}: (14, {}), {2}: (10, {})} | custom-call | flops 36238786560 | bytes 300000000 | tf_op jit(solution)/shard_map/attend_back/pallas_call | solution.py:392
  361.5 8.2 %attend_back.12 = (bf16[512,768]{1,0:T(8,128)(2,1)}, f32[16,768]{1,0:T(8,128)S(1)}, f32[2,512,768]{2,1,0:T(8,128)}, bf16[3,4,512,768]{3,2,1,0:T(8,128)(2,1)}) custom-call(s32[1]{0:T(128)} %bitcast.23.m_ref, bf16[3,512,768]{2,1,0:T(8,128)(2,1)} %get-tuple-element.494.refs_0_, ...), custom_call_target="tpu_custom_call", output_to_operand_aliasing={{3}: (13, {}), {2}: (9, {})} | custom-call | flops 36238786560 | bytes 300000000 | tf_op jit(solution)/shard_map/attend_back/pallas_call | solution.py:392
  372.0 8.2 %attend_back.13 = (bf16[512,768]{1,0:T(8,128)(2,1)}, f32[16,768]{1,0:T(8,128)S(1)}, f32[2,512,768]{2,1,0:T(8,128)}, bf16[3,4,512,768]{3,2,1,0:T(8,128)(2,1)}) custom-call(s32[1]{0:T(128)} %bitcast.23.m_ref, bf16[3,512,768]{2,1,0:T(8,128)(2,1)} %get-tuple-element.494.refs_0_, ...), custom_call_target="tpu_custom_call", output_to_operand_aliasing={{3}: (13, {}), {2}: (9, {})} | custom-call | flops 36238786560 | bytes 300000000 | tf_op jit(solution)/shard_map/attend_back/pallas_call | solution.py:392
  380.2 6.0 %collective-permute-done.53.there_ref = bf16[2,192,768]{2,1,0:T(8,128)(2,1)S(1)} collective-permute-done((bf16[2,192,768]{2,1,0:T(8,128)(2,1)S(1)}, bf16[2,192,768]{2,1,0:T(8,128)(2,1)S(1)}, u32[]{:S(2)}, u32[]{:S(2)}) %collective-permute-start.53) | collective-permute-done | bytes 589856 | tf_op jit(solution)/shard_map/ppermute | solution.py:53
  386.2 10.7 %weight_attn.1 = (bf16[8,192,768]{2,1,0:T(8,128)(2,1)S(1)}, bf16[8,192,768]{2,1,0:T(8,128)(2,1)S(1)}) custom-call(s32[16]{0:T(128)S(1)} %select_reduce_fusion.slot_ref, bf16[2,512,768]{2,1,0:T(8,128)(2,1)} %maximum_select_fusion.x_ref, bf16[3,512,768]{2,1,0:T(8,128)(2,1)} %get-tuple-element.493.mixed_ref, bf16[3,4,512,768]{3,2,1,0:T(8,128)(2,1)} %get-tuple-element.649.grad_ref), custom_call_target="tpu_custom_call" | custom-call | flops 48318382080 | bytes 300000000 | tf_op jit(solution)/shard_map/weight_attn/pallas_call | solution.py:837
  407.2 6.3 %collective-permute-done.58.there_ref = bf16[2,192,768]{2,1,0:T(8,128)(2,1)S(1)} collective-permute-done((bf16[2,192,768]{2,1,0:T(8,128)(2,1)S(1)}, bf16[2,192,768]{2,1,0:T(8,128)(2,1)S(1)}, u32[]{:S(2)}, u32[]{:S(2)}) %collective-permute-start.58) | collective-permute-done | bytes 589856 | tf_op jit(solution)/shard_map/ppermute | solution.py:53
  420.0 4.0 collective-permute-done.62
  424.4 5.2 %collective-permute-done.61 = f32[16,768]{1,0:T(8,128)S(1)} collective-permute-done((f32[16,768]{1,0:T(8,128)S(1)}, f32[16,768]{1,0:T(8,128)S(1)}, u32[]{:S(2)}, u32[]{:S(2)}) %collective-permute-start.61) | collective-permute-done | bytes 49184 | tf_op jit(solution)/shard_map/ppermute | solution.py:38
  433.8 8.4 %collective-permute-done.65 = f32[16,768]{1,0:T(8,128)} collective-permute-done((f32[16,768]{1,0:T(8,128)}, f32[16,768]{1,0:T(8,128)}, u32[]{:S(2)}, u32[]{:S(2)}) %collective-permute-start.65) | collective-permute-done | bytes 49184 | tf_op jit(solution)/shard_map/ppermute | solution.py:38
  450.0 4.2 collective-permute-done.67
  (407 shorter events, 166.3 us)
Async XLA Ops:
  16.3 12.3 %collective-permute-start.10 = (bf16[2,1,16,768]{3,2,1,0:T(8,128)(2,1)S(1)}, bf16[2,1,16,768]{3,2,1,0:T(8,128)(2,1)S(1)}, u32[]{:S(2)}, u32[]{:S(2)}) collective-permute-start(bf16[2,1,16,768]{3,2,1,0:T(8,128)(2,1)S(1)} %collective-permute-done.5.refs_1_), channel_id=1, source_target_pairs={{0,1},{1,0},{2,3},{3,2},{4,5},{5,4},{6,7},{7,6},{8,9},{9,8},{10,11... | collective-permute-start | bytes 147464 | tf_op jit(solution)/shard_map/ppermute | solution.py:38
  16.3 12.3 %collective-permute-start.9 = (bf16[2,1,16,768]{3,2,1,0:T(8,128)(2,1)S(1)}, bf16[2,1,16,768]{3,2,1,0:T(8,128)(2,1)S(1)}, u32[]{:S(2)}, u32[]{:S(2)}) collective-permute-start(bf16[2,1,16,768]{3,2,1,0:T(8,128)(2,1)S(1)} %collective-permute-done.5.refs_1_), channel_id=1, source_target_pairs={{0,4},{1,3},{4,8},{5,1},{8,12},{9,5},{12,14},{13,9},{14,10},{15,13... | collective-permute-start | bytes 147464 | tf_op jit(solution)/shard_map/ppermute | solution.py:53
  30.3 20.1 %collective-permute-start.17 = (bf16[2,5,48,768]{3,2,1,0:T(8,128)(2,1)S(1)}, bf16[2,5,48,768]{3,2,1,0:T(8,128)(2,1)}, u32[]{:S(2)}, u32[]{:S(2)}) collective-permute-start(bf16[2,5,48,768]{3,2,1,0:T(8,128)(2,1)S(1)} %pad_maximum_fusion.refs_0_), channel_id=1, source_target_pairs={{0,4},{1,3},{4,8},{5,1},{8,12},{9,5},{12,14},{13,9},{14,10},{15,13... | collective-permute-start | bytes 2211848 | tf_op jit(solution)/shard_map/ppermute | solution.py:53
  32.2 11.9 %collective-permute-start.13 = (bf16[2,1,16,768]{3,2,1,0:T(8,128)(2,1)S(1)}, bf16[2,1,16,768]{3,2,1,0:T(8,128)(2,1)S(1)}, u32[]{:S(2)}, u32[]{:S(2)}) collective-permute-start(bf16[2,1,16,768]{3,2,1,0:T(8,128)(2,1)S(1)} %collective-permute-done.9.refs_2_), channel_id=1, source_target_pairs={{0,4},{1,3},{4,8},{5,1},{8,12},{9,5},{12,14},{13,9},{14,10},{15,13... | collective-permute-start | bytes 147464 | tf_op jit(solution)/shard_map/ppermute | solution.py:53
  35.7 12.3 %collective-permute-start.12 = (bf16[2,3,48,768]{3,2,1,0:T(8,128)(2,1)S(1)}, bf16[2,3,48,768]{3,2,1,0:T(8,128)(2,1)S(1)}, u32[]{:S(2)}, u32[]{:S(2)}) collective-permute-start(bf16[2,3,48,768]{3,2,1,0:T(8,128)(2,1)S(1)} %collective-permute-done.6.refs_3_), channel_id=1, source_target_pairs={{0,1},{1,0},{2,3},{3,2},{4,5},{5,4},{6,7},{7,6},{8,9},{9,8},{10,11... | collective-permute-start | bytes 1327112 | tf_op jit(solution)/shard_map/ppermute | solution.py:38
  35.7 10.7 %collective-permute-start.11 = (bf16[1,3,48,768]{3,2,1,0:T(8,128)(2,1)S(1)}, bf16[1,3,48,768]{3,2,1,0:T(8,128)(2,1)S(1)}, u32[]{:S(2)}, u32[]{:S(2)}) collective-permute-start(bf16[1,3,48,768]{3,2,1,0:T(8,128)(2,1)S(1)} %slice.72), channel_id=1, source_target_pairs={{0,4},{1,3},{4,8},{5,1},{8,12},{9,5},{12,14},{13,9},{14,10},{15,13... | collective-permute-start | bytes 663560 | tf_op jit(solution)/shard_map/ppermute | solution.py:53
  37.3 14.7 %collective-permute-start.16 = (bf16[1,192,768]{2,1,0:T(8,128)(2,1)S(1)}, bf16[1,192,768]{2,1,0:T(8,128)(2,1)S(1)}, u32[]{:S(2)}, u32[]{:S(2)}) collective-permute-start(bf16[1,192,768]{2,1,0:T(8,128)(2,1)S(1)} %convert_element_type.89), channel_id=1, source_target_pairs={{0,1},{1,0},{2,3},{3,2},{4,5},{5,4},{6,7},{7,6},{8,9},{9,8},{10,11... | collective-permute-start | bytes 884744 | tf_op jit(solution)/shard_map/ppermute | solution.py:38
  50.4 14.7 %collective-permute-start.23 = (bf16[2,5,48,768]{3,2,1,0:T(8,128)(2,1)}, bf16[2,5,48,768]{3,2,1,0:T(8,128)(2,1)}, u32[]{:S(2)}, u32[]{:S(2)}) collective-permute-start(bf16[2,5,48,768]{3,2,1,0:T(8,128)(2,1)} %collective-permute-done.17.refs_1_), channel_id=1, source_target_pairs={{0,1},{1,0},{2,3},{3,2},{4,5},{5,4},{6,7},{7,6},{8,9},{9,8},{10,11... | collective-permute-start | bytes 2211848 | tf_op jit(solution)/shard_map/ppermute | solution.py:38
  50.5 14.6 %collective-permute-start.22 = (bf16[2,5,48,768]{3,2,1,0:T(8,128)(2,1)}, bf16[2,5,48,768]{3,2,1,0:T(8,128)(2,1)}, u32[]{:S(2)}, u32[]{:S(2)}) collective-permute-start(bf16[2,5,48,768]{3,2,1,0:T(8,128)(2,1)} %collective-permute-done.17.refs_1_), channel_id=1, source_target_pairs={{0,4},{1,3},{4,8},{5,1},{8,12},{9,5},{12,14},{13,9},{14,10},{15,13... | collective-permute-start | bytes 2211848 | tf_op jit(solution)/shard_map/ppermute | solution.py:53
  52.1 16.4 %collective-permute-start.21 = (bf16[2,1,192,768]{3,2,1,0:T(8,128)(2,1)S(1)}, bf16[2,1,192,768]{3,2,1,0:T(8,128)(2,1)S(1)}, u32[]{:S(2)}, u32[]{:S(2)}) collective-permute-start(bf16[2,1,192,768]{3,2,1,0:T(8,128)(2,1)S(1)} %pad_maximum_fusion.1.refs_0_), channel_id=1, source_target_pairs={{0,4},{1,3},{4,8},{5,1},{8,12},{9,5},{12,14},{13,9},{14,10},{15,13... | collective-permute-start | bytes 1769480 | tf_op jit(solution)/shard_map/ppermute | solution.py:53
  68.5 17.8 %collective-permute-start.29 = (bf16[2,1,192,768]{3,2,1,0:T(8,128)(2,1)S(1)}, bf16[2,1,192,768]{3,2,1,0:T(8,128)(2,1)S(1)}, u32[]{:S(2)}, u32[]{:S(2)}) collective-permute-start(bf16[2,1,192,768]{3,2,1,0:T(8,128)(2,1)S(1)} %collective-permute-done.21.refs_1_), channel_id=1, source_target_pairs={{0,1},{1,0},{2,3},{3,2},{4,5},{5,4},{6,7},{7,6},{8,9},{9,8},{10,11... | collective-permute-start | bytes 1769480 | tf_op jit(solution)/shard_map/ppermute | solution.py:38
  68.5 17.8 %collective-permute-start.28 = (bf16[2,1,192,768]{3,2,1,0:T(8,128)(2,1)S(1)}, bf16[2,1,192,768]{3,2,1,0:T(8,128)(2,1)S(1)}, u32[]{:S(2)}, u32[]{:S(2)}) collective-permute-start(bf16[2,1,192,768]{3,2,1,0:T(8,128)(2,1)S(1)} %collective-permute-done.21.refs_1_), channel_id=1, source_target_pairs={{0,4},{1,3},{4,8},{5,1},{8,12},{9,5},{12,14},{13,9},{14,10},{15,13... | collective-permute-start | bytes 1769480 | tf_op jit(solution)/shard_map/ppermute | solution.py:53
  70.0 12.7 %collective-permute-start.25 = (bf16[2,5,48,768]{3,2,1,0:T(8,128)(2,1)}, bf16[2,5,48,768]{3,2,1,0:T(8,128)(2,1)S(1)}, u32[]{:S(2)}, u32[]{:S(2)}) collective-permute-start(bf16[2,5,48,768]{3,2,1,0:T(8,128)(2,1)} %collective-permute-done.22.refs_2_), channel_id=1, source_target_pairs={{0,1},{1,0},{2,3},{3,2},{4,5},{5,4},{6,7},{7,6},{8,9},{9,8},{10,11... | collective-permute-start | bytes 2211848 | tf_op jit(solution)/shard_map/ppermute | solution.py:38
  70.3 16.0 %collective-permute-start.24 = (bf16[2,5,48,768]{3,2,1,0:T(8,128)(2,1)}, bf16[2,5,48,768]{3,2,1,0:T(8,128)(2,1)S(1)}, u32[]{:S(2)}, u32[]{:S(2)}) collective-permute-start(bf16[2,5,48,768]{3,2,1,0:T(8,128)(2,1)} %collective-permute-done.22.refs_2_), channel_id=1, source_target_pairs={{0,4},{1,3},{4,8},{5,1},{8,12},{9,5},{12,14},{13,9},{14,10},{15,13... | collective-permute-start | bytes 2211848 | tf_op jit(solution)/shard_map/ppermute | solution.py:53
  86.3 14.4 %collective-permute-start.27 = (bf16[2,5,48,768]{3,2,1,0:T(8,128)(2,1)S(1)}, bf16[2,5,48,768]{3,2,1,0:T(8,128)(2,1)S(1)}, u32[]{:S(2)}, u32[]{:S(2)}) collective-permute-start(bf16[2,5,48,768]{3,2,1,0:T(8,128)(2,1)S(1)} %collective-permute-done.24.refs_3_), channel_id=1, source_target_pairs={{0,1},{1,0},{2,3},{3,2},{4,5},{5,4},{6,7},{7,6},{8,9},{9,8},{10,11... | collective-permute-start | bytes 2211848 | tf_op jit(solution)/shard_map/ppermute | solution.py:38
  86.3 14.4 %collective-permute-start.32 = (bf16[2,1,192,768]{3,2,1,0:T(8,128)(2,1)S(1)}, bf16[2,1,192,768]{3,2,1,0:T(8,128)(2,1)S(1)}, u32[]{:S(2)}, u32[]{:S(2)}) collective-permute-start(bf16[2,1,192,768]{3,2,1,0:T(8,128)(2,1)S(1)} %collective-permute-done.28.refs_2_), channel_id=1, source_target_pairs={{0,1},{1,0},{2,3},{3,2},{4,5},{5,4},{6,7},{7,6},{8,9},{9,8},{10,11... | collective-permute-start | bytes 1769480 | tf_op jit(solution)/shard_map/ppermute | solution.py:38
  86.9 13.9 %collective-permute-start.31 = (bf16[2,1,192,768]{3,2,1,0:T(8,128)(2,1)S(1)}, bf16[2,1,192,768]{3,2,1,0:T(8,128)(2,1)S(1)}, u32[]{:S(2)}, u32[]{:S(2)}) collective-permute-start(bf16[2,1,192,768]{3,2,1,0:T(8,128)(2,1)S(1)} %collective-permute-done.28.refs_2_), channel_id=1, source_target_pairs={{0,4},{1,3},{4,8},{5,1},{8,12},{9,5},{12,14},{13,9},{14,10},{15,13... | collective-permute-start | bytes 1769480 | tf_op jit(solution)/shard_map/ppermute | solution.py:53
  88.4 12.4 %collective-permute-start.26 = (bf16[1,5,48,768]{3,2,1,0:T(8,128)(2,1)S(1)}, bf16[1,5,48,768]{3,2,1,0:T(8,128)(2,1)S(1)}, u32[]{:S(2)}, u32[]{:S(2)}) collective-permute-start(bf16[1,5,48,768]{3,2,1,0:T(8,128)(2,1)S(1)} %slice.78), channel_id=1, source_target_pairs={{0,4},{1,3},{4,8},{5,1},{8,12},{9,5},{12,14},{13,9},{14,10},{15,13... | collective-permute-start | bytes 1105928 | tf_op jit(solution)/shard_map/ppermute | solution.py:53
  131.6 25.4 %collective-permute-start.36 = (bf16[512,768]{1,0:T(8,128)(2,1)S(1)}, bf16[512,768]{1,0:T(8,128)(2,1)S(1)}, u32[]{:S(2)}, u32[]{:S(2)}) collective-permute-start(bf16[512,768]{1,0:T(8,128)(2,1)S(1)} %get-tuple-element.424), channel_id=1, source_target_pairs={{0,16},{1,17},{2,18},{3,19},{4,20},{5,21},{6,22},{7,23},{8,24},{9,... | collective-permute-start | bytes 2359304 | tf_op jit(solution)/shard_map/ppermute | solution.py:219
  157.0 19.0 %collective-permute-start.37 = (bf16[512,768]{1,0:T(8,128)(2,1)S(1)}, bf16[512,768]{1,0:T(8,128)(2,1)S(1)}, u32[]{:S(2)}, u32[]{:S(2)}) collective-permute-start(bf16[512,768]{1,0:T(8,128)(2,1)S(1)} %get-tuple-element.452), channel_id=1, source_target_pairs={{0,16},{1,17},{2,18},{3,19},{4,20},{5,21},{6,22},{7,23},{8,24},{9,... | collective-permute-start | bytes 2359304 | tf_op jit(solution)/shard_map/ppermute | solution.py:219
  209.7 66.9 %collective-permute-start.46 = (bf16[512,768]{1,0:T(8,128)(2,1)S(1)}, bf16[512,768]{1,0:T(8,128)(2,1)S(1)}, u32[]{:S(2)}, u32[]{:S(2)}) collective-permute-start(bf16[512,768]{1,0:T(8,128)(2,1)S(1)} %get-tuple-element.568), channel_id=1, source_target_pairs={{16,0},{17,1},{18,2},{19,3},{20,4},{21,5},{22,6},{23,7},{24,8},{25... | collective-permute-start | bytes 2359304 | tf_op jit(solution)/shard_map/ppermute | solution.py:219
  276.6 39.1 %collective-permute-start.47 = (bf16[512,768]{1,0:T(8,128)(2,1)}, bf16[512,768]{1,0:T(8,128)(2,1)}, u32[]{:S(2)}, u32[]{:S(2)}) collective-permute-start(bf16[512,768]{1,0:T(8,128)(2,1)} %get-tuple-element.571), channel_id=1, source_target_pairs={{16,0},{17,1},{18,2},{19,3},{20,4},{21,5},{22,6},{23,7},{24,8},{25... | collective-permute-start | bytes 2359304 | tf_op jit(solution)/shard_map/ppermute | solution.py:219
  347.3 10.5 %collective-permute-start.49 = (bf16[8,192,768]{2,1,0:T(8,128)(2,1)S(1)}, bf16[8,192,768]{2,1,0:T(8,128)(2,1)S(1)}, u32[]{:S(2)}, u32[]{:S(2)}) collective-permute-start(bf16[8,192,768]{2,1,0:T(8,128)(2,1)S(1)} %get-tuple-element.618), channel_id=1, source_target_pairs={{0,1},{1,0},{2,3},{3,2},{4,5},{5,4},{6,7},{7,6},{8,9},{9,8},{10,11... | collective-permute-start | bytes 7077896 | tf_op jit(solution)/shard_map/ppermute | solution.py:38
  358.1 11.6 %collective-permute-start.52 = (bf16[2,192,768]{2,1,0:T(8,128)(2,1)S(1)}, bf16[2,192,768]{2,1,0:T(8,128)(2,1)S(1)}, u32[]{:S(2)}, u32[]{:S(2)}) collective-permute-start(bf16[2,192,768]{2,1,0:T(8,128)(2,1)S(1)} %fold.9), channel_id=1, source_target_pairs={{0,4},{1,3},{4,8},{5,1},{8,12},{9,5},{12,14},{13,9},{14,10},{15,13... | collective-permute-start | bytes 1769480 | tf_op jit(solution)/shard_map/ppermute | solution.py:53
  360.1 11.1 %collective-permute-start.51 = (bf16[1,192,768]{2,1,0:T(8,128)(2,1)S(1)}, bf16[1,192,768]{2,1,0:T(8,128)(2,1)S(1)}, u32[]{:S(2)}, u32[]{:S(2)}) collective-permute-start(bf16[1,192,768]{2,1,0:T(8,128)(2,1)S(1)} %get-tuple-element.633), channel_id=1, source_target_pairs={{0,4},{1,3},{4,8},{5,1},{8,12},{9,5},{12,14},{13,9},{14,10},{15,13... | collective-permute-start | bytes 884744 | tf_op jit(solution)/shard_map/ppermute | solution.py:53
  371.5 14.7 %collective-permute-start.53 = (bf16[2,192,768]{2,1,0:T(8,128)(2,1)S(1)}, bf16[2,192,768]{2,1,0:T(8,128)(2,1)S(1)}, u32[]{:S(2)}, u32[]{:S(2)}) collective-permute-start(bf16[2,192,768]{2,1,0:T(8,128)(2,1)S(1)} %fold.10), channel_id=1, source_target_pairs={{0,4},{1,3},{4,8},{5,1},{8,12},{9,5},{12,14},{13,9},{14,10},{15,13... | collective-permute-start | bytes 1769480 | tf_op jit(solution)/shard_map/ppermute | solution.py:53
  397.9 15.6 %collective-permute-start.58 = (bf16[2,192,768]{2,1,0:T(8,128)(2,1)S(1)}, bf16[2,192,768]{2,1,0:T(8,128)(2,1)S(1)}, u32[]{:S(2)}, u32[]{:S(2)}) collective-permute-start(bf16[2,192,768]{2,1,0:T(8,128)(2,1)S(1)} %fold.12), channel_id=1, source_target_pairs={{0,4},{1,3},{4,8},{5,1},{8,12},{9,5},{12,14},{13,9},{14,10},{15,13... | collective-permute-start | bytes 1769480 | tf_op jit(solution)/shard_map/ppermute | solution.py:53
  402.0 14.7 %collective-permute-start.56 = (bf16[1,192,768]{2,1,0:T(8,128)(2,1)S(1)}, bf16[1,192,768]{2,1,0:T(8,128)(2,1)S(1)}, u32[]{:S(2)}, u32[]{:S(2)}) collective-permute-start(bf16[1,192,768]{2,1,0:T(8,128)(2,1)S(1)} %get-tuple-element.654), channel_id=1, source_target_pairs={{0,4},{1,3},{4,8},{5,1},{8,12},{9,5},{12,14},{13,9},{14,10},{15,13... | collective-permute-start | bytes 884744 | tf_op jit(solution)/shard_map/ppermute | solution.py:53
  402.3 13.2 %collective-permute-start.57 = (f32[16,768]{1,0:T(8,128)S(1)}, f32[16,768]{1,0:T(8,128)S(1)}, u32[]{:S(2)}, u32[]{:S(2)}) collective-permute-start(f32[16,768]{1,0:T(8,128)S(1)} %get-tuple-element.655), channel_id=1, source_target_pairs={{0,8},{1,9},{2,10},{3,11},{4,12},{5,13},{6,14},{7,15},{8,0},{9,1},... | collective-permute-start | bytes 147464 | tf_op jit(solution)/shard_map/ppermute | solution.py:38
  417.0 13.2 %collective-permute-start.60 = (bf16[2,192,768]{2,1,0:T(8,128)(2,1)S(1)}, bf16[2,192,768]{2,1,0:T(8,128)(2,1)S(1)}, u32[]{:S(2)}, u32[]{:S(2)}) collective-permute-start(bf16[2,192,768]{2,1,0:T(8,128)(2,1)S(1)} %fold.14), channel_id=1, source_target_pairs={{0,4},{1,3},{4,8},{5,1},{8,12},{9,5},{12,14},{13,9},{14,10},{15,13... | collective-permute-start | bytes 1769480 | tf_op jit(solution)/shard_map/ppermute | solution.py:53
  417.9 11.7 %collective-permute-start.61 = (f32[16,768]{1,0:T(8,128)S(1)}, f32[16,768]{1,0:T(8,128)S(1)}, u32[]{:S(2)}, u32[]{:S(2)}) collective-permute-start(f32[16,768]{1,0:T(8,128)S(1)} %add.202), channel_id=1, source_target_pairs={{0,4},{1,5},{2,6},{3,7},{4,0},{5,1},{6,2},{7,3},{8,12},{9,13},{10,... | collective-permute-start | bytes 147464 | tf_op jit(solution)/shard_map/ppermute | solution.py:38
  430.4 11.8 %collective-permute-start.64 = (bf16[2,192,768]{2,1,0:T(8,128)(2,1)S(1)}, bf16[2,192,768]{2,1,0:T(8,128)(2,1)S(1)}, u32[]{:S(2)}, u32[]{:S(2)}) collective-permute-start(bf16[2,192,768]{2,1,0:T(8,128)(2,1)S(1)} %fold.16), channel_id=1, source_target_pairs={{0,4},{1,3},{4,8},{5,1},{8,12},{9,5},{12,14},{13,9},{14,10},{15,13... | collective-permute-start | bytes 1769480 | tf_op jit(solution)/shard_map/ppermute | solution.py:53
  (117 other events, 1285.8 us)

commit v4 on v3

--- a/solution.py
+++ b/solution.py
@@ -29,8 +29,10 @@
     return pltpu.CompilerParams(vmem_limit_bytes=size)
 
 
-def cost(flops, size):
-    return pl.CostEstimate(flops=int(10 * flops), bytes_accessed=int(10 * size), transcendentals=0)
+def cost(flops, size, factor=2):
+    return pl.CostEstimate(
+        flops=int(factor * flops), bytes_accessed=int(factor * size), transcendentals=0
+    )
 
 
 def swapped(value, axis, mask):
@@ -401,12 +403,12 @@
         out_shape=outs,
         input_output_aliases=aliases,
         compiler_params=params(slot_vmem),
-        cost_estimate=cost(0, 0) if m.ahead else cost(size * product, 3e7),
+        cost_estimate=cost(0, 0) if m.ahead else cost(size * product, 3e7, 10 if "back" in name else 2),
         name=name,
     )(m.entry, *[in_place(value) for value in ins], *[in_place(value) for value in before])
 
 
-def attend_kernel(n_before, m_ref, *refs):
+def attend_kernel(first, n_before, m_ref, *refs):
     x_ref, wq_ref, wk_ref, wv_ref, vec_ref, seg_col_ref, seg_row_ref, *refs = refs
     q_ref, k_ref, v_ref, mixed_ref, lse_ref, mask_ref = refs[n_before:]
     i = pl.program_id(0)
@@ -417,7 +419,7 @@
         def _():
             mask_ref[...] = jnp.where(seg_col_ref[...] == seg_row_ref[...], 0.0, masked_value)
 
-        lanes = pl.ds(pl.multiple_of(i * group, group), group)
+        lanes = pl.ds(pl.multiple_of((first + i) * group, group), group)
         x = x_ref[...]
         q = (mm(x, wq_ref[...]) + vec_ref[2:3, lanes]).astype(bf16)
         k = mm(x, wk_ref[...]).astype(bf16)
@@ -436,30 +438,31 @@
             outs.append(mm(raw.astype(bf16), v[:, c]) / total)
             lses.append(top + jnp.log(total))
         mixed_ref[...] = jnp.concatenate(outs, axis=1).astype(bf16)
-        lse_ref[...] = jnp.concatenate(lses + [jnp.zeros((SEQ, 128 - len(lses)), f32)], axis=1)
+        lses = jnp.concatenate(lses + [jnp.zeros((SEQ, 128 - len(lses)), f32)], axis=1)
+        lse_ref[...] = jnp.transpose(lses)[:8]
 
 
 vec_spec = full((table_rows, D))
 
 
-def attend(m, x, w_in, vec, seg_col, seg_row, before):
+def attend(m, x, w_in, vec, seg_col, seg_row, before, first=0, count=groups):
     def weight(b):
-        return pl.BlockSpec((None, D, group), lambda i, m: (b, 0, busy(i, m)))
-
-    heads = at_entry((SEQ, group), lambda i: (0, i))
+        return pl.BlockSpec((None, D, group), lambda i, m: (b, 0, first + busy(i, m)))
+
+    heads = at_entry((SEQ, group), lambda i: (0, first + i))
     return slot_call(
-        partial(attend_kernel, len(before)),
+        partial(attend_kernel, first, len(before)),
         m,
-        groups,
+        count,
         [x, w_in, w_in, w_in, vec, seg_col, seg_row],
         [full(token_block)]
         + [weight(b) for b in range(3)]
         + [vec_spec, at_entry((SEQ, 1)), at_entry((1, SEQ))],
-        [tokens_buffer(D, bf16)] * 4 + [far((entries, groups, SEQ, 128), f32)],
-        [heads] * 4 + [at_entry((None, SEQ, 128), lambda i: (i, 0, 0))],
+        [tokens_buffer(D, bf16)] * 4 + [far((entries, groups, 8, SEQ), f32)],
+        [heads] * 4 + [at_entry((None, 8, SEQ), lambda i: (first + i, 0, 0))],
         before,
         [pltpu.VMEM((SEQ, SEQ), f32)],
-        5,
+        2 * count,
         "attend",
     )
 
@@ -766,7 +769,7 @@
     def _():
         q, k, v, gm = q_ref[...], k_ref[...], v_ref[...], gm_ref[...]
         scaled = q * jnp.asarray(HEAD**-0.5, bf16)
-        lse = jnp.transpose(lse_ref[...])
+        lse = lse_ref[...]
         parts = [[], [], []]
         for h in range(group // HEAD):
             c = slice(h * HEAD, (h + 1) * HEAD)
@@ -806,7 +809,7 @@
         [q, k, v, gm, lse, w_in, w_in, w_in, *totals, seg_col, seg_row, small],
         [heads] * 3
         + [pl.BlockSpec((SEQ, group), lambda i, m: (0, first + busy(i, m)))]
-        + [at_entry((None, SEQ, 128), lambda i: (first + i, 0, 0))]
+        + [at_entry((None, 8, SEQ), lambda i: (first + i, 0, 0))]
         + [weight(b) for b in range(3)]
         + total_specs
         + [at_entry((SEQ, 1)), at_entry((1, SEQ)), full((16, D))],
@@ -845,7 +848,7 @@
         ),
         out_shape=outs,
         compiler_params=params(),
-        cost_estimate=cost(8 * product, 3e7),
+        cost_estimate=cost(8 * product, 3e7, 10),
         name=name,
     )(slot, *[in_place(value) for value in ins])
 
@@ -1091,8 +1094,7 @@
     m = Slot(entry(0, 1))
     state = ff_slot(m, cots, segs0, small)
     state = onward([near1], state)
-    two_calls = ((0, 2), (2, 1))
-    low, small, hidden_grads, grads = heads_slot(m, *state, lambda: [near1], two_calls)
+    low, small, hidden_grads, grads = heads_slot(m, *state, lambda: [near1], all_heads)
     sent0 = Sent(low, pairs)
 
     m = Slot(entry(1, 1), True)

time: 468 us -> 461 us (0.985)
  waiting for transfers between devices: 150 us -> 141 us
    ppermute x28, waiting for transfers between devices: 66.2 us -> 56 us  [ring_hop(): return lax.ppermute(value, 'dp', pairs)]
    ppermute x28, starting transfers between devices: 34.8 us -> 41.1 us  [ring_hop(): return lax.ppermute(value, 'dp', pairs)]
    pallas_call x19 -> x18, Pallas kernels: 148 us -> 144 us  [slot_call(): pl.pallas_call(kernel, grid_spec=pltpu.PrefetchScalarGridSpec(num_scalar_...]
    unnamed x166 -> x156, local copies, waits for them, and re-layouts: 16.3 us -> 16 us
  transfers between devices with their start and end apart: 71 -> 71, of which waited for: 31 -> 31; matrix products, arithmetic and copies ran while one was open for 6% -> 7% of each run, Pallas kernels for 31% -> 31%
where the time goes in v4:
time: 461 us; the launch traced here: 454 us
  Pallas kernels  192 us (42%)
  waiting for transfers between devices  141 us (31%)
  starting transfers between devices  64.8 us (14%)
  local copies, waits for them, and re-layouts  31.3 us (7%)
  other arithmetic  20 us (4%)
    pallas_call x18, Pallas kernels, slot_call(): pl.pallas_call(kernel, grid_spec=pltpu.PrefetchScalarGridSpec(num_scalar_...  144 us
    ppermute x4, waiting for transfers between devices, __init__(): self.moving = [lax.ppermute(value, 'section', pairs)]  58.2 us
    ppermute x28, waiting for transfers between devices, ring_hop(): return lax.ppermute(value, 'dp', pairs)  56 us
    ppermute x28, starting transfers between devices, ring_hop(): return lax.ppermute(value, 'dp', pairs)  41.1 us
    pallas_call x3, Pallas kernels, weight_call(): pl.pallas_call(kernel, grid_spec=pltpu.PrefetchScalarGridSpec(num_scalar_...  29.3 us
    ppermute x39, waiting for transfers between devices, swapped(): return lax.ppermute(value, axis, [(i, i ^ mask) for i in range(count)])  27.3 us
    ppermute x39, starting transfers between devices, swapped(): return lax.ppermute(value, axis, [(i, i ^ mask) for i in range(count)])  18.1 us
    unnamed x156, local copies, waits for them, and re-layouts  16 us
  transfers between devices with their start and end apart: 71, of which 31 were waited for; matrix products, arithmetic and copies ran while one was open for 7% of the time, Pallas kernels for 31%

profile of v4, /device:TPU:0, one launch (start us, length us, event | category | flops | bytes accessed | tf_op | source)
XLA Modules:
  0.0 453.8 jit_solution(7282004809707849826)
XLA Ops:
  12.4 3.5 collective-permute-done.1.refs_1_
  38.5 5.6 %collective-permute-done.13.refs_3_ = bf16[2,1,16,768]{3,2,1,0:T(8,128)(2,1)S(1)} collective-permute-done((bf16[2,1,16,768]{3,2,1,0:T(8,128)(2,1)}, bf16[2,1,16,768]{3,2,1,0:T(8,128)(2,1)S(1)}, u32[]{:S(2)}, u32[]{:S(2)}) %collective-permute-start.13) | collective-permute-done | bytes 49184 | tf_op jit(solution)/shard_map/ppermute | solution.py:55
  68.9 11.3 %attend.4 = (bf16[3,512,768]{2,1,0:T(8,128)(2,1)}, bf16[3,512,768]{2,1,0:T(8,128)(2,1)}, bf16[3,512,768]{2,1,0:T(8,128)(2,1)}, bf16[3,512,768]{2,1,0:T(8,128)(2,1)}, f32[3,3,8,512]{3,2,1,0:T(8,128)}) custom-call(s32[1]{0:T(128)} %bitcast.8.m_ref, bf16[512,768]{1,0:T(8,128)(2,1)S(1)} %get-tuple-element.710.refs_0_.x_ref, bf16[3,768,768]{2,1,0:T(8,128)(2,1)} %copy-done.3, ...), custom_call_target="tpu_custom_call" | custom-call | flops 7247757312 | bytes 60000000 | tf_op jit(solution)/shard_map/attend/pallas_call | solution.py:394
  84.6 11.1 %collective-permute-done.26.refs_4_ = bf16[1,5,48,768]{3,2,1,0:T(8,128)(2,1)S(1)} collective-permute-done((bf16[1,5,48,768]{3,2,1,0:T(8,128)(2,1)S(1)}, bf16[1,5,48,768]{3,2,1,0:T(8,128)(2,1)S(1)}, u32[]{:S(2)}, u32[]{:S(2)}) %collective-permute-start.26) | collective-permute-done | bytes 368672 | tf_op jit(solution)/shard_map/ppermute | solution.py:55
  98.4 5.0 %collective-permute-done.33.refs_4_ = bf16[1,1,192,768]{3,2,1,0:T(8,128)(2,1)S(1)} collective-permute-done((bf16[1,1,192,768]{3,2,1,0:T(8,128)(2,1)S(1)}, bf16[1,1,192,768]{3,2,1,0:T(8,128)(2,1)S(1)}, u32[]{:S(2)}, u32[]{:S(2)}) %collective-permute-start.33) | collective-permute-done | bytes 294944 | tf_op jit(solution)/shard_map/ppermute | solution.py:55
  103.5 3.3 assemble.6.wo_ref.wi_ref.refs_8_.refs_11_.refs_5_
  107.8 3.7 assemble.7.wf_ref.refs_6_.refs_3_
  111.5 13.4 %forward.4 = (bf16[512,768]{1,0:T(8,128)(2,1)}, bf16[3,512,768]{2,1,0:T(8,128)(2,1)}, f32[3,512,1]{2,1,0:T(8,128)S(1)}, bf16[3,512,3072]{2,1,0:T(8,128)(2,1)}, b...) custom-call(s32[1]{0:T(128)} %bitcast.8.m_ref, ...), custom_call_target="tpu_custom_call" | custom-call | flops 10871635968 | bytes 60000000 | tf_op jit(solution)/shard_map/forward/pallas_call | solution.py:394
  128.1 11.5 %attend.5 = (bf16[3,512,768]{2,1,0:T(8,128)(2,1)}, bf16[3,512,768]{2,1,0:T(8,128)(2,1)}, bf16[3,512,768]{2,1,0:T(8,128)(2,1)}, bf16[3,512,768]{2,1,0:T(8,128)(2,1)}, f32[3,3,8,512]{3,2,1,0:T(8,128)}) custom-call(s32[1]{0:T(128)} %bitcast.23.m_ref, ...), custom_call_target="tpu_custom_call", output_to_operand_aliasing={{0}: (8, {}), {1}: (9, {}), {2}: (10, {}), {3}: (11, {}), {... | custom-call | tf_op jit(solution)/shard_map/attend/pallas_call | solution.py:394
  139.6 12.8 %forward.5 = (bf16[512,768]{1,0:T(8,128)(2,1)S(1)}, bf16[3,512,768]{2,1,0:T(8,128)(2,1)}, f32[3,512,1]{2,1,0:T(8,128)}, bf16[3,512,3072]{2,1,0:T(8,128)(2,1)}, b...) custom-call(s32[1]{0:T(128)} %bitcast.23.m_ref, ...), custom_call_target="tpu_custom_call", output_to_operand_aliasing={{1}: (8, {}), {2}: (9, {}), {3}: (10, {}), {4}: (11, {}), {... | custom-call | tf_op jit(solution)/shard_map/forward/pallas_call | solution.py:394
  164.5 6.9 %collective-permute-done.37.refs_0_.x_ref = bf16[512,768]{1,0:T(8,128)(2,1)S(1)} collective-permute-done((bf16[512,768]{1,0:T(8,128)(2,1)S(1)}, bf16[512,768]{1,0:T(8,128)(2,1)S(1)}, u32[]{:S(2)}, u32[]{:S(2)}) %collective-permute-start.37) | collective-permute-done | bytes 786464 | tf_op jit(solution)/shard_map/ppermute | solution.py:221
  175.7 3.6 forward.7
  182.3 3.9 collective-permute-done.41
  190.7 3.6 ff_back.4
  194.4 3.9 attend_back.6
  209.3 3.9 ff_back.5
  213.2 4.5 attend_back.7
  217.7 48.5 %collective-permute-done.46.cot_ref = bf16[512,768]{1,0:T(8,128)(2,1)S(1)} collective-permute-done((bf16[512,768]{1,0:T(8,128)(2,1)S(1)}, bf16[512,768]{1,0:T(8,128)(2,1)S(1)}, u32[]{:S(2)}, u32[]{:S(2)}) %collective-permute-start.46) | collective-permute-done | bytes 786464 | tf_op jit(solution)/shard_map/ppermute | solution.py:221
  275.6 13.1 %ff_back.6 = (f32[512,768]{1,0:T(8,128)S(1)}, bf16[512,768]{1,0:T(8,128)(2,1)S(1)}, f32[16,768]{1,0:T(8,128)S(1)}, bf16[3,512,768]{2,1,0:T(8,128)(2,1)}, bf16[3,...) custom-call(s32[1]{0:T(128)} %bitcast.8.m_ref, ...), custom_call_target="tpu_custom_call", output_to_operand_aliasing={{3}: (12, {}), {4}: (13, {}), {5}: (14, {})} | custom-call | tf_op jit(solution)/shard_map/ff_back/pallas_call | solution.py:394
  288.6 17.0 %attend_back.8 = (bf16[512,768]{1,0:T(8,128)(2,1)}, f32[16,768]{1,0:T(8,128)S(1)}, f32[2,512,768]{2,1,0:T(8,128)}, bf16[3,4,512,768]{3,2,1,0:T(8,128)(2,1)}) custom-call(s32[1]{0:T(128)} %bitcast.8.m_ref, bf16[3,512,768]{2,1,0:T(8,128)(2,1)} %get-tuple-element.487.refs_0_, ...), custom_call_target="tpu_custom_call", output_to_operand_aliasing={{3}: (14, {}), {2}: (10, {})} | custom-call | tf_op jit(solution)/shard_map/attend_back/pallas_call | solution.py:394
  308.4 12.7 %ff_back.7 = (f32[512,768]{1,0:T(8,128)S(1)}, bf16[512,768]{1,0:T(8,128)(2,1)S(1)}, f32[16,768]{1,0:T(8,128)S(1)}, bf16[3,512,768]{2,1,0:T(8,128)(2,1)}, bf16[3,...) custom-call(s32[1]{0:T(128)} %bitcast.23.m_ref, ...), custom_call_target="tpu_custom_call", output_to_operand_aliasing={{3}: (12, {}), {4}: (13, {}), {5}: (14, {})} | custom-call | flops 72477573120 | bytes 300000000 | tf_op jit(solution)/shard_map/ff_back/pallas_call | solution.py:394
  321.1 8.8 %weight_out.1 = (bf16[8,192,768]{2,1,0:T(8,128)(2,1)S(1)}, bf16[8,192,768]{2,1,0:T(8,128)(2,1)S(1)}) custom-call(s32[16]{0:T(128)S(1)} %select_reduce_fusion.slot_ref, bf16[3,512,3072]{2,1,0:T(8,128)(2,1)} %get-tuple-element.592.gelu_ref, bf16[3,512,768]{2,1,0:T(8,128)(2,1)} %get-tuple-element.589.gbranch_ref), custom_call_target="tpu_custom_call" | custom-call | flops 48318382080 | bytes 300000000 | tf_op jit(solution)/shard_map/weight_out/pallas_call | solution.py:840
  330.0 9.8 %weight_wide.1 = (bf16[8,192,768]{2,1,0:T(8,128)(2,1)S(1)}, bf16[8,192,768]{2,1,0:T(8,128)(2,1)S(1)}) custom-call(s32[16]{0:T(128)S(1)} %select_reduce_fusion.slot_ref, bf16[3,512,768]{2,1,0:T(8,128)(2,1)} %get-tuple-element.513.refs_9_.refs_6_.xhat_ref, f32[12,768]{1,0:T(8,128)S(1)} %maximum_convert_fusion.refs_4_.vec_ref.refs_5_.refs_2_, ...), custom_call_target="tpu_custom_call" | custom-call | flops 48318382080 | bytes 300000000 | tf_op jit(solution)/shard_map/weight_wide/pallas_call | solution.py:840
  343.1 8.1 %attend_back.9 = (bf16[512,768]{1,0:T(8,128)(2,1)}, f32[16,768]{1,0:T(8,128)S(1)}, f32[2,512,768]{2,1,0:T(8,128)}, bf16[3,4,512,768]{3,2,1,0:T(8,128)(2,1)}) custom-call(s32[1]{0:T(128)} %bitcast.23.m_ref, bf16[3,512,768]{2,1,0:T(8,128)(2,1)} %get-tuple-element.487.refs_0_, ...), custom_call_target="tpu_custom_call", output_to_operand_aliasing={{3}: (14, {}), {2}: (10, {})} | custom-call | flops 36238786560 | bytes 300000000 | tf_op jit(solution)/shard_map/attend_back/pallas_call | solution.py:394
  354.1 8.1 %attend_back.10 = (bf16[512,768]{1,0:T(8,128)(2,1)}, f32[16,768]{1,0:T(8,128)S(1)}, f32[2,512,768]{2,1,0:T(8,128)}, bf16[3,4,512,768]{3,2,1,0:T(8,128)(2,1)}) custom-call(s32[1]{0:T(128)} %bitcast.23.m_ref, bf16[3,512,768]{2,1,0:T(8,128)(2,1)} %get-tuple-element.487.refs_0_, ...), custom_call_target="tpu_custom_call", output_to_operand_aliasing={{3}: (13, {}), {2}: (9, {})} | custom-call | flops 36238786560 | bytes 300000000 | tf_op jit(solution)/shard_map/attend_back/pallas_call | solution.py:394
  365.1 8.1 %attend_back.11 = (bf16[512,768]{1,0:T(8,128)(2,1)}, f32[16,768]{1,0:T(8,128)S(1)}, f32[2,512,768]{2,1,0:T(8,128)}, bf16[3,4,512,768]{3,2,1,0:T(8,128)(2,1)}) custom-call(s32[1]{0:T(128)} %bitcast.23.m_ref, bf16[3,512,768]{2,1,0:T(8,128)(2,1)} %get-tuple-element.487.refs_0_, ...), custom_call_target="tpu_custom_call", output_to_operand_aliasing={{3}: (13, {}), {2}: (9, {})} | custom-call | flops 36238786560 | bytes 300000000 | tf_op jit(solution)/shard_map/attend_back/pallas_call | solution.py:394
  373.2 5.5 %collective-permute-done.53.there_ref = bf16[2,192,768]{2,1,0:T(8,128)(2,1)S(1)} collective-permute-done((bf16[2,192,768]{2,1,0:T(8,128)(2,1)S(1)}, bf16[2,192,768]{2,1,0:T(8,128)(2,1)S(1)}, u32[]{:S(2)}, u32[]{:S(2)}) %collective-permute-start.53) | collective-permute-done | bytes 589856 | tf_op jit(solution)/shard_map/ppermute | solution.py:55
  378.8 10.7 %weight_attn.1 = (bf16[8,192,768]{2,1,0:T(8,128)(2,1)S(1)}, bf16[8,192,768]{2,1,0:T(8,128)(2,1)S(1)}) custom-call(s32[16]{0:T(128)S(1)} %select_reduce_fusion.slot_ref, bf16[2,512,768]{2,1,0:T(8,128)(2,1)} %maximum_select_fusion.x_ref, bf16[3,512,768]{2,1,0:T(8,128)(2,1)} %get-tuple-element.486.mixed_ref, bf16[3,4,512,768]{3,2,1,0:T(8,128)(2,1)} %get-tuple-element.635.grad_ref), custom_call_target="tpu_custom_call" | custom-call | flops 48318382080 | bytes 300000000 | tf_op jit(solution)/shard_map/weight_attn/pallas_call | solution.py:840
  399.8 6.3 %collective-permute-done.58.there_ref = bf16[2,192,768]{2,1,0:T(8,128)(2,1)S(1)} collective-permute-done((bf16[2,192,768]{2,1,0:T(8,128)(2,1)S(1)}, bf16[2,192,768]{2,1,0:T(8,128)(2,1)S(1)}, u32[]{:S(2)}, u32[]{:S(2)}) %collective-permute-start.58) | collective-permute-done | bytes 589856 | tf_op jit(solution)/shard_map/ppermute | solution.py:55
  417.1 6.1 %collective-permute-done.61 = f32[16,768]{1,0:T(8,128)S(1)} collective-permute-done((f32[16,768]{1,0:T(8,128)S(1)}, f32[16,768]{1,0:T(8,128)S(1)}, u32[]{:S(2)}, u32[]{:S(2)}) %collective-permute-start.61) | collective-permute-done | bytes 49184 | tf_op jit(solution)/shard_map/ppermute | solution.py:40
  427.1 8.4 %collective-permute-done.65 = f32[16,768]{1,0:T(8,128)} collective-permute-done((f32[16,768]{1,0:T(8,128)}, f32[16,768]{1,0:T(8,128)}, u32[]{:S(2)}, u32[]{:S(2)}) %collective-permute-start.65) | collective-permute-done | bytes 49184 | tf_op jit(solution)/shard_map/ppermute | solution.py:40
  443.2 4.2 collective-permute-done.67
  (396 shorter events, 162.5 us)
Async XLA Ops:
  16.4 12.3 %collective-permute-start.10 = (bf16[2,1,16,768]{3,2,1,0:T(8,128)(2,1)}, bf16[2,1,16,768]{3,2,1,0:T(8,128)(2,1)S(1)}, u32[]{:S(2)}, u32[]{:S(2)}) collective-permute-start(bf16[2,1,16,768]{3,2,1,0:T(8,128)(2,1)} %collective-permute-done.5.refs_1_), channel_id=1, source_target_pairs={{0,1},{1,0},{2,3},{3,2},{4,5},{5,4},{6,7},{7,6},{8,9},{9,8},{10,11... | collective-permute-start | bytes 147464 | tf_op jit(solution)/shard_map/ppermute | solution.py:40
  16.4 12.3 %collective-permute-start.9 = (bf16[2,1,16,768]{3,2,1,0:T(8,128)(2,1)}, bf16[2,1,16,768]{3,2,1,0:T(8,128)(2,1)}, u32[]{:S(2)}, u32[]{:S(2)}) collective-permute-start(bf16[2,1,16,768]{3,2,1,0:T(8,128)(2,1)} %collective-permute-done.5.refs_1_), channel_id=1, source_target_pairs={{0,4},{1,3},{4,8},{5,1},{8,12},{9,5},{12,14},{13,9},{14,10},{15,13... | collective-permute-start | bytes 147464 | tf_op jit(solution)/shard_map/ppermute | solution.py:55
  30.4 18.2 %collective-permute-start.17 = (bf16[2,5,48,768]{3,2,1,0:T(8,128)(2,1)S(1)}, bf16[2,5,48,768]{3,2,1,0:T(8,128)(2,1)}, u32[]{:S(2)}, u32[]{:S(2)}) collective-permute-start(bf16[2,5,48,768]{3,2,1,0:T(8,128)(2,1)S(1)} %pad_maximum_fusion.refs_0_), channel_id=1, source_target_pairs={{0,4},{1,3},{4,8},{5,1},{8,12},{9,5},{12,14},{13,9},{14,10},{15,13... | collective-permute-start | bytes 2211848 | tf_op jit(solution)/shard_map/ppermute | solution.py:55
  32.8 11.4 %collective-permute-start.13 = (bf16[2,1,16,768]{3,2,1,0:T(8,128)(2,1)}, bf16[2,1,16,768]{3,2,1,0:T(8,128)(2,1)S(1)}, u32[]{:S(2)}, u32[]{:S(2)}) collective-permute-start(bf16[2,1,16,768]{3,2,1,0:T(8,128)(2,1)} %collective-permute-done.9.refs_2_), channel_id=1, source_target_pairs={{0,4},{1,3},{4,8},{5,1},{8,12},{9,5},{12,14},{13,9},{14,10},{15,13... | collective-permute-start | bytes 147464 | tf_op jit(solution)/shard_map/ppermute | solution.py:55
  36.8 11.8 %collective-permute-start.12 = (bf16[2,3,48,768]{3,2,1,0:T(8,128)(2,1)}, bf16[2,3,48,768]{3,2,1,0:T(8,128)(2,1)S(1)}, u32[]{:S(2)}, u32[]{:S(2)}) collective-permute-start(bf16[2,3,48,768]{3,2,1,0:T(8,128)(2,1)} %collective-permute-done.6.refs_3_), channel_id=1, source_target_pairs={{0,1},{1,0},{2,3},{3,2},{4,5},{5,4},{6,7},{7,6},{8,9},{9,8},{10,11... | collective-permute-start | bytes 1327112 | tf_op jit(solution)/shard_map/ppermute | solution.py:40
  48.6 15.2 %collective-permute-start.23 = (bf16[2,5,48,768]{3,2,1,0:T(8,128)(2,1)}, bf16[2,5,48,768]{3,2,1,0:T(8,128)(2,1)}, u32[]{:S(2)}, u32[]{:S(2)}) collective-permute-start(bf16[2,5,48,768]{3,2,1,0:T(8,128)(2,1)} %collective-permute-done.17.refs_1_), channel_id=1, source_target_pairs={{0,1},{1,0},{2,3},{3,2},{4,5},{5,4},{6,7},{7,6},{8,9},{9,8},{10,11... | collective-permute-start | bytes 2211848 | tf_op jit(solution)/shard_map/ppermute | solution.py:40
  49.3 14.5 %collective-permute-start.22 = (bf16[2,5,48,768]{3,2,1,0:T(8,128)(2,1)}, bf16[2,5,48,768]{3,2,1,0:T(8,128)(2,1)}, u32[]{:S(2)}, u32[]{:S(2)}) collective-permute-start(bf16[2,5,48,768]{3,2,1,0:T(8,128)(2,1)} %collective-permute-done.17.refs_1_), channel_id=1, source_target_pairs={{0,4},{1,3},{4,8},{5,1},{8,12},{9,5},{12,14},{13,9},{14,10},{15,13... | collective-permute-start | bytes 2211848 | tf_op jit(solution)/shard_map/ppermute | solution.py:55
  50.9 16.5 %collective-permute-start.21 = (bf16[2,1,192,768]{3,2,1,0:T(8,128)(2,1)S(1)}, bf16[2,1,192,768]{3,2,1,0:T(8,128)(2,1)}, u32[]{:S(2)}, u32[]{:S(2)}) collective-permute-start(bf16[2,1,192,768]{3,2,1,0:T(8,128)(2,1)S(1)} %pad_maximum_fusion.1.refs_0_), channel_id=1, source_target_pairs={{0,4},{1,3},{4,8},{5,1},{8,12},{9,5},{12,14},{13,9},{14,10},{15,13... | collective-permute-start | bytes 1769480 | tf_op jit(solution)/shard_map/ppermute | solution.py:55
  63.9 16.3 %collective-permute-start.25 = (bf16[2,5,48,768]{3,2,1,0:T(8,128)(2,1)}, bf16[2,5,48,768]{3,2,1,0:T(8,128)(2,1)S(1)}, u32[]{:S(2)}, u32[]{:S(2)}) collective-permute-start(bf16[2,5,48,768]{3,2,1,0:T(8,128)(2,1)} %collective-permute-done.22.refs_2_), channel_id=1, source_target_pairs={{0,1},{1,0},{2,3},{3,2},{4,5},{5,4},{6,7},{7,6},{8,9},{9,8},{10,11... | collective-permute-start | bytes 2211848 | tf_op jit(solution)/shard_map/ppermute | solution.py:40
  64.0 16.2 %collective-permute-start.24 = (bf16[2,5,48,768]{3,2,1,0:T(8,128)(2,1)}, bf16[2,5,48,768]{3,2,1,0:T(8,128)(2,1)S(1)}, u32[]{:S(2)}, u32[]{:S(2)}) collective-permute-start(bf16[2,5,48,768]{3,2,1,0:T(8,128)(2,1)} %collective-permute-done.22.refs_2_), channel_id=1, source_target_pairs={{0,4},{1,3},{4,8},{5,1},{8,12},{9,5},{12,14},{13,9},{14,10},{15,13... | collective-permute-start | bytes 2211848 | tf_op jit(solution)/shard_map/ppermute | solution.py:55
  67.4 13.2 %collective-permute-start.29 = (bf16[2,1,192,768]{3,2,1,0:T(8,128)(2,1)}, bf16[2,1,192,768]{3,2,1,0:T(8,128)(2,1)S(1)}, u32[]{:S(2)}, u32[]{:S(2)}) collective-permute-start(bf16[2,1,192,768]{3,2,1,0:T(8,128)(2,1)} %collective-permute-done.21.refs_1_), channel_id=1, source_target_pairs={{0,1},{1,0},{2,3},{3,2},{4,5},{5,4},{6,7},{7,6},{8,9},{9,8},{10,11... | collective-permute-start | bytes 1769480 | tf_op jit(solution)/shard_map/ppermute | solution.py:40
  67.4 14.5 %collective-permute-start.28 = (bf16[2,1,192,768]{3,2,1,0:T(8,128)(2,1)}, bf16[2,1,192,768]{3,2,1,0:T(8,128)(2,1)S(1)}, u32[]{:S(2)}, u32[]{:S(2)}) collective-permute-start(bf16[2,1,192,768]{3,2,1,0:T(8,128)(2,1)} %collective-permute-done.21.refs_1_), channel_id=1, source_target_pairs={{0,4},{1,3},{4,8},{5,1},{8,12},{9,5},{12,14},{13,9},{14,10},{15,13... | collective-permute-start | bytes 1769480 | tf_op jit(solution)/shard_map/ppermute | solution.py:55
  80.2 15.6 %collective-permute-start.27 = (bf16[2,5,48,768]{3,2,1,0:T(8,128)(2,1)S(1)}, bf16[2,5,48,768]{3,2,1,0:T(8,128)(2,1)S(1)}, u32[]{:S(2)}, u32[]{:S(2)}) collective-permute-start(bf16[2,5,48,768]{3,2,1,0:T(8,128)(2,1)S(1)} %collective-permute-done.24.refs_3_), channel_id=1, source_target_pairs={{0,1},{1,0},{2,3},{3,2},{4,5},{5,4},{6,7},{7,6},{8,9},{9,8},{10,11... | collective-permute-start | bytes 2211848 | tf_op jit(solution)/shard_map/ppermute | solution.py:40
  81.9 13.8 %collective-permute-start.32 = (bf16[2,1,192,768]{3,2,1,0:T(8,128)(2,1)S(1)}, bf16[2,1,192,768]{3,2,1,0:T(8,128)(2,1)S(1)}, u32[]{:S(2)}, u32[]{:S(2)}) collective-permute-start(bf16[2,1,192,768]{3,2,1,0:T(8,128)(2,1)S(1)} %collective-permute-done.28.refs_2_), channel_id=1, source_target_pairs={{0,1},{1,0},{2,3},{3,2},{4,5},{5,4},{6,7},{7,6},{8,9},{9,8},{10,11... | collective-permute-start | bytes 1769480 | tf_op jit(solution)/shard_map/ppermute | solution.py:40
  82.0 13.9 %collective-permute-start.31 = (bf16[2,1,192,768]{3,2,1,0:T(8,128)(2,1)S(1)}, bf16[2,1,192,768]{3,2,1,0:T(8,128)(2,1)S(1)}, u32[]{:S(2)}, u32[]{:S(2)}) collective-permute-start(bf16[2,1,192,768]{3,2,1,0:T(8,128)(2,1)S(1)} %collective-permute-done.28.refs_2_), channel_id=1, source_target_pairs={{0,4},{1,3},{4,8},{5,1},{8,12},{9,5},{12,14},{13,9},{14,10},{15,13... | collective-permute-start | bytes 1769480 | tf_op jit(solution)/shard_map/ppermute | solution.py:55
  83.4 12.3 %collective-permute-start.26 = (bf16[1,5,48,768]{3,2,1,0:T(8,128)(2,1)S(1)}, bf16[1,5,48,768]{3,2,1,0:T(8,128)(2,1)S(1)}, u32[]{:S(2)}, u32[]{:S(2)}) collective-permute-start(bf16[1,5,48,768]{3,2,1,0:T(8,128)(2,1)S(1)} %slice.78), channel_id=1, source_target_pairs={{0,4},{1,3},{4,8},{5,1},{8,12},{9,5},{12,14},{13,9},{14,10},{15,13... | collective-permute-start | bytes 1105928 | tf_op jit(solution)/shard_map/ppermute | solution.py:55
  126.7 25.7 %collective-permute-start.36 = (bf16[512,768]{1,0:T(8,128)(2,1)}, bf16[512,768]{1,0:T(8,128)(2,1)S(1)}, u32[]{:S(2)}, u32[]{:S(2)}) collective-permute-start(bf16[512,768]{1,0:T(8,128)(2,1)} %get-tuple-element.417), channel_id=1, source_target_pairs={{0,16},{1,17},{2,18},{3,19},{4,20},{5,21},{6,22},{7,23},{8,24},{9,... | collective-permute-start | bytes 2359304 | tf_op jit(solution)/shard_map/ppermute | solution.py:221
  152.4 19.0 %collective-permute-start.37 = (bf16[512,768]{1,0:T(8,128)(2,1)S(1)}, bf16[512,768]{1,0:T(8,128)(2,1)S(1)}, u32[]{:S(2)}, u32[]{:S(2)}) collective-permute-start(bf16[512,768]{1,0:T(8,128)(2,1)S(1)} %get-tuple-element.445), channel_id=1, source_target_pairs={{0,16},{1,17},{2,18},{3,19},{4,20},{5,21},{6,22},{7,23},{8,24},{9,... | collective-permute-start | bytes 2359304 | tf_op jit(solution)/shard_map/ppermute | solution.py:221
  198.3 67.9 %collective-permute-start.46 = (bf16[512,768]{1,0:T(8,128)(2,1)S(1)}, bf16[512,768]{1,0:T(8,128)(2,1)S(1)}, u32[]{:S(2)}, u32[]{:S(2)}) collective-permute-start(bf16[512,768]{1,0:T(8,128)(2,1)S(1)} %get-tuple-element.554), channel_id=1, source_target_pairs={{16,0},{17,1},{18,2},{19,3},{20,4},{21,5},{22,6},{23,7},{24,8},{25... | collective-permute-start | bytes 2359304 | tf_op jit(solution)/shard_map/ppermute | solution.py:221
  266.2 42.2 %collective-permute-start.47 = (bf16[512,768]{1,0:T(8,128)(2,1)}, bf16[512,768]{1,0:T(8,128)(2,1)}, u32[]{:S(2)}, u32[]{:S(2)}) collective-permute-start(bf16[512,768]{1,0:T(8,128)(2,1)} %get-tuple-element.557), channel_id=1, source_target_pairs={{16,0},{17,1},{18,2},{19,3},{20,4},{21,5},{22,6},{23,7},{24,8},{25... | collective-permute-start | bytes 2359304 | tf_op jit(solution)/shard_map/ppermute | solution.py:221
  339.8 11.5 %collective-permute-start.49 = (bf16[8,192,768]{2,1,0:T(8,128)(2,1)S(1)}, bf16[8,192,768]{2,1,0:T(8,128)(2,1)S(1)}, u32[]{:S(2)}, u32[]{:S(2)}) collective-permute-start(bf16[8,192,768]{2,1,0:T(8,128)(2,1)S(1)} %get-tuple-element.604), channel_id=1, source_target_pairs={{0,1},{1,0},{2,3},{3,2},{4,5},{5,4},{6,7},{7,6},{8,9},{9,8},{10,11... | collective-permute-start | bytes 7077896 | tf_op jit(solution)/shard_map/ppermute | solution.py:40
  351.6 10.7 %collective-permute-start.52 = (bf16[2,192,768]{2,1,0:T(8,128)(2,1)S(1)}, bf16[2,192,768]{2,1,0:T(8,128)(2,1)S(1)}, u32[]{:S(2)}, u32[]{:S(2)}) collective-permute-start(bf16[2,192,768]{2,1,0:T(8,128)(2,1)S(1)} %fold.9), channel_id=1, source_target_pairs={{0,4},{1,3},{4,8},{5,1},{8,12},{9,5},{12,14},{13,9},{14,10},{15,13... | collective-permute-start | bytes 1769480 | tf_op jit(solution)/shard_map/ppermute | solution.py:55
  352.8 11.9 %collective-permute-start.51 = (bf16[1,192,768]{2,1,0:T(8,128)(2,1)S(1)}, bf16[1,192,768]{2,1,0:T(8,128)(2,1)S(1)}, u32[]{:S(2)}, u32[]{:S(2)}) collective-permute-start(bf16[1,192,768]{2,1,0:T(8,128)(2,1)S(1)} %get-tuple-element.619), channel_id=1, source_target_pairs={{0,4},{1,3},{4,8},{5,1},{8,12},{9,5},{12,14},{13,9},{14,10},{15,13... | collective-permute-start | bytes 884744 | tf_op jit(solution)/shard_map/ppermute | solution.py:55
  362.5 10.7 %collective-permute-start.54 = (bf16[2,192,768]{2,1,0:T(8,128)(2,1)S(1)}, bf16[2,192,768]{2,1,0:T(8,128)(2,1)S(1)}, u32[]{:S(2)}, u32[]{:S(2)}) collective-permute-start(bf16[2,192,768]{2,1,0:T(8,128)(2,1)S(1)} %fold.11), channel_id=1, source_target_pairs={{0,4},{1,3},{4,8},{5,1},{8,12},{9,5},{12,14},{13,9},{14,10},{15,13... | collective-permute-start | bytes 1769480 | tf_op jit(solution)/shard_map/ppermute | solution.py:55
  365.0 13.8 %collective-permute-start.53 = (bf16[2,192,768]{2,1,0:T(8,128)(2,1)S(1)}, bf16[2,192,768]{2,1,0:T(8,128)(2,1)S(1)}, u32[]{:S(2)}, u32[]{:S(2)}) collective-permute-start(bf16[2,192,768]{2,1,0:T(8,128)(2,1)S(1)} %fold.10), channel_id=1, source_target_pairs={{0,4},{1,3},{4,8},{5,1},{8,12},{9,5},{12,14},{13,9},{14,10},{15,13... | collective-permute-start | bytes 1769480 | tf_op jit(solution)/shard_map/ppermute | solution.py:55
  391.5 14.6 %collective-permute-start.58 = (bf16[2,192,768]{2,1,0:T(8,128)(2,1)S(1)}, bf16[2,192,768]{2,1,0:T(8,128)(2,1)S(1)}, u32[]{:S(2)}, u32[]{:S(2)}) collective-permute-start(bf16[2,192,768]{2,1,0:T(8,128)(2,1)S(1)} %fold.12), channel_id=1, source_target_pairs={{0,4},{1,3},{4,8},{5,1},{8,12},{9,5},{12,14},{13,9},{14,10},{15,13... | collective-permute-start | bytes 1769480 | tf_op jit(solution)/shard_map/ppermute | solution.py:55
  394.4 14.9 %collective-permute-start.56 = (bf16[1,192,768]{2,1,0:T(8,128)(2,1)S(1)}, bf16[1,192,768]{2,1,0:T(8,128)(2,1)S(1)}, u32[]{:S(2)}, u32[]{:S(2)}) collective-permute-start(bf16[1,192,768]{2,1,0:T(8,128)(2,1)S(1)} %get-tuple-element.640), channel_id=1, source_target_pairs={{0,4},{1,3},{4,8},{5,1},{8,12},{9,5},{12,14},{13,9},{14,10},{15,13... | collective-permute-start | bytes 884744 | tf_op jit(solution)/shard_map/ppermute | solution.py:55
  396.0 13.1 %collective-permute-start.57 = (f32[16,768]{1,0:T(8,128)S(1)}, f32[16,768]{1,0:T(8,128)S(1)}, u32[]{:S(2)}, u32[]{:S(2)}) collective-permute-start(f32[16,768]{1,0:T(8,128)S(1)} %get-tuple-element.641), channel_id=1, source_target_pairs={{0,8},{1,9},{2,10},{3,11},{4,12},{5,13},{6,14},{7,15},{8,0},{9,1},... | collective-permute-start | bytes 147464 | tf_op jit(solution)/shard_map/ppermute | solution.py:40
  409.6 13.7 %collective-permute-start.60 = (bf16[2,192,768]{2,1,0:T(8,128)(2,1)S(1)}, bf16[2,192,768]{2,1,0:T(8,128)(2,1)S(1)}, u32[]{:S(2)}, u32[]{:S(2)}) collective-permute-start(bf16[2,192,768]{2,1,0:T(8,128)(2,1)S(1)} %fold.14), channel_id=1, source_target_pairs={{0,4},{1,3},{4,8},{5,1},{8,12},{9,5},{12,14},{13,9},{14,10},{15,13... | collective-permute-start | bytes 1769480 | tf_op jit(solution)/shard_map/ppermute | solution.py:55
  411.5 11.7 %collective-permute-start.61 = (f32[16,768]{1,0:T(8,128)S(1)}, f32[16,768]{1,0:T(8,128)S(1)}, u32[]{:S(2)}, u32[]{:S(2)}) collective-permute-start(f32[16,768]{1,0:T(8,128)S(1)} %add.202), channel_id=1, source_target_pairs={{0,4},{1,5},{2,6},{3,7},{4,0},{5,1},{6,2},{7,3},{8,12},{9,13},{10,... | collective-permute-start | bytes 147464 | tf_op jit(solution)/shard_map/ppermute | solution.py:40
  416.5 10.5 %collective-permute-start.66 = (bf16[2,192,768]{2,1,0:T(8,128)(2,1)}, bf16[2,192,768]{2,1,0:T(8,128)(2,1)}, u32[]{:S(2)}, u32[]{:S(2)}) collective-permute-start(bf16[2,192,768]{2,1,0:T(8,128)(2,1)} %collective-permute-done.62), channel_id=1, source_target_pairs={{0,1},{1,0},{2,3},{3,2},{4,5},{5,4},{6,7},{7,6},{8,9},{9,8},{10,11... | collective-permute-start | bytes 1769480 | tf_op jit(solution)/shard_map/ppermute | solution.py:40
  423.5 12.0 %collective-permute-start.64 = (bf16[2,192,768]{2,1,0:T(8,128)(2,1)S(1)}, bf16[2,192,768]{2,1,0:T(8,128)(2,1)S(1)}, u32[]{:S(2)}, u32[]{:S(2)}) collective-permute-start(bf16[2,192,768]{2,1,0:T(8,128)(2,1)S(1)} %fold.16), channel_id=1, source_target_pairs={{0,4},{1,3},{4,8},{5,1},{8,12},{9,5},{12,14},{13,9},{14,10},{15,13... | collective-permute-start | bytes 1769480 | tf_op jit(solution)/shard_map/ppermute | solution.py:55
  (112 other events, 1205.3 us)

commit v5 on v4

--- a/solution.py
+++ b/solution.py
@@ -1132,7 +1132,7 @@
     while True:
         if loss is None and not small.moving:
             loss = Swapped(small.value[loss_row : loss_row + 1, :128])
-            running.append(loss)
+            running.insert(0, loss)
         if not any(item.moving for item in running):
             break
         onward([reduced_attn])

time: 461 us -> 461 us (level)
  no operation moved by 1% of the time
where the time goes in v5:
time: 461 us; the launch traced here: 454 us
  Pallas kernels  192 us (42%)
  waiting for transfers between devices  141 us (31%)
  starting transfers between devices  64.8 us (14%)
  local copies, waits for them, and re-layouts  31.3 us (7%)
  other arithmetic  20 us (4%)
    pallas_call x18, Pallas kernels, slot_call(): pl.pallas_call(kernel, grid_spec=pltpu.PrefetchScalarGridSpec(num_scalar_...  144 us
    ppermute x4, waiting for transfers between devices, __init__(): self.moving = [lax.ppermute(value, 'section', pairs)]  58.2 us
    ppermute x28, waiting for transfers between devices, ring_hop(): return lax.ppermute(value, 'dp', pairs)  56 us
    ppermute x28, starting transfers between devices, ring_hop(): return lax.ppermute(value, 'dp', pairs)  41.1 us
    pallas_call x3, Pallas kernels, weight_call(): pl.pallas_call(kernel, grid_spec=pltpu.PrefetchScalarGridSpec(num_scalar_...  29.3 us
    ppermute x39, waiting for transfers between devices, swapped(): return lax.ppermute(value, axis, [(i, i ^ mask) for i in range(count)])  27.3 us
    ppermute x39, starting transfers between devices, swapped(): return lax.ppermute(value, axis, [(i, i ^ mask) for i in range(count)])  18.1 us
    unnamed x156, local copies, waits for them, and re-layouts  16 us
  transfers between devices with their start and end apart: 71, of which 31 were waited for; matrix products, arithmetic and copies ran while one was open for 7% of the time, Pallas kernels for 31%

profile of v5, /device:TPU:0, one launch (start us, length us, event | category | flops | bytes accessed | tf_op | source)
XLA Modules:
  0.0 453.8 jit_solution(7282004809707849826)
XLA Ops:
  12.4 3.5 collective-permute-done.1.refs_1_
  38.5 5.6 %collective-permute-done.13.refs_3_ = bf16[2,1,16,768]{3,2,1,0:T(8,128)(2,1)S(1)} collective-permute-done((bf16[2,1,16,768]{3,2,1,0:T(8,128)(2,1)}, bf16[2,1,16,768]{3,2,1,0:T(8,128)(2,1)S(1)}, u32[]{:S(2)}, u32[]{:S(2)}) %collective-permute-start.13) | collective-permute-done | bytes 49184 | tf_op jit(solution)/shard_map/ppermute | solution.py:55
  68.9 11.3 %attend.4 = (bf16[3,512,768]{2,1,0:T(8,128)(2,1)}, bf16[3,512,768]{2,1,0:T(8,128)(2,1)}, bf16[3,512,768]{2,1,0:T(8,128)(2,1)}, bf16[3,512,768]{2,1,0:T(8,128)(2,1)}, f32[3,3,8,512]{3,2,1,0:T(8,128)}) custom-call(s32[1]{0:T(128)} %bitcast.8.m_ref, bf16[512,768]{1,0:T(8,128)(2,1)S(1)} %get-tuple-element.710.refs_0_.x_ref, bf16[3,768,768]{2,1,0:T(8,128)(2,1)} %copy-done.3, ...), custom_call_target="tpu_custom_call" | custom-call | flops 7247757312 | bytes 60000000 | tf_op jit(solution)/shard_map/attend/pallas_call | solution.py:394
  84.6 11.1 %collective-permute-done.26.refs_4_ = bf16[1,5,48,768]{3,2,1,0:T(8,128)(2,1)S(1)} collective-permute-done((bf16[1,5,48,768]{3,2,1,0:T(8,128)(2,1)S(1)}, bf16[1,5,48,768]{3,2,1,0:T(8,128)(2,1)S(1)}, u32[]{:S(2)}, u32[]{:S(2)}) %collective-permute-start.26) | collective-permute-done | bytes 368672 | tf_op jit(solution)/shard_map/ppermute | solution.py:55
  98.4 5.0 %collective-permute-done.33.refs_4_ = bf16[1,1,192,768]{3,2,1,0:T(8,128)(2,1)S(1)} collective-permute-done((bf16[1,1,192,768]{3,2,1,0:T(8,128)(2,1)S(1)}, bf16[1,1,192,768]{3,2,1,0:T(8,128)(2,1)S(1)}, u32[]{:S(2)}, u32[]{:S(2)}) %collective-permute-start.33) | collective-permute-done | bytes 294944 | tf_op jit(solution)/shard_map/ppermute | solution.py:55
  103.5 3.3 assemble.6.wo_ref.wi_ref.refs_8_.refs_11_.refs_5_
  107.8 3.7 assemble.7.wf_ref.refs_6_.refs_3_
  111.5 13.4 %forward.4 = (bf16[512,768]{1,0:T(8,128)(2,1)}, bf16[3,512,768]{2,1,0:T(8,128)(2,1)}, f32[3,512,1]{2,1,0:T(8,128)S(1)}, bf16[3,512,3072]{2,1,0:T(8,128)(2,1)}, b...) custom-call(s32[1]{0:T(128)} %bitcast.8.m_ref, ...), custom_call_target="tpu_custom_call" | custom-call | flops 10871635968 | bytes 60000000 | tf_op jit(solution)/shard_map/forward/pallas_call | solution.py:394
  128.1 11.5 %attend.5 = (bf16[3,512,768]{2,1,0:T(8,128)(2,1)}, bf16[3,512,768]{2,1,0:T(8,128)(2,1)}, bf16[3,512,768]{2,1,0:T(8,128)(2,1)}, bf16[3,512,768]{2,1,0:T(8,128)(2,1)}, f32[3,3,8,512]{3,2,1,0:T(8,128)}) custom-call(s32[1]{0:T(128)} %bitcast.23.m_ref, ...), custom_call_target="tpu_custom_call", output_to_operand_aliasing={{0}: (8, {}), {1}: (9, {}), {2}: (10, {}), {3}: (11, {}), {... | custom-call | tf_op jit(solution)/shard_map/attend/pallas_call | solution.py:394
  139.6 12.8 %forward.5 = (bf16[512,768]{1,0:T(8,128)(2,1)S(1)}, bf16[3,512,768]{2,1,0:T(8,128)(2,1)}, f32[3,512,1]{2,1,0:T(8,128)}, bf16[3,512,3072]{2,1,0:T(8,128)(2,1)}, b...) custom-call(s32[1]{0:T(128)} %bitcast.23.m_ref, ...), custom_call_target="tpu_custom_call", output_to_operand_aliasing={{1}: (8, {}), {2}: (9, {}), {3}: (10, {}), {4}: (11, {}), {... | custom-call | tf_op jit(solution)/shard_map/forward/pallas_call | solution.py:394
  164.5 6.9 %collective-permute-done.37.refs_0_.x_ref = bf16[512,768]{1,0:T(8,128)(2,1)S(1)} collective-permute-done((bf16[512,768]{1,0:T(8,128)(2,1)S(1)}, bf16[512,768]{1,0:T(8,128)(2,1)S(1)}, u32[]{:S(2)}, u32[]{:S(2)}) %collective-permute-start.37) | collective-permute-done | bytes 786464 | tf_op jit(solution)/shard_map/ppermute | solution.py:221
  175.7 3.6 forward.7
  182.3 3.9 collective-permute-done.41
  190.7 3.6 ff_back.4
  194.4 3.9 attend_back.6
  209.3 3.9 ff_back.5
  213.2 4.5 attend_back.7
  217.7 48.5 %collective-permute-done.46.cot_ref = bf16[512,768]{1,0:T(8,128)(2,1)S(1)} collective-permute-done((bf16[512,768]{1,0:T(8,128)(2,1)S(1)}, bf16[512,768]{1,0:T(8,128)(2,1)S(1)}, u32[]{:S(2)}, u32[]{:S(2)}) %collective-permute-start.46) | collective-permute-done | bytes 786464 | tf_op jit(solution)/shard_map/ppermute | solution.py:221
  275.6 13.1 %ff_back.6 = (f32[512,768]{1,0:T(8,128)S(1)}, bf16[512,768]{1,0:T(8,128)(2,1)S(1)}, f32[16,768]{1,0:T(8,128)S(1)}, bf16[3,512,768]{2,1,0:T(8,128)(2,1)}, bf16[3,...) custom-call(s32[1]{0:T(128)} %bitcast.8.m_ref, ...), custom_call_target="tpu_custom_call", output_to_operand_aliasing={{3}: (12, {}), {4}: (13, {}), {5}: (14, {})} | custom-call | tf_op jit(solution)/shard_map/ff_back/pallas_call | solution.py:394
  288.6 17.0 %attend_back.8 = (bf16[512,768]{1,0:T(8,128)(2,1)}, f32[16,768]{1,0:T(8,128)S(1)}, f32[2,512,768]{2,1,0:T(8,128)}, bf16[3,4,512,768]{3,2,1,0:T(8,128)(2,1)}) custom-call(s32[1]{0:T(128)} %bitcast.8.m_ref, bf16[3,512,768]{2,1,0:T(8,128)(2,1)} %get-tuple-element.487.refs_0_, ...), custom_call_target="tpu_custom_call", output_to_operand_aliasing={{3}: (14, {}), {2}: (10, {})} | custom-call | tf_op jit(solution)/shard_map/attend_back/pallas_call | solution.py:394
  308.4 12.7 %ff_back.7 = (f32[512,768]{1,0:T(8,128)S(1)}, bf16[512,768]{1,0:T(8,128)(2,1)S(1)}, f32[16,768]{1,0:T(8,128)S(1)}, bf16[3,512,768]{2,1,0:T(8,128)(2,1)}, bf16[3,...) custom-call(s32[1]{0:T(128)} %bitcast.23.m_ref, ...), custom_call_target="tpu_custom_call", output_to_operand_aliasing={{3}: (12, {}), {4}: (13, {}), {5}: (14, {})} | custom-call | flops 72477573120 | bytes 300000000 | tf_op jit(solution)/shard_map/ff_back/pallas_call | solution.py:394
  321.1 8.8 %weight_out.1 = (bf16[8,192,768]{2,1,0:T(8,128)(2,1)S(1)}, bf16[8,192,768]{2,1,0:T(8,128)(2,1)S(1)}) custom-call(s32[16]{0:T(128)S(1)} %select_reduce_fusion.slot_ref, bf16[3,512,3072]{2,1,0:T(8,128)(2,1)} %get-tuple-element.592.gelu_ref, bf16[3,512,768]{2,1,0:T(8,128)(2,1)} %get-tuple-element.589.gbranch_ref), custom_call_target="tpu_custom_call" | custom-call | flops 48318382080 | bytes 300000000 | tf_op jit(solution)/shard_map/weight_out/pallas_call | solution.py:840
  330.0 9.8 %weight_wide.1 = (bf16[8,192,768]{2,1,0:T(8,128)(2,1)S(1)}, bf16[8,192,768]{2,1,0:T(8,128)(2,1)S(1)}) custom-call(s32[16]{0:T(128)S(1)} %select_reduce_fusion.slot_ref, bf16[3,512,768]{2,1,0:T(8,128)(2,1)} %get-tuple-element.513.refs_9_.refs_6_.xhat_ref, f32[12,768]{1,0:T(8,128)S(1)} %maximum_convert_fusion.refs_4_.vec_ref.refs_5_.refs_2_, ...), custom_call_target="tpu_custom_call" | custom-call | flops 48318382080 | bytes 300000000 | tf_op jit(solution)/shard_map/weight_wide/pallas_call | solution.py:840
  343.1 8.1 %attend_back.9 = (bf16[512,768]{1,0:T(8,128)(2,1)}, f32[16,768]{1,0:T(8,128)S(1)}, f32[2,512,768]{2,1,0:T(8,128)}, bf16[3,4,512,768]{3,2,1,0:T(8,128)(2,1)}) custom-call(s32[1]{0:T(128)} %bitcast.23.m_ref, bf16[3,512,768]{2,1,0:T(8,128)(2,1)} %get-tuple-element.487.refs_0_, ...), custom_call_target="tpu_custom_call", output_to_operand_aliasing={{3}: (14, {}), {2}: (10, {})} | custom-call | flops 36238786560 | bytes 300000000 | tf_op jit(solution)/shard_map/attend_back/pallas_call | solution.py:394
  354.1 8.1 %attend_back.10 = (bf16[512,768]{1,0:T(8,128)(2,1)}, f32[16,768]{1,0:T(8,128)S(1)}, f32[2,512,768]{2,1,0:T(8,128)}, bf16[3,4,512,768]{3,2,1,0:T(8,128)(2,1)}) custom-call(s32[1]{0:T(128)} %bitcast.23.m_ref, bf16[3,512,768]{2,1,0:T(8,128)(2,1)} %get-tuple-element.487.refs_0_, ...), custom_call_target="tpu_custom_call", output_to_operand_aliasing={{3}: (13, {}), {2}: (9, {})} | custom-call | flops 36238786560 | bytes 300000000 | tf_op jit(solution)/shard_map/attend_back/pallas_call | solution.py:394
  365.1 8.1 %attend_back.11 = (bf16[512,768]{1,0:T(8,128)(2,1)}, f32[16,768]{1,0:T(8,128)S(1)}, f32[2,512,768]{2,1,0:T(8,128)}, bf16[3,4,512,768]{3,2,1,0:T(8,128)(2,1)}) custom-call(s32[1]{0:T(128)} %bitcast.23.m_ref, bf16[3,512,768]{2,1,0:T(8,128)(2,1)} %get-tuple-element.487.refs_0_, ...), custom_call_target="tpu_custom_call", output_to_operand_aliasing={{3}: (13, {}), {2}: (9, {})} | custom-call | flops 36238786560 | bytes 300000000 | tf_op jit(solution)/shard_map/attend_back/pallas_call | solution.py:394
  373.2 5.5 %collective-permute-done.53.there_ref = bf16[2,192,768]{2,1,0:T(8,128)(2,1)S(1)} collective-permute-done((bf16[2,192,768]{2,1,0:T(8,128)(2,1)S(1)}, bf16[2,192,768]{2,1,0:T(8,128)(2,1)S(1)}, u32[]{:S(2)}, u32[]{:S(2)}) %collective-permute-start.53) | collective-permute-done | bytes 589856 | tf_op jit(solution)/shard_map/ppermute | solution.py:55
  378.8 10.7 %weight_attn.1 = (bf16[8,192,768]{2,1,0:T(8,128)(2,1)S(1)}, bf16[8,192,768]{2,1,0:T(8,128)(2,1)S(1)}) custom-call(s32[16]{0:T(128)S(1)} %select_reduce_fusion.slot_ref, bf16[2,512,768]{2,1,0:T(8,128)(2,1)} %maximum_select_fusion.x_ref, bf16[3,512,768]{2,1,0:T(8,128)(2,1)} %get-tuple-element.486.mixed_ref, bf16[3,4,512,768]{3,2,1,0:T(8,128)(2,1)} %get-tuple-element.635.grad_ref), custom_call_target="tpu_custom_call" | custom-call | flops 48318382080 | bytes 300000000 | tf_op jit(solution)/shard_map/weight_attn/pallas_call | solution.py:840
  399.8 6.3 %collective-permute-done.58.there_ref = bf16[2,192,768]{2,1,0:T(8,128)(2,1)S(1)} collective-permute-done((bf16[2,192,768]{2,1,0:T(8,128)(2,1)S(1)}, bf16[2,192,768]{2,1,0:T(8,128)(2,1)S(1)}, u32[]{:S(2)}, u32[]{:S(2)}) %collective-permute-start.58) | collective-permute-done | bytes 589856 | tf_op jit(solution)/shard_map/ppermute | solution.py:55
  417.1 6.1 %collective-permute-done.61 = f32[16,768]{1,0:T(8,128)S(1)} collective-permute-done((f32[16,768]{1,0:T(8,128)S(1)}, f32[16,768]{1,0:T(8,128)S(1)}, u32[]{:S(2)}, u32[]{:S(2)}) %collective-permute-start.61) | collective-permute-done | bytes 49184 | tf_op jit(solution)/shard_map/ppermute | solution.py:40
  427.1 8.4 %collective-permute-done.65 = f32[16,768]{1,0:T(8,128)} collective-permute-done((f32[16,768]{1,0:T(8,128)}, f32[16,768]{1,0:T(8,128)}, u32[]{:S(2)}, u32[]{:S(2)}) %collective-permute-start.65) | collective-permute-done | bytes 49184 | tf_op jit(solution)/shard_map/ppermute | solution.py:40
  443.2 4.2 collective-permute-done.67
  (396 shorter events, 162.5 us)
Async XLA Ops:
  16.4 12.3 %collective-permute-start.10 = (bf16[2,1,16,768]{3,2,1,0:T(8,128)(2,1)}, bf16[2,1,16,768]{3,2,1,0:T(8,128)(2,1)S(1)}, u32[]{:S(2)}, u32[]{:S(2)}) collective-permute-start(bf16[2,1,16,768]{3,2,1,0:T(8,128)(2,1)} %collective-permute-done.5.refs_1_), channel_id=1, source_target_pairs={{0,1},{1,0},{2,3},{3,2},{4,5},{5,4},{6,7},{7,6},{8,9},{9,8},{10,11... | collective-permute-start | bytes 147464 | tf_op jit(solution)/shard_map/ppermute | solution.py:40
  16.4 12.3 %collective-permute-start.9 = (bf16[2,1,16,768]{3,2,1,0:T(8,128)(2,1)}, bf16[2,1,16,768]{3,2,1,0:T(8,128)(2,1)}, u32[]{:S(2)}, u32[]{:S(2)}) collective-permute-start(bf16[2,1,16,768]{3,2,1,0:T(8,128)(2,1)} %collective-permute-done.5.refs_1_), channel_id=1, source_target_pairs={{0,4},{1,3},{4,8},{5,1},{8,12},{9,5},{12,14},{13,9},{14,10},{15,13... | collective-permute-start | bytes 147464 | tf_op jit(solution)/shard_map/ppermute | solution.py:55
  30.4 18.2 %collective-permute-start.17 = (bf16[2,5,48,768]{3,2,1,0:T(8,128)(2,1)S(1)}, bf16[2,5,48,768]{3,2,1,0:T(8,128)(2,1)}, u32[]{:S(2)}, u32[]{:S(2)}) collective-permute-start(bf16[2,5,48,768]{3,2,1,0:T(8,128)(2,1)S(1)} %pad_maximum_fusion.refs_0_), channel_id=1, source_target_pairs={{0,4},{1,3},{4,8},{5,1},{8,12},{9,5},{12,14},{13,9},{14,10},{15,13... | collective-permute-start | bytes 2211848 | tf_op jit(solution)/shard_map/ppermute | solution.py:55
  32.8 11.4 %collective-permute-start.13 = (bf16[2,1,16,768]{3,2,1,0:T(8,128)(2,1)}, bf16[2,1,16,768]{3,2,1,0:T(8,128)(2,1)S(1)}, u32[]{:S(2)}, u32[]{:S(2)}) collective-permute-start(bf16[2,1,16,768]{3,2,1,0:T(8,128)(2,1)} %collective-permute-done.9.refs_2_), channel_id=1, source_target_pairs={{0,4},{1,3},{4,8},{5,1},{8,12},{9,5},{12,14},{13,9},{14,10},{15,13... | collective-permute-start | bytes 147464 | tf_op jit(solution)/shard_map/ppermute | solution.py:55
  36.8 11.8 %collective-permute-start.12 = (bf16[2,3,48,768]{3,2,1,0:T(8,128)(2,1)}, bf16[2,3,48,768]{3,2,1,0:T(8,128)(2,1)S(1)}, u32[]{:S(2)}, u32[]{:S(2)}) collective-permute-start(bf16[2,3,48,768]{3,2,1,0:T(8,128)(2,1)} %collective-permute-done.6.refs_3_), channel_id=1, source_target_pairs={{0,1},{1,0},{2,3},{3,2},{4,5},{5,4},{6,7},{7,6},{8,9},{9,8},{10,11... | collective-permute-start | bytes 1327112 | tf_op jit(solution)/shard_map/ppermute | solution.py:40
  48.6 15.2 %collective-permute-start.23 = (bf16[2,5,48,768]{3,2,1,0:T(8,128)(2,1)}, bf16[2,5,48,768]{3,2,1,0:T(8,128)(2,1)}, u32[]{:S(2)}, u32[]{:S(2)}) collective-permute-start(bf16[2,5,48,768]{3,2,1,0:T(8,128)(2,1)} %collective-permute-done.17.refs_1_), channel_id=1, source_target_pairs={{0,1},{1,0},{2,3},{3,2},{4,5},{5,4},{6,7},{7,6},{8,9},{9,8},{10,11... | collective-permute-start | bytes 2211848 | tf_op jit(solution)/shard_map/ppermute | solution.py:40
  49.3 14.5 %collective-permute-start.22 = (bf16[2,5,48,768]{3,2,1,0:T(8,128)(2,1)}, bf16[2,5,48,768]{3,2,1,0:T(8,128)(2,1)}, u32[]{:S(2)}, u32[]{:S(2)}) collective-permute-start(bf16[2,5,48,768]{3,2,1,0:T(8,128)(2,1)} %collective-permute-done.17.refs_1_), channel_id=1, source_target_pairs={{0,4},{1,3},{4,8},{5,1},{8,12},{9,5},{12,14},{13,9},{14,10},{15,13... | collective-permute-start | bytes 2211848 | tf_op jit(solution)/shard_map/ppermute | solution.py:55
  50.9 16.5 %collective-permute-start.21 = (bf16[2,1,192,768]{3,2,1,0:T(8,128)(2,1)S(1)}, bf16[2,1,192,768]{3,2,1,0:T(8,128)(2,1)}, u32[]{:S(2)}, u32[]{:S(2)}) collective-permute-start(bf16[2,1,192,768]{3,2,1,0:T(8,128)(2,1)S(1)} %pad_maximum_fusion.1.refs_0_), channel_id=1, source_target_pairs={{0,4},{1,3},{4,8},{5,1},{8,12},{9,5},{12,14},{13,9},{14,10},{15,13... | collective-permute-start | bytes 1769480 | tf_op jit(solution)/shard_map/ppermute | solution.py:55
  63.9 16.3 %collective-permute-start.25 = (bf16[2,5,48,768]{3,2,1,0:T(8,128)(2,1)}, bf16[2,5,48,768]{3,2,1,0:T(8,128)(2,1)S(1)}, u32[]{:S(2)}, u32[]{:S(2)}) collective-permute-start(bf16[2,5,48,768]{3,2,1,0:T(8,128)(2,1)} %collective-permute-done.22.refs_2_), channel_id=1, source_target_pairs={{0,1},{1,0},{2,3},{3,2},{4,5},{5,4},{6,7},{7,6},{8,9},{9,8},{10,11... | collective-permute-start | bytes 2211848 | tf_op jit(solution)/shard_map/ppermute | solution.py:40
  64.0 16.2 %collective-permute-start.24 = (bf16[2,5,48,768]{3,2,1,0:T(8,128)(2,1)}, bf16[2,5,48,768]{3,2,1,0:T(8,128)(2,1)S(1)}, u32[]{:S(2)}, u32[]{:S(2)}) collective-permute-start(bf16[2,5,48,768]{3,2,1,0:T(8,128)(2,1)} %collective-permute-done.22.refs_2_), channel_id=1, source_target_pairs={{0,4},{1,3},{4,8},{5,1},{8,12},{9,5},{12,14},{13,9},{14,10},{15,13... | collective-permute-start | bytes 2211848 | tf_op jit(solution)/shard_map/ppermute | solution.py:55
  67.4 13.2 %collective-permute-start.29 = (bf16[2,1,192,768]{3,2,1,0:T(8,128)(2,1)}, bf16[2,1,192,768]{3,2,1,0:T(8,128)(2,1)S(1)}, u32[]{:S(2)}, u32[]{:S(2)}) collective-permute-start(bf16[2,1,192,768]{3,2,1,0:T(8,128)(2,1)} %collective-permute-done.21.refs_1_), channel_id=1, source_target_pairs={{0,1},{1,0},{2,3},{3,2},{4,5},{5,4},{6,7},{7,6},{8,9},{9,8},{10,11... | collective-permute-start | bytes 1769480 | tf_op jit(solution)/shard_map/ppermute | solution.py:40
  67.4 14.5 %collective-permute-start.28 = (bf16[2,1,192,768]{3,2,1,0:T(8,128)(2,1)}, bf16[2,1,192,768]{3,2,1,0:T(8,128)(2,1)S(1)}, u32[]{:S(2)}, u32[]{:S(2)}) collective-permute-start(bf16[2,1,192,768]{3,2,1,0:T(8,128)(2,1)} %collective-permute-done.21.refs_1_), channel_id=1, source_target_pairs={{0,4},{1,3},{4,8},{5,1},{8,12},{9,5},{12,14},{13,9},{14,10},{15,13... | collective-permute-start | bytes 1769480 | tf_op jit(solution)/shard_map/ppermute | solution.py:55
  80.2 15.6 %collective-permute-start.27 = (bf16[2,5,48,768]{3,2,1,0:T(8,128)(2,1)S(1)}, bf16[2,5,48,768]{3,2,1,0:T(8,128)(2,1)S(1)}, u32[]{:S(2)}, u32[]{:S(2)}) collective-permute-start(bf16[2,5,48,768]{3,2,1,0:T(8,128)(2,1)S(1)} %collective-permute-done.24.refs_3_), channel_id=1, source_target_pairs={{0,1},{1,0},{2,3},{3,2},{4,5},{5,4},{6,7},{7,6},{8,9},{9,8},{10,11... | collective-permute-start | bytes 2211848 | tf_op jit(solution)/shard_map/ppermute | solution.py:40
  81.9 13.8 %collective-permute-start.32 = (bf16[2,1,192,768]{3,2,1,0:T(8,128)(2,1)S(1)}, bf16[2,1,192,768]{3,2,1,0:T(8,128)(2,1)S(1)}, u32[]{:S(2)}, u32[]{:S(2)}) collective-permute-start(bf16[2,1,192,768]{3,2,1,0:T(8,128)(2,1)S(1)} %collective-permute-done.28.refs_2_), channel_id=1, source_target_pairs={{0,1},{1,0},{2,3},{3,2},{4,5},{5,4},{6,7},{7,6},{8,9},{9,8},{10,11... | collective-permute-start | bytes 1769480 | tf_op jit(solution)/shard_map/ppermute | solution.py:40
  82.0 13.9 %collective-permute-start.31 = (bf16[2,1,192,768]{3,2,1,0:T(8,128)(2,1)S(1)}, bf16[2,1,192,768]{3,2,1,0:T(8,128)(2,1)S(1)}, u32[]{:S(2)}, u32[]{:S(2)}) collective-permute-start(bf16[2,1,192,768]{3,2,1,0:T(8,128)(2,1)S(1)} %collective-permute-done.28.refs_2_), channel_id=1, source_target_pairs={{0,4},{1,3},{4,8},{5,1},{8,12},{9,5},{12,14},{13,9},{14,10},{15,13... | collective-permute-start | bytes 1769480 | tf_op jit(solution)/shard_map/ppermute | solution.py:55
  83.4 12.3 %collective-permute-start.26 = (bf16[1,5,48,768]{3,2,1,0:T(8,128)(2,1)S(1)}, bf16[1,5,48,768]{3,2,1,0:T(8,128)(2,1)S(1)}, u32[]{:S(2)}, u32[]{:S(2)}) collective-permute-start(bf16[1,5,48,768]{3,2,1,0:T(8,128)(2,1)S(1)} %slice.78), channel_id=1, source_target_pairs={{0,4},{1,3},{4,8},{5,1},{8,12},{9,5},{12,14},{13,9},{14,10},{15,13... | collective-permute-start | bytes 1105928 | tf_op jit(solution)/shard_map/ppermute | solution.py:55
  126.7 25.7 %collective-permute-start.36 = (bf16[512,768]{1,0:T(8,128)(2,1)}, bf16[512,768]{1,0:T(8,128)(2,1)S(1)}, u32[]{:S(2)}, u32[]{:S(2)}) collective-permute-start(bf16[512,768]{1,0:T(8,128)(2,1)} %get-tuple-element.417), channel_id=1, source_target_pairs={{0,16},{1,17},{2,18},{3,19},{4,20},{5,21},{6,22},{7,23},{8,24},{9,... | collective-permute-start | bytes 2359304 | tf_op jit(solution)/shard_map/ppermute | solution.py:221
  152.4 19.0 %collective-permute-start.37 = (bf16[512,768]{1,0:T(8,128)(2,1)S(1)}, bf16[512,768]{1,0:T(8,128)(2,1)S(1)}, u32[]{:S(2)}, u32[]{:S(2)}) collective-permute-start(bf16[512,768]{1,0:T(8,128)(2,1)S(1)} %get-tuple-element.445), channel_id=1, source_target_pairs={{0,16},{1,17},{2,18},{3,19},{4,20},{5,21},{6,22},{7,23},{8,24},{9,... | collective-permute-start | bytes 2359304 | tf_op jit(solution)/shard_map/ppermute | solution.py:221
  198.3 67.9 %collective-permute-start.46 = (bf16[512,768]{1,0:T(8,128)(2,1)S(1)}, bf16[512,768]{1,0:T(8,128)(2,1)S(1)}, u32[]{:S(2)}, u32[]{:S(2)}) collective-permute-start(bf16[512,768]{1,0:T(8,128)(2,1)S(1)} %get-tuple-element.554), channel_id=1, source_target_pairs={{16,0},{17,1},{18,2},{19,3},{20,4},{21,5},{22,6},{23,7},{24,8},{25... | collective-permute-start | bytes 2359304 | tf_op jit(solution)/shard_map/ppermute | solution.py:221
  266.2 42.2 %collective-permute-start.47 = (bf16[512,768]{1,0:T(8,128)(2,1)}, bf16[512,768]{1,0:T(8,128)(2,1)}, u32[]{:S(2)}, u32[]{:S(2)}) collective-permute-start(bf16[512,768]{1,0:T(8,128)(2,1)} %get-tuple-element.557), channel_id=1, source_target_pairs={{16,0},{17,1},{18,2},{19,3},{20,4},{21,5},{22,6},{23,7},{24,8},{25... | collective-permute-start | bytes 2359304 | tf_op jit(solution)/shard_map/ppermute | solution.py:221
  339.8 11.5 %collective-permute-start.49 = (bf16[8,192,768]{2,1,0:T(8,128)(2,1)S(1)}, bf16[8,192,768]{2,1,0:T(8,128)(2,1)S(1)}, u32[]{:S(2)}, u32[]{:S(2)}) collective-permute-start(bf16[8,192,768]{2,1,0:T(8,128)(2,1)S(1)} %get-tuple-element.604), channel_id=1, source_target_pairs={{0,1},{1,0},{2,3},{3,2},{4,5},{5,4},{6,7},{7,6},{8,9},{9,8},{10,11... | collective-permute-start | bytes 7077896 | tf_op jit(solution)/shard_map/ppermute | solution.py:40
  351.6 10.7 %collective-permute-start.52 = (bf16[2,192,768]{2,1,0:T(8,128)(2,1)S(1)}, bf16[2,192,768]{2,1,0:T(8,128)(2,1)S(1)}, u32[]{:S(2)}, u32[]{:S(2)}) collective-permute-start(bf16[2,192,768]{2,1,0:T(8,128)(2,1)S(1)} %fold.9), channel_id=1, source_target_pairs={{0,4},{1,3},{4,8},{5,1},{8,12},{9,5},{12,14},{13,9},{14,10},{15,13... | collective-permute-start | bytes 1769480 | tf_op jit(solution)/shard_map/ppermute | solution.py:55
  352.8 11.9 %collective-permute-start.51 = (bf16[1,192,768]{2,1,0:T(8,128)(2,1)S(1)}, bf16[1,192,768]{2,1,0:T(8,128)(2,1)S(1)}, u32[]{:S(2)}, u32[]{:S(2)}) collective-permute-start(bf16[1,192,768]{2,1,0:T(8,128)(2,1)S(1)} %get-tuple-element.619), channel_id=1, source_target_pairs={{0,4},{1,3},{4,8},{5,1},{8,12},{9,5},{12,14},{13,9},{14,10},{15,13... | collective-permute-start | bytes 884744 | tf_op jit(solution)/shard_map/ppermute | solution.py:55
  362.5 10.7 %collective-permute-start.54 = (bf16[2,192,768]{2,1,0:T(8,128)(2,1)S(1)}, bf16[2,192,768]{2,1,0:T(8,128)(2,1)S(1)}, u32[]{:S(2)}, u32[]{:S(2)}) collective-permute-start(bf16[2,192,768]{2,1,0:T(8,128)(2,1)S(1)} %fold.11), channel_id=1, source_target_pairs={{0,4},{1,3},{4,8},{5,1},{8,12},{9,5},{12,14},{13,9},{14,10},{15,13... | collective-permute-start | bytes 1769480 | tf_op jit(solution)/shard_map/ppermute | solution.py:55
  365.0 13.8 %collective-permute-start.53 = (bf16[2,192,768]{2,1,0:T(8,128)(2,1)S(1)}, bf16[2,192,768]{2,1,0:T(8,128)(2,1)S(1)}, u32[]{:S(2)}, u32[]{:S(2)}) collective-permute-start(bf16[2,192,768]{2,1,0:T(8,128)(2,1)S(1)} %fold.10), channel_id=1, source_target_pairs={{0,4},{1,3},{4,8},{5,1},{8,12},{9,5},{12,14},{13,9},{14,10},{15,13... | collective-permute-start | bytes 1769480 | tf_op jit(solution)/shard_map/ppermute | solution.py:55
  391.5 14.6 %collective-permute-start.58 = (bf16[2,192,768]{2,1,0:T(8,128)(2,1)S(1)}, bf16[2,192,768]{2,1,0:T(8,128)(2,1)S(1)}, u32[]{:S(2)}, u32[]{:S(2)}) collective-permute-start(bf16[2,192,768]{2,1,0:T(8,128)(2,1)S(1)} %fold.12), channel_id=1, source_target_pairs={{0,4},{1,3},{4,8},{5,1},{8,12},{9,5},{12,14},{13,9},{14,10},{15,13... | collective-permute-start | bytes 1769480 | tf_op jit(solution)/shard_map/ppermute | solution.py:55
  394.4 14.9 %collective-permute-start.56 = (bf16[1,192,768]{2,1,0:T(8,128)(2,1)S(1)}, bf16[1,192,768]{2,1,0:T(8,128)(2,1)S(1)}, u32[]{:S(2)}, u32[]{:S(2)}) collective-permute-start(bf16[1,192,768]{2,1,0:T(8,128)(2,1)S(1)} %get-tuple-element.640), channel_id=1, source_target_pairs={{0,4},{1,3},{4,8},{5,1},{8,12},{9,5},{12,14},{13,9},{14,10},{15,13... | collective-permute-start | bytes 884744 | tf_op jit(solution)/shard_map/ppermute | solution.py:55
  396.0 13.1 %collective-permute-start.57 = (f32[16,768]{1,0:T(8,128)S(1)}, f32[16,768]{1,0:T(8,128)S(1)}, u32[]{:S(2)}, u32[]{:S(2)}) collective-permute-start(f32[16,768]{1,0:T(8,128)S(1)} %get-tuple-element.641), channel_id=1, source_target_pairs={{0,8},{1,9},{2,10},{3,11},{4,12},{5,13},{6,14},{7,15},{8,0},{9,1},... | collective-permute-start | bytes 147464 | tf_op jit(solution)/shard_map/ppermute | solution.py:40
  409.6 13.7 %collective-permute-start.60 = (bf16[2,192,768]{2,1,0:T(8,128)(2,1)S(1)}, bf16[2,192,768]{2,1,0:T(8,128)(2,1)S(1)}, u32[]{:S(2)}, u32[]{:S(2)}) collective-permute-start(bf16[2,192,768]{2,1,0:T(8,128)(2,1)S(1)} %fold.14), channel_id=1, source_target_pairs={{0,4},{1,3},{4,8},{5,1},{8,12},{9,5},{12,14},{13,9},{14,10},{15,13... | collective-permute-start | bytes 1769480 | tf_op jit(solution)/shard_map/ppermute | solution.py:55
  411.5 11.7 %collective-permute-start.61 = (f32[16,768]{1,0:T(8,128)S(1)}, f32[16,768]{1,0:T(8,128)S(1)}, u32[]{:S(2)}, u32[]{:S(2)}) collective-permute-start(f32[16,768]{1,0:T(8,128)S(1)} %add.202), channel_id=1, source_target_pairs={{0,4},{1,5},{2,6},{3,7},{4,0},{5,1},{6,2},{7,3},{8,12},{9,13},{10,... | collective-permute-start | bytes 147464 | tf_op jit(solution)/shard_map/ppermute | solution.py:40
  416.5 10.5 %collective-permute-start.66 = (bf16[2,192,768]{2,1,0:T(8,128)(2,1)}, bf16[2,192,768]{2,1,0:T(8,128)(2,1)}, u32[]{:S(2)}, u32[]{:S(2)}) collective-permute-start(bf16[2,192,768]{2,1,0:T(8,128)(2,1)} %collective-permute-done.62), channel_id=1, source_target_pairs={{0,1},{1,0},{2,3},{3,2},{4,5},{5,4},{6,7},{7,6},{8,9},{9,8},{10,11... | collective-permute-start | bytes 1769480 | tf_op jit(solution)/shard_map/ppermute | solution.py:40
  423.5 12.0 %collective-permute-start.64 = (bf16[2,192,768]{2,1,0:T(8,128)(2,1)S(1)}, bf16[2,192,768]{2,1,0:T(8,128)(2,1)S(1)}, u32[]{:S(2)}, u32[]{:S(2)}) collective-permute-start(bf16[2,192,768]{2,1,0:T(8,128)(2,1)S(1)} %fold.16), channel_id=1, source_target_pairs={{0,4},{1,3},{4,8},{5,1},{8,12},{9,5},{12,14},{13,9},{14,10},{15,13... | collective-permute-start | bytes 1769480 | tf_op jit(solution)/shard_map/ppermute | solution.py:55
  (112 other events, 1205.3 us)
